TPU v7x, 32 devices: a whole 2x2x4 slice. The times are simulated.
32 devices in a mesh: grp: 2 (over y), ex: 4 (over z), proj: 4 (over x, core).
Axes of the slice: x: 2, y: 2, z: 4, core: 2. Of those that a mesh axis runs over, the one named last changes fastest.
Arguments:
- inputs: bfloat16 [32, 144, 5120], P(('grp', 'ex'), None, 'proj'), parts along dimension 0, may hold values from -6 to 6
- cotangents: bfloat16 [32, 144, 5120], P(('grp', 'ex'), None, 'proj'), parts along dimension 0, may hold values from -6 to 6
- lengths: int32 [32], P(('grp', 'ex')), parts along dimension 0, may hold values from 1 to 144, 1152 in all
- adapter_down_matrix: bfloat16 [128, 5120], P(None, 'proj'), may hold values from -0.078125 to 0.078125
- adapter_up_matrix: bfloat16 [5120, 128], P('proj'), may hold values from -0.078125 to 0.078125
- width_side_sketch: bfloat16 [5120, 512], P('proj'), may hold values from -0.078125 to 0.078125
- rank_side_sketch: bfloat16 [2, 128, 8], replicated, may hold values from -0.5 to 0.5
- heldout_gradient_rows: bfloat16 [256, 8192], P(('grp', 'ex'), 'proj'), parts along dimension 0, may hold values from -20 to 20
Outputs:
- train_proj: bfloat16 [32, 8192], P(('grp', 'ex'), 'proj'), parts along dimension 0
- scores: float32 [32, 128], P(('grp', 'ex'), 'proj'), parts along dimension 0
There are 2 independent parts, one for each index of `grp`. A program takes and returns all parts, laid end to end along the dimension named above; an argument that names none is the same for every part. Nothing has to cross between parts.
Inputs may be any that keep to these rules, and one draw needn't show every extreme that they name: The lengths of each part along grp sum to 1152.
All inputs are finite; a program needn't handle non-finite values. No bound on the sum of `lengths` on one device may be relied on, other than what follows from the above.
Results may differ from a plain program's by a relative error of at most 0.01.
Values may be sent and summed in bfloat16 or wider, within the bound.
No kernel may reach another device: no remote copies, remote signals or barrier semaphores. Data moves between devices by JAX's collectives and lax.ppermute only.
A program may use at most 64 MiB of HBM per device.

v0:
```python
import math

import jax
import jax.numpy as jnp
from jax import lax
from jax.sharding import PartitionSpec as P

PDIM = 8192


epsilon = 1e-06


def shards(
    inputs,
    cotangents,
    lengths,
    adapter_down_matrix,
    adapter_up_matrix,
    width_side_sketch,
    rank_side_sketch,
    heldout_gradient_rows,
):
    ex_dev, seq_len, model_cols = inputs.shape
    row_count = ex_dev * seq_len
    flattened_input = inputs.reshape(row_count, model_cols)
    flattened_output = cotangents.reshape(row_count, model_cols)
    partial_in = lax.dot_general(
        flattened_input,
        adapter_down_matrix,
        (((1,), (1,)), ((), ())),
        preferred_element_type=jnp.float32,
    )
    incomplete_output = jnp.dot(
        flattened_output, adapter_up_matrix, preferred_element_type=jnp.float32
    )
    summed_in, summed_out = lax.psum((partial_in, incomplete_output), "proj")
    right_out = jnp.dot(
        summed_in.astype(jnp.bfloat16), rank_side_sketch[0], preferred_element_type=jnp.float32
    )
    right_in = jnp.dot(
        summed_out.astype(jnp.bfloat16), rank_side_sketch[1], preferred_element_type=jnp.float32
    )
    narrow_cols = rank_side_sketch.shape[2]
    right_rows = jnp.stack([right_out.astype(jnp.bfloat16), right_in.astype(jnp.bfloat16)], axis=1)
    right_rows = right_rows.reshape(ex_dev, seq_len, 2, narrow_cols)
    positions = jnp.arange(seq_len, dtype=jnp.int32)
    live_mask = positions[None, :] < lengths[:, None]
    right_rows = jnp.where(live_mask[:, :, None, None], right_rows, jnp.zeros_like(right_rows))
    right_f32 = right_rows.astype(jnp.float32)
    local_out = jnp.dot(flattened_output, width_side_sketch, preferred_element_type=jnp.float32)
    local_in = jnp.dot(flattened_input, width_side_sketch, preferred_element_type=jnp.float32)
    local_left = jnp.stack([local_out, local_in], axis=1).reshape(
        ex_dev, seq_len, 2, width_side_sketch.shape[1]
    )
    partial_proj = jnp.einsum("etpk,etpq->ekpq", local_left, right_f32)
    partial_proj = partial_proj.reshape(ex_dev, width_side_sketch.shape[1] * 2 * narrow_cols)
    summed = lax.psum_scatter(partial_proj, "proj", scatter_dimension=1, tiled=True)
    summed = summed / lengths.astype(jnp.float32)[:, None]
    train_proj = summed.astype(jnp.bfloat16)
    train_f32 = train_proj.astype(jnp.float32)
    train_sq = jnp.sum(train_f32 * train_f32, axis=1)
    nval_all = heldout_gradient_rows.shape[0] * lax.axis_size("ex")
    shard_piece = lax.all_gather(heldout_gradient_rows, "ex", axis=0, tiled=True)
    products = lax.dot_general(
        train_proj, shard_piece, (((1,), (1,)), ((), ())), preferred_element_type=jnp.float32
    )
    piece_f32 = shard_piece.astype(jnp.float32)
    squares = jnp.sum(piece_f32 * piece_f32, axis=1)[None, :]
    dots_whole, train_total, val_whole = lax.psum((products, train_sq, squares), "proj")
    col_share = nval_all // lax.axis_size("proj")
    col_begin = lax.axis_index("proj") * col_share
    dots_own = lax.dynamic_slice_in_dim(dots_whole, col_begin, col_share, 1)
    val_own = lax.dynamic_slice_in_dim(val_whole, col_begin, col_share, 1)
    scale_factor = math.sqrt(PDIM)
    scores = (
        scale_factor
        * dots_own
        * lax.rsqrt(train_total + epsilon)[:, None]
        * lax.rsqrt(val_own + epsilon)
    )
    return (train_proj, scores)


def solution(mesh):
    in_specs = (
        P(("grp", "ex"), None, "proj"),
        P(("grp", "ex"), None, "proj"),
        P(("grp", "ex")),
        P(None, "proj"),
        P("proj", None),
        P("proj", None),
        P(),
        P(("grp", "ex"), "proj"),
    )
    out_specs = (P(("grp", "ex"), "proj"), P(("grp", "ex"), "proj"))
    return jax.shard_map(shards, mesh=mesh, in_specs=in_specs, out_specs=out_specs, check_vma=False)
```

profile of v0, /device:TPU:0, one launch (start us, length us, event | category | flops | bytes accessed | tf_op | source)
XLA Modules:
  0.0 98.1 jit_solution(624040984430771321)
XLA Ops:
  7.2 0.0 reduce-scatter.4.cloned.1.call-start
  7.2 1.3 %copy-done = bf16[4,144,1280]{2,1,0:T(8,128)(2,1)S(1)} copy-done((bf16[4,144,1280]{2,1,0:T(8,128)(2,1)S(1)}, bf16[4,144,1280]{2,1,0:T(8,128)(2,1)}, u32[]{:S(2)}) %copy-start) | copy-done | bytes 1474584
  8.5 1.5 %fusion.19 = f32[576,128]{1,0:T(8,128)S(1)} fusion(bf16[576,1280]{1,0:T(8,128)(2,1)S(1)} %bitcast.40, bf16[128,1280]{1,0:T(8,128)(2,1)} %param.11), kind=kOutput, calls=%fused_computation.30 | convolution fusion | flops 188743680 | bytes 2097152 | tf_op jit(solution)/shard_map/dot_general | solution.py:28
  10.1 1.7 %convolution_bitcast_fusion = bf16[4,144,1,512]{3,1,0,2:T(8,128)(2,1)} fusion(bf16[4,144,1280]{2,1,0:T(8,128)(2,1)S(1)} %copy-done, bf16[1280,512]{1,0:T(8,128)(2,1)S(1)} %copy-done.6), kind=kOutput, calls=%fused_computation.3 | convolution fusion | flops 754974720 | bytes 3375104 | tf_op jit(solution)/shard_map/dot_general | solution.py:52
  11.8 1.7 %convolution_bitcast_fusion.1 = bf16[4,144,1,512]{3,1,0,2:T(8,128)(2,1)} fusion(bf16[4,144,1280]{2,1,0:T(8,128)(2,1)S(1)} %copy-done.1, bf16[1280,512]{1,0:T(8,128)(2,1)S(1)} %copy-done.6), kind=kOutput, calls=%fused_computation.4 | convolution fusion | flops 754974720 | bytes 3375104 | tf_op jit(solution)/shard_map/dot_general | solution.py:51
  13.6 0.5 fusion.20
  14.1 18.8 %all-reduce.3 = (bf16[576,128]{1,0:T(8,128)(2,1)S(1)}, bf16[576,128]{1,0:T(8,128)(2,1)S(1)}) all-reduce(f32[576,128]{1,0:T(8,128)S(1)} %fusion.20, f32[576,128]{1,0:T(8,128)S(1)} %fusion.19), channel_id=1, replica_groups=mesh['grp'=2,'ex'=4,'proj'=4] {'proj'}, use_global_device_ids=true, to_apply=%region_1.0 | all-reduce | flops 147456 | bytes 884736 | tf_op jit(solution)/shard_map/psum | solution.py:37
  32.9 0.1 convolution_convert_fusion.1
  33.1 0.1 stack.14
  33.2 0.1 convolution_convert_fusion
  33.3 0.1 stack.15
  33.5 0.1 iota_compare_fusion
  33.6 0.3 fusion.4
  33.8 3.5 %copy.23 = f32[4,512,2,8]{0,3,2,1:T(8,128)} copy(f32[4,512,2,8]{1,3,2,0:T(8,128)S(1)} %fusion.4) | data formatting | bytes 262144
  37.3 0.9 copy-done.3
  38.2 15.5 %all_gather.3 = bf16[128,2048]{1,0:T(8,128)(2,1)S(1)} all-gather(bf16[32,2048]{1,0:T(8,128)(2,1)S(1)} %copy-done.3), channel_id=1, replica_groups=mesh['grp'=2,'ex'=4,'proj'=4] {'ex'}, dimensions={0}, use_global_device_ids=true | all-gather | bytes 655360 | tf_op jit(solution)/shard_map/all_gather | solution.py:64
  53.7 0.2 multiply_reduce_fusion
  53.9 28.9 %reduce-scatter.4.cloned.1.call-done = f32[2048,4]{1,0:T(8,128)} async-done(((f32[8192,4]{1,0:T(8,128)}), f32[2048,4]{1,0:T(8,128)}) %reduce-scatter.4.cloned.1.call-update) | async-done | bytes 32784
  82.7 1.6 %copy.22 = f32[4,2048]{1,0:T(4,128)S(1)} copy(f32[4,2048]{0,1:T(8,128)} %bitcast.43) | data formatting | bytes 65536
  84.3 0.2 multiply_reduce_fusion.1
  84.5 0.2 fusion.21
  84.7 5.7 %all-reduce = (f32[4,128]{1,0:T(4,128)S(1)}, f32[1,128]{1,0:T(1,128)S(1)}, f32[4]{0:T(128)S(1)}) all-reduce(f32[4,128]{1,0:T(4,128)S(1)} %fusion.21, f32[1,128]{1,0:T(1,128)S(1)} %bitcast.44, f32[4]{0:T(128)S(1)} %get-tuple-element.7), channel_id=1, replica_groups=mesh['grp'=2,'ex'=4,'proj'=4] {'proj'}, use_global_device_ids=true, to_apply=%region_3.4 | all-reduce | flops 644 | bytes 5152 | tf_op jit(solution)/shard_map/psum | solution.py:70
  90.5 0.1 rsqrt_bitcast_fusion
  90.6 0.7 multiply_multiply_fusion
  (23 shorter events, 0.1 us)
Async XLA Ops:
  7.2 1.4 %copy-start = (bf16[4,144,1280]{2,1,0:T(8,128)(2,1)S(1)}, bf16[4,144,1280]{2,1,0:T(8,128)(2,1)}, u32[]{:S(2)}) copy-start(bf16[4,144,1280]{2,1,0:T(8,128)(2,1)} %param.8) | copy-start | bytes 4423684
  7.2 2.9 %copy-start.6 = (bf16[1280,512]{1,0:T(8,128)(2,1)S(1)}, bf16[1280,512]{1,0:T(8,128)(2,1)}, u32[]{:S(2)}) copy-start(bf16[1280,512]{1,0:T(8,128)(2,1)} %param.13) | copy-start | bytes 3932164
  7.2 75.5 %reduce-scatter.4.cloned.1.call-start = ((), (), s32[]{:S(2)}) async-start(), calls=%async_computation.1 | async-start | bytes 5242880
  10.1 1.8 %copy-start.1 = (bf16[4,144,1280]{2,1,0:T(8,128)(2,1)S(1)}, bf16[4,144,1280]{2,1,0:T(8,128)(2,1)}, u32[]{:S(2)}) copy-start(bf16[4,144,1280]{2,1,0:T(8,128)(2,1)} %param.9) | copy-start | bytes 4423684
  11.8 1.7 %copy-start.2 = (bf16[1280,128]{1,0:T(8,128)(2,1)S(1)}, bf16[1280,128]{1,0:T(8,128)(2,1)}, u32[]{:S(2)}) copy-start(bf16[1280,128]{1,0:T(8,128)(2,1)} %param.12) | copy-start | bytes 983044
  13.6 19.4 %copy-start.5 = (bf16[2,128,8]{1,2,0:T(8,128)(2,1)S(1)}, bf16[2,128,8]{1,2,0:T(8,128)(2,1)}, u32[]{:S(2)}) copy-start(bf16[2,128,8]{1,2,0:T(8,128)(2,1)} %param.14) | copy-start | bytes 12292
  13.6 19.9 %copy-start.7 = (s32[4]{0:T(128)S(1)}, s32[4]{0:T(128)}, u32[]{:S(2)}) copy-start(s32[4]{0:T(128)} %param.10) | copy-start | bytes 52
  13.6 20.0 %copy-start.8 = (bf16[4,144,1,512]{3,1,0,2:T(8,128)(2,1)S(1)}, bf16[4,144,1,512]{3,1,0,2:T(8,128)(2,1)}, u32[]{:S(2)}) copy-start(bf16[4,144,1,512]{3,1,0,2:T(8,128)(2,1)} %convolution_bitcast_fusion) | copy-start | bytes 1769476
  13.6 20.0 %copy-start.9 = (bf16[4,144,1,512]{3,1,0,2:T(8,128)(2,1)S(1)}, bf16[4,144,1,512]{3,1,0,2:T(8,128)(2,1)}, u32[]{:S(2)}) copy-start(bf16[4,144,1,512]{3,1,0,2:T(8,128)(2,1)} %convolution_bitcast_fusion.1) | copy-start | bytes 1769476
  37.3 0.9 copy-start.3
  84.5 6.7 %copy-start.4 = (bf16[4,2048]{1,0:T(4,128)(2,1)}, bf16[4,2048]{1,0:T(4,128)(2,1)S(1)}, u32[]{:S(2)}) copy-start(bf16[4,2048]{1,0:T(4,128)(2,1)S(1)} %get-tuple-element.8) | copy-start | bytes 49156
Sparse Core Ops, SparseCore 0:
  37.4 45.2 reduce-scatter.3
where the time goes:
time: 98.3 us; the launch traced here: 98.1 us
  blocking collectives  40 us (41%)
  waiting for transfers between devices  28.9 us (29%)
  between operations  14.2 us (14%)
  local copies, waits for them, and re-layouts  7.42 us (8%)
  matrix products  6.31 us (6%)
  other arithmetic  1.22 us (1%)
    unnamed x2, waiting for transfers between devices  28.9 us
    psum x1, blocking collectives, shards(): summed_in, summed_out = lax.psum((partial_in, incomplete_output), 'proj')  18.8 us
    all_gather x1, blocking collectives, shards(): lax.all_gather(heldout_gradient_rows, 'ex', axis=0, tiled=True)  15.5 us
    unnamed x22, local copies, waits for them, and re-layouts  7.23 us
    psum x1, blocking collectives, shards(): lax.psum((products, train_sq, squares), 'proj')  5.75 us
  transfers between devices with their start and end apart: 1, of which 1 were waited for; matrix products, arithmetic and copies ran while one was open for 0% of the time, Pallas kernels for 0%

commit v1 on v0

v1 whole, which is shorter than its diff:
```python
import math

import jax
import jax.numpy as jnp
from jax import lax
from jax.sharding import PartitionSpec as P

epsilon = 1e-06


def swap(x, axis, mask):
    size = lax.axis_size(axis)
    return lax.ppermute(x, axis, [(i, i ^ mask) for i in range(size)])


def shards(
    inputs,
    cotangents,
    lengths,
    adapter_down_matrix,
    adapter_up_matrix,
    width_side_sketch,
    rank_side_sketch,
    heldout_gradient_rows,
):
    ex_dev, seq_len, model_cols = inputs.shape
    row_count = ex_dev * seq_len
    k1 = width_side_sketch.shape[1]
    k2 = rank_side_sketch.shape[2]
    n_proj, n_ex = lax.axis_size("proj"), lax.axis_size("ex")
    me_proj, me_ex = lax.axis_index("proj"), lax.axis_index("ex")
    k_own = k1 // n_proj
    pdim = k1 * 2 * k2
    f32, bf16 = jnp.float32, jnp.bfloat16
    acts = inputs.reshape(row_count, model_cols)
    cots = cotangents.reshape(row_count, model_cols)

    if n_ex == n_proj:
        rows = [heldout_gradient_rows] + [swap(heldout_gradient_rows, "ex", m) for m in range(1, n_ex)]
        order = [me_ex ^ m for m in range(n_ex)]
    else:
        every = lax.all_gather(heldout_gradient_rows, "ex", axis=0, tiled=True)
        share = every.shape[0] // n_proj
        rows = [every[s * share : (s + 1) * share] for s in range(n_proj)]
        order = list(range(n_proj))

    down = lax.dot_general(rank_side_sketch[0], adapter_down_matrix, (((0,), (0,)), ((), ())), preferred_element_type=f32)
    up = lax.dot_general(rank_side_sketch[1], adapter_up_matrix, (((0,), (1,)), ((), ())), preferred_element_type=f32)
    right_out = lax.dot_general(down.astype(bf16), acts, (((1,), (1,)), ((), ())), preferred_element_type=f32)
    right_in = lax.dot_general(up.astype(bf16), cots, (((1,), (1,)), ((), ())), preferred_element_type=f32)
    right = jnp.concatenate([right_out, right_in], axis=0)
    right = sum([swap(right, "proj", m) for m in range(1, n_proj)], right).astype(bf16)

    t = jnp.arange(row_count, dtype=jnp.int32)
    e = jnp.arange(ex_dev, dtype=jnp.int32)[:, None]
    live = (t[None, :] >= e * seq_len) & (t[None, :] < e * seq_len + lengths[:, None])
    spread = jnp.where(live[None, :, None, :], right.reshape(2, 1, k2, row_count), jnp.zeros((), bf16))
    spread = spread.reshape(2, ex_dev * k2, row_count)
    parts = []
    for p, rows_of in enumerate((cots, acts)):
        wide = jnp.dot(spread[p], rows_of, preferred_element_type=f32)
        parts.append(jnp.dot(wide.astype(bf16), width_side_sketch, preferred_element_type=f32))
    partial = jnp.concatenate(parts, axis=0)
    own = lax.dynamic_slice_in_dim(partial, me_proj * k_own, k_own, 1)
    for m in range(1, n_proj):
        piece = lax.dynamic_slice_in_dim(partial, (me_proj ^ m) * k_own, k_own, 1)
        own = own + swap(piece, "proj", m)
    own = own.reshape(2, ex_dev, k2, k_own) / lengths.astype(f32)[None, :, None, None]
    train_proj = own.transpose(1, 3, 0, 2).reshape(ex_dev, k_own * 2 * k2).astype(bf16)
    train_f32 = train_proj.astype(f32)
    train_sq = jnp.sum(train_f32 * train_f32, axis=1, keepdims=True)

    notes = []
    for block in rows:
        dots = lax.dot_general(train_proj, block, (((1,), (1,)), ((), ())), preferred_element_type=f32)
        block_f32 = block.astype(f32)
        val_sq = jnp.sum(block_f32 * block_f32, axis=1)[None, :]
        notes.append(jnp.concatenate([dots, val_sq], axis=0))
    notes = jnp.stack(notes)
    train_total = train_sq
    if n_ex == n_proj:
        place = [me_ex ^ me_proj ^ m for m in range(n_proj)]
    else:
        place = [me_proj ^ m for m in range(n_proj)]
    share = notes.shape[2]
    tail = jnp.concatenate([train_sq, jnp.zeros((1, 1), f32)], axis=0)
    total = None
    for m in range(n_proj):
        note = jnp.concatenate([lax.dynamic_index_in_dim(notes, place[m], 0, keepdims=False), tail], axis=1)
        got = note if m == 0 else swap(note, "proj", m)
        total = got if total is None else total + got
    scores = (
        math.sqrt(pdim)
        * total[:ex_dev, :share]
        * lax.rsqrt(total[:ex_dev, share:] + epsilon)
        * lax.rsqrt(total[ex_dev:, :share] + epsilon)
    )
    return (train_proj, scores)


def solution(mesh):
    in_specs = (
        P(("grp", "ex"), None, "proj"),
        P(("grp", "ex"), None, "proj"),
        P(("grp", "ex")),
        P(None, "proj"),
        P("proj", None),
        P("proj", None),
        P(),
        P(("grp", "ex"), "proj"),
    )
    out_specs = (P(("grp", "ex"), "proj"), P(("grp", "ex"), "proj"))
    return jax.shard_map(shards, mesh=mesh, in_specs=in_specs, out_specs=out_specs, check_vma=False)
```

time: 98.3 us -> 32.7 us (0.33)
  blocking collectives: 40 us -> 0 us
  waiting for transfers between devices: 28.9 us -> 6.32 us
  between operations: 14.2 us -> 0.86 us
  starting transfers between devices: 0.04 us -> 13.1 us
  local copies, waits for them, and re-layouts: 7.42 us -> 0.63 us
  other arithmetic: 1.22 us -> 4.59 us
    unnamed x2 -> x0, waiting for transfers between devices: 28.9 us -> none
    psum x2 -> x0, blocking collectives: 24.5 us -> none  [the longest x1 18.8 us: shards(): summed_in, summed_out = lax.psum((partial_in, incomplete_output), 'proj')]
    all_gather x1 -> x0, blocking collectives: 15.5 us -> none  [shards(): lax.all_gather(heldout_gradient_rows, 'ex', axis=0, tiled=True)]
    ppermute x0 -> x12, starting transfers between devices: none -> 13.1 us  [swap(): return lax.ppermute(x, axis, [(i, i ^ mask) for i in range(size)])]
    unnamed x22 -> x14, local copies, waits for them, and re-layouts: 7.23 us -> 0.06 us
    ppermute x0 -> x12, waiting for transfers between devices: none -> 6.32 us  [swap(): return lax.ppermute(x, axis, [(i, i ^ mask) for i in range(size)])]
    reduce_sum x2 -> x5, other arithmetic: 0.4 us -> 1.42 us  [the longest x1 0.84 us: shards(): train_sq = jnp.sum(train_f32 * train_f32, axis=1, keepdims=True)]
  transfers between devices with their start and end apart: 1 -> 12, of which waited for: 1 -> 5; matrix products, arithmetic and copies ran while one was open for 0% -> 25% of each run, Pallas kernels for 0% -> 0%
where the time goes in v1:
time: 32.7 us; the launch traced here: 32.5 us
  starting transfers between devices  13.1 us (40%)
  matrix products  7.03 us (21%)
  waiting for transfers between devices  6.32 us (19%)
  other arithmetic  4.59 us (14%)
  between operations  0.86 us (3%)
  local copies, waits for them, and re-layouts  0.63 us (2%)
    ppermute x12, starting transfers between devices, swap(): return lax.ppermute(x, axis, [(i, i ^ mask) for i in range(size)])  13.1 us
    ppermute x12, waiting for transfers between devices, swap(): return lax.ppermute(x, axis, [(i, i ^ mask) for i in range(size)])  6.32 us
    dot_general x2, matrix products, shards(): jnp.dot(wide.astype(bf16), width_side_sketch, preferred_element_type=f32)  3.69 us
    dot_general x1, matrix products, shards(): lax.dot_general(down.astype(bf16), acts, (((1,), (1,)), ((), ())), prefer...  2.18 us
    mul x3, other arithmetic, shards(): math.sqrt(pdim) * total[:ex_dev, :share]  0.85 us
    reduce_sum x1, other arithmetic, shards(): train_sq = jnp.sum(train_f32 * train_f32, axis=1, keepdims=True)  0.84 us
    select_n x1, other arithmetic, shards(): jnp.where(live[None, :, None, :], right.reshape(2, 1, k2, row_count), jnp...  0.82 us
  transfers between devices with their start and end apart: 12, of which 5 were waited for; matrix products, arithmetic and copies ran while one was open for 25% of the time, Pallas kernels for 0%

profile of v1, /device:TPU:0, one launch (start us, length us, event | category | flops | bytes accessed | tf_op | source)
XLA Modules:
  0.0 32.5 jit_solution(9689652412700423818)
XLA Ops:
  0.7 2.2 %fusion.2 = f32[8,576]{1,0:T(8,128)S(1)} fusion(bf16[576,1280]{1,0:T(8,128)(2,1)} %bitcast.63, bf16[128,1280]{1,0:T(8,128)(2,1)} %param.11, bf16[2,128,8]{1,2,0:T(8,128)(2,1)} %param.14), kind=kOutput, calls=%fused_computation.6 | convolution fusion | flops 14428160 | bytes 1822720 | tf_op jit(solution)/shard_map/dot_general | solution.py:49
  2.9 0.6 %fusion.3 = f32[8,576]{1,0:T(8,128)S(1)} fusion(bf16[576,1280]{1,0:T(8,128)(2,1)S(1)} %bitcast.61, bf16[1280,128]{1,0:T(8,128)(2,1)S(1)} %copy-done.2, bf16[2,128,8]{1,2,0:T(8,128)(2,1)S(1)} %copy-done.5), kind=kOutput, calls=%fused_computation.7 | convolution fusion | flops 14428160 | bytes 1822720 | tf_op jit(solution)/shard_map/dot_general | solution.py:50
  3.5 0.5 %collective-permute-start = (f32[16,576]{1,0:T(8,128)S(1)}, f32[16,576]{1,0:T(8,128)S(1)}, u32[]{:S(2)}, u32[]{:S(2)}) collective-permute-start(f32[16,576]{1,0:T(8,128)S(1)} %pad_maximum_fusion), channel_id=1, source_target_pairs={{0,1},{1,0},{2,3},{3,2},{4,5},{5,4},{6,7},{7,6},{8,9},{9,8},{10,11... | collective-permute-start | bytes 110600 | tf_op jit(solution)/shard_map/ppermute | solution.py:13
  4.0 2.6 %collective-permute-start.1 = (f32[16,576]{1,0:T(8,128)S(1)}, f32[16,576]{1,0:T(8,128)S(1)}, u32[]{:S(2)}, u32[]{:S(2)}) collective-permute-start(f32[16,576]{1,0:T(8,128)S(1)} %pad_maximum_fusion), channel_id=1, source_target_pairs={{0,2},{1,3},{2,0},{3,1},{4,6},{5,7},{6,4},{7,5},{8,10},{9,11},{10,... | collective-permute-start | bytes 110600 | tf_op jit(solution)/shard_map/ppermute | solution.py:13
  6.6 1.8 %collective-permute-start.6 = (bf16[32,2048]{1,0:T(8,128)(2,1)S(1)}, bf16[32,2048]{1,0:T(8,128)(2,1)S(1)}, u32[]{:S(2)}, u32[]{:S(2)}) collective-permute-start(bf16[32,2048]{1,0:T(8,128)(2,1)S(1)} %copy-done.3), channel_id=1, source_target_pairs={{0,4},{4,0},{8,12},{12,8},{1,5},{5,1},{9,13},{13,9},{2,6},{6,2},{1... | collective-permute-start | bytes 393224 | tf_op jit(solution)/shard_map/ppermute | solution.py:13
  8.5 2.6 %collective-permute-start.7 = (bf16[32,2048]{1,0:T(8,128)(2,1)S(1)}, bf16[32,2048]{1,0:T(8,128)(2,1)S(1)}, u32[]{:S(2)}, u32[]{:S(2)}) collective-permute-start(bf16[32,2048]{1,0:T(8,128)(2,1)S(1)} %copy-done.3), channel_id=1, source_target_pairs={{0,8},{4,12},{8,0},{12,4},{1,9},{5,13},{9,1},{13,5},{2,10},{6,14},... | collective-permute-start | bytes 393224 | tf_op jit(solution)/shard_map/ppermute | solution.py:13
  11.0 0.5 %fusion.24 = (f32[4]{0:T(128)}, s32[4]{0:T(128)S(1)}) fusion(s32[4]{0:T(128)S(1)} %copy-done.6), kind=kLoop, calls=%fused_computation.63 | loop fusion | flops 12 | bytes 48 | tf_op jit(solution)/shard_map/convert_element_type | solution.py:68
  11.6 0.7 %fusion.12 = pred[4,576]{1,0:T(4,128)(4,1)} fusion(s32[4]{0:T(128)S(1)} %get-tuple-element.15, s32[4]{0:T(128)S(1)} %iota_multiply_fusion), kind=kLoop, calls=%fused_computation.38 | loop fusion | flops 6912 | bytes 2336 | tf_op jit(solution)/shard_map/and | solution.py:56
  12.3 0.8 %broadcast_select_fusion = bf16[2,4,8,576]{3,2,1,0:T(8,128)(2,1)S(1)} fusion(pred[4,576]{1,0:T(4,128)(4,1)} %fusion.12, bf16[2,8,576]{2,1,0:T(8,128)(2,1)S(1)} %fusion.11), kind=kLoop, calls=%fused_computation.20 | loop fusion | flops 36864 | bytes 94464 | tf_op jit(solution)/shard_map/jit(_where)/select_n | solution.py:57
  13.1 1.8 %fusion = f32[32,512]{1,0:T(8,128)S(1)} fusion(bf16[1280,512]{1,0:T(8,128)(2,1)} %param.13, bf16[576,1280]{1,0:T(8,128)(2,1)S(1)} %bitcast.62, bf16[2,4,8,576]{3,2,1,0:T(8,128)(2,1)S(1)} %broadcast_select_fusion), kind=kOutput, calls=%fused_computation.4 | convolution fusion | flops 89169920 | bytes 2891776 | tf_op jit(solution)/shard_map/dot_general | solution.py:62
  14.9 1.8 %fusion.1 = f32[32,512]{1,0:T(8,128)S(1)} fusion(bf16[1280,512]{1,0:T(8,128)(2,1)} %param.13, bf16[576,1280]{1,0:T(8,128)(2,1)S(1)} %bitcast.64, bf16[2,4,8,576]{3,2,1,0:T(8,128)(2,1)S(1)} %broadcast_select_fusion), kind=kOutput, calls=%fused_computation.5 | convolution fusion | flops 89169920 | bytes 2891776 | tf_op jit(solution)/shard_map/dot_general | solution.py:62
  16.9 1.6 %collective-permute-start.4 = (f32[64,128]{1,0:T(8,128)S(1)}, f32[64,128]{1,0:T(8,128)S(1)}, u32[]{:S(2)}, u32[]{:S(2)}) collective-permute-start(f32[64,128]{1,0:T(8,128)S(1)} %get-tuple-element.5), channel_id=1, source_target_pairs={{0,2},{1,3},{2,0},{3,1},{4,6},{5,7},{6,4},{7,5},{8,10},{9,11},{10,... | collective-permute-start | bytes 98312 | tf_op jit(solution)/shard_map/ppermute | solution.py:13
  18.5 0.3 collective-permute-start.5
  18.9 1.5 %collective-permute-start.8 = (bf16[32,2048]{1,0:T(8,128)(2,1)S(1)}, bf16[32,2048]{1,0:T(8,128)(2,1)S(1)}, u32[]{:S(2)}, u32[]{:S(2)}) collective-permute-start(bf16[32,2048]{1,0:T(8,128)(2,1)S(1)} %copy-done.3), channel_id=1, source_target_pairs={{0,12},{4,8},{8,4},{12,0},{1,13},{5,9},{9,5},{13,1},{2,14},{6,10},... | collective-permute-start | bytes 393224 | tf_op jit(solution)/shard_map/ppermute | solution.py:13
  20.5 0.4 %collective-permute-done.4 = f32[64,128]{1,0:T(8,128)S(1)} collective-permute-done((f32[64,128]{1,0:T(8,128)S(1)}, f32[64,128]{1,0:T(8,128)S(1)}, u32[]{:S(2)}, u32[]{:S(2)}) %collective-permute-start.4) | collective-permute-done | bytes 32800 | tf_op jit(solution)/shard_map/ppermute | solution.py:13
  20.9 0.9 %collective-permute-done.5 = f32[64,128]{1,0:T(8,128)S(1)} collective-permute-done((f32[64,128]{1,0:T(8,128)S(1)}, f32[64,128]{1,0:T(8,128)S(1)}, u32[]{:S(2)}, u32[]{:S(2)}) %collective-permute-start.5) | collective-permute-done | bytes 32800 | tf_op jit(solution)/shard_map/ppermute | solution.py:13
  21.8 0.8 %multiply_reduce_fusion.4 = (f32[4]{0:T(128)S(1)}, bf16[2,4,8,128]{3,2,1,0:T(8,128)(2,1)S(1)}) fusion(f32[2,4,8,128]{3,2,1,0:T(8,128)S(1)} %bitcast.65, f32[4]{0:T(128)} %get-tuple-element.14), kind=kLoop, calls=%fused_computation.32 | loop fusion | flops 40956 | bytes 49184 | tf_op jit(solution)/shard_map/reduce_sum | solution.py:71
  22.8 0.3 convert_element_type.54
  24.1 2.6 %collective-permute-done.8 = bf16[32,2048]{1,0:T(8,128)(2,1)S(1)} collective-permute-done((bf16[32,2048]{1,0:T(8,128)(2,1)S(1)}, bf16[32,2048]{1,0:T(8,128)(2,1)S(1)}, u32[]{:S(2)}, u32[]{:S(2)}) %collective-permute-start.8) | collective-permute-done | bytes 131104 | tf_op jit(solution)/shard_map/ppermute | solution.py:13
  27.1 1.5 %collective-permute-start.10 = (f32[5,33]{1,0:T(8,128)S(1)}, f32[5,33]{1,0:T(8,128)S(1)}, u32[]{:S(2)}, u32[]{:S(2)}) collective-permute-start(f32[5,33]{1,0:T(8,128)S(1)} %get-tuple-element.12), channel_id=1, source_target_pairs={{0,2},{1,3},{2,0},{3,1},{4,6},{5,7},{6,4},{7,5},{8,10},{9,11},{10,... | collective-permute-start | bytes 1988 | tf_op jit(solution)/shard_map/ppermute | solution.py:13
  28.6 0.6 %collective-permute-start.9 = (f32[5,33]{1,0:T(8,128)S(1)}, f32[5,33]{1,0:T(8,128)S(1)}, u32[]{:S(2)}, u32[]{:S(2)}) collective-permute-start(f32[5,33]{1,0:T(8,128)S(1)} %get-tuple-element.11), channel_id=1, source_target_pairs={{0,1},{1,0},{2,3},{3,2},{4,5},{5,4},{6,7},{7,6},{8,9},{9,8},{10,11... | collective-permute-start | bytes 1988 | tf_op jit(solution)/shard_map/ppermute | solution.py:13
  29.2 1.5 %collective-permute-done.10 = f32[5,33]{1,0:T(8,128)S(1)} collective-permute-done((f32[5,33]{1,0:T(8,128)S(1)}, f32[5,33]{1,0:T(8,128)S(1)}, u32[]{:S(2)}, u32[]{:S(2)}) %collective-permute-start.10) | collective-permute-done | bytes 692 | tf_op jit(solution)/shard_map/ppermute | solution.py:13
  30.7 0.9 %collective-permute-done.11 = f32[5,33]{1,0:T(8,128)S(1)} collective-permute-done((f32[5,33]{1,0:T(8,128)S(1)}, f32[5,33]{1,0:T(8,128)S(1)}, u32[]{:S(2)}, u32[]{:S(2)}) %collective-permute-start.11) | collective-permute-done | bytes 692 | tf_op jit(solution)/shard_map/ppermute | solution.py:13
  31.9 0.7 %multiply_multiply_fusion = f32[4,32]{1,0:T(4,128)} fusion(f32[5,33]{1,0:T(8,128)S(1)} %fusion.14, f32[32]{0:T(128)S(1)} %rsqrt_bitcast_fusion, f32[4]{0:T(128)S(1)} %multiply_reduce_fusion.5), kind=kLoop, calls=%fused_computation.55 | loop fusion | flops 256 | bytes 1168 | tf_op jit(solution)/shard_map/mul | solution.py:93
  (50 shorter events, 2.2 us)
Async XLA Ops:
  0.6 2.2 %copy-start = (bf16[4,144,1280]{2,1,0:T(8,128)(2,1)S(1)}, bf16[4,144,1280]{2,1,0:T(8,128)(2,1)}, u32[]{:S(2)}) copy-start(bf16[4,144,1280]{2,1,0:T(8,128)(2,1)} %param.9) | copy-start | bytes 4423684
  0.6 2.2 %copy-start.5 = (bf16[2,128,8]{1,2,0:T(8,128)(2,1)S(1)}, bf16[2,128,8]{1,2,0:T(8,128)(2,1)}, u32[]{:S(2)}) copy-start(bf16[2,128,8]{1,2,0:T(8,128)(2,1)} %param.14) | copy-start | bytes 12292
  0.7 2.2 %copy-start.2 = (bf16[1280,128]{1,0:T(8,128)(2,1)S(1)}, bf16[1280,128]{1,0:T(8,128)(2,1)}, u32[]{:S(2)}) copy-start(bf16[1280,128]{1,0:T(8,128)(2,1)} %param.12) | copy-start | bytes 983044
  0.7 6.0 %copy-start.3 = (bf16[32,2048]{1,0:T(8,128)(2,1)S(1)}, bf16[32,2048]{1,0:T(8,128)(2,1)}, u32[]{:S(2)}) copy-start(bf16[32,2048]{1,0:T(8,128)(2,1)} %param.15) | copy-start | bytes 393220
  0.7 10.4 %copy-start.6 = (s32[4]{0:T(128)S(1)}, s32[4]{0:T(128)}, u32[]{:S(2)}) copy-start(s32[4]{0:T(128)} %param.10) | copy-start | bytes 52
  3.5 8.7 %collective-permute-start = (f32[16,576]{1,0:T(8,128)S(1)}, f32[16,576]{1,0:T(8,128)S(1)}, u32[]{:S(2)}, u32[]{:S(2)}) collective-permute-start(f32[16,576]{1,0:T(8,128)S(1)} %pad_maximum_fusion), channel_id=1, source_target_pairs={{0,1},{1,0},{2,3},{3,2},{4,5},{5,4},{6,7},{7,6},{8,9},{9,8},{10,11... | collective-permute-start | bytes 110600 | tf_op jit(solution)/shard_map/ppermute | solution.py:13
  4.0 8.2 %collective-permute-start.1 = (f32[16,576]{1,0:T(8,128)S(1)}, f32[16,576]{1,0:T(8,128)S(1)}, u32[]{:S(2)}, u32[]{:S(2)}) collective-permute-start(f32[16,576]{1,0:T(8,128)S(1)} %pad_maximum_fusion), channel_id=1, source_target_pairs={{0,2},{1,3},{2,0},{3,1},{4,6},{5,7},{6,4},{7,5},{8,10},{9,11},{10,... | collective-permute-start | bytes 110600 | tf_op jit(solution)/shard_map/ppermute | solution.py:13
  6.6 5.7 %collective-permute-start.2 = (f32[16,576]{1,0:T(8,128)S(1)}, f32[16,576]{1,0:T(8,128)S(1)}, u32[]{:S(2)}, u32[]{:S(2)}) collective-permute-start(f32[16,576]{1,0:T(8,128)S(1)} %pad_maximum_fusion), channel_id=1, source_target_pairs={{0,3},{1,2},{2,1},{3,0},{4,7},{5,6},{6,5},{7,4},{8,11},{9,10},{10,... | collective-permute-start | bytes 110600 | tf_op jit(solution)/shard_map/ppermute | solution.py:13
  6.6 16.8 %collective-permute-start.6 = (bf16[32,2048]{1,0:T(8,128)(2,1)S(1)}, bf16[32,2048]{1,0:T(8,128)(2,1)S(1)}, u32[]{:S(2)}, u32[]{:S(2)}) collective-permute-start(bf16[32,2048]{1,0:T(8,128)(2,1)S(1)} %copy-done.3), channel_id=1, source_target_pairs={{0,4},{4,0},{8,12},{12,8},{1,5},{5,1},{9,13},{13,9},{2,6},{6,2},{1... | collective-permute-start | bytes 393224 | tf_op jit(solution)/shard_map/ppermute | solution.py:13
  8.5 15.3 %collective-permute-start.7 = (bf16[32,2048]{1,0:T(8,128)(2,1)S(1)}, bf16[32,2048]{1,0:T(8,128)(2,1)S(1)}, u32[]{:S(2)}, u32[]{:S(2)}) collective-permute-start(bf16[32,2048]{1,0:T(8,128)(2,1)S(1)} %copy-done.3), channel_id=1, source_target_pairs={{0,8},{4,12},{8,0},{12,4},{1,9},{5,13},{9,1},{13,5},{2,10},{6,14},... | collective-permute-start | bytes 393224 | tf_op jit(solution)/shard_map/ppermute | solution.py:13
  12.2 2.7 %copy-start.1 = (bf16[4,144,1280]{2,1,0:T(8,128)(2,1)S(1)}, bf16[4,144,1280]{2,1,0:T(8,128)(2,1)}, u32[]{:S(2)}) copy-start(bf16[4,144,1280]{2,1,0:T(8,128)(2,1)} %param.8) | copy-start | bytes 4423684
  16.8 2.1 %collective-permute-start.3 = (f32[64,128]{1,0:T(8,128)S(1)}, f32[64,128]{1,0:T(8,128)S(1)}, u32[]{:S(2)}, u32[]{:S(2)}) collective-permute-start(f32[64,128]{1,0:T(8,128)S(1)} %get-tuple-element.4), channel_id=1, source_target_pairs={{0,1},{1,0},{2,3},{3,2},{4,5},{5,4},{6,7},{7,6},{8,9},{9,8},{10,11... | collective-permute-start | bytes 98312 | tf_op jit(solution)/shard_map/ppermute | solution.py:13
  16.9 4.0 %collective-permute-start.4 = (f32[64,128]{1,0:T(8,128)S(1)}, f32[64,128]{1,0:T(8,128)S(1)}, u32[]{:S(2)}, u32[]{:S(2)}) collective-permute-start(f32[64,128]{1,0:T(8,128)S(1)} %get-tuple-element.5), channel_id=1, source_target_pairs={{0,2},{1,3},{2,0},{3,1},{4,6},{5,7},{6,4},{7,5},{8,10},{9,11},{10,... | collective-permute-start | bytes 98312 | tf_op jit(solution)/shard_map/ppermute | solution.py:13
  18.5 3.3 %collective-permute-start.5 = (f32[64,128]{1,0:T(8,128)S(1)}, f32[64,128]{1,0:T(8,128)S(1)}, u32[]{:S(2)}, u32[]{:S(2)}) collective-permute-start(f32[64,128]{1,0:T(8,128)S(1)} %get-tuple-element.6), channel_id=1, source_target_pairs={{0,3},{1,2},{2,1},{3,0},{4,7},{5,6},{6,5},{7,4},{8,11},{9,10},{10,... | collective-permute-start | bytes 98312 | tf_op jit(solution)/shard_map/ppermute | solution.py:13
  18.9 7.7 %collective-permute-start.8 = (bf16[32,2048]{1,0:T(8,128)(2,1)S(1)}, bf16[32,2048]{1,0:T(8,128)(2,1)S(1)}, u32[]{:S(2)}, u32[]{:S(2)}) collective-permute-start(bf16[32,2048]{1,0:T(8,128)(2,1)S(1)} %copy-done.3), channel_id=1, source_target_pairs={{0,12},{4,8},{8,4},{12,0},{1,13},{5,9},{9,5},{13,1},{2,14},{6,10},... | collective-permute-start | bytes 393224 | tf_op jit(solution)/shard_map/ppermute | solution.py:13
  23.1 9.4 %copy-start.4 = (bf16[4,2048]{1,0:T(4,128)(2,1)}, bf16[4,2048]{1,0:T(4,128)(2,1)S(1)}, u32[]{:S(2)}) copy-start(bf16[4,2048]{1,0:T(4,128)(2,1)S(1)} %convert_element_type.54) | copy-start | bytes 49156
  27.1 3.6 %collective-permute-start.10 = (f32[5,33]{1,0:T(8,128)S(1)}, f32[5,33]{1,0:T(8,128)S(1)}, u32[]{:S(2)}, u32[]{:S(2)}) collective-permute-start(f32[5,33]{1,0:T(8,128)S(1)} %get-tuple-element.12), channel_id=1, source_target_pairs={{0,2},{1,3},{2,0},{3,1},{4,6},{5,7},{6,4},{7,5},{8,10},{9,11},{10,... | collective-permute-start | bytes 1988 | tf_op jit(solution)/shard_map/ppermute | solution.py:13
  28.6 3.0 %collective-permute-start.11 = (f32[5,33]{1,0:T(8,128)S(1)}, f32[5,33]{1,0:T(8,128)S(1)}, u32[]{:S(2)}, u32[]{:S(2)}) collective-permute-start(f32[5,33]{1,0:T(8,128)S(1)} %get-tuple-element.13), channel_id=1, source_target_pairs={{0,3},{1,2},{2,1},{3,0},{4,7},{5,6},{6,5},{7,4},{8,11},{9,10},{10,... | collective-permute-start | bytes 1988 | tf_op jit(solution)/shard_map/ppermute | solution.py:13
  28.6 3.0 %collective-permute-start.9 = (f32[5,33]{1,0:T(8,128)S(1)}, f32[5,33]{1,0:T(8,128)S(1)}, u32[]{:S(2)}, u32[]{:S(2)}) collective-permute-start(f32[5,33]{1,0:T(8,128)S(1)} %get-tuple-element.11), channel_id=1, source_target_pairs={{0,1},{1,0},{2,3},{3,2},{4,5},{5,4},{6,7},{7,6},{8,9},{9,8},{10,11... | collective-permute-start | bytes 1988 | tf_op jit(solution)/shard_map/ppermute | solution.py:13

commit v2 on v1

v2 whole, which is shorter than its diff:
```python
import functools
import math

import jax
import jax.numpy as jnp
from jax import lax
from jax.experimental import pallas as pl
from jax.experimental.pallas import tpu as pltpu
from jax.sharding import PartitionSpec as P

epsilon = 1e-06
LANES = 128
F32, BF16 = jnp.float32, jnp.bfloat16
NT = (((1,), (1,)), ((), ()))
HBM = pl.BlockSpec(memory_space=pl.ANY)
VMEM = pl.BlockSpec(memory_space=pltpu.VMEM)
SMEM = pl.BlockSpec(memory_space=pltpu.SMEM)
PARAMS = pltpu.CompilerParams(vmem_limit_bytes=48 * 1024 * 1024)


def swap(x, axis, mask):
    size = lax.axis_size(axis)
    return lax.ppermute(x, axis, [(i, i ^ mask) for i in range(size)])


def dot(a, b, dims=(((1,), (0,)), ((), ()))):
    return lax.dot_general(a, b, dims, preferred_element_type=F32)


def row_chunks(rows):
    return [(at, min(LANES, rows - at)) for at in range(0, rows, LANES)]


def rank_kernel(acts, cots, down, up, sketch, right, acts_keep, cots_keep, down_v, up_v, sketch_v, sems):
    chunks = row_chunks(acts.shape[0])
    small = [
        pltpu.make_async_copy(src, dst, sems.at[at])
        for at, (src, dst) in enumerate(((sketch, sketch_v), (down, down_v), (up, up_v)))
    ]
    big = []
    for at, rows in chunks:
        for src, dst in ((acts, acts_keep), (cots, cots_keep)):
            cut = pl.ds(at, rows)
            big.append(pltpu.make_async_copy(src.at[cut], dst.at[cut], sems.at[3 + len(big)]))
    for copy in small + big:
        copy.start()
    small[0].wait()
    small[1].wait()
    k2 = sketch.shape[1]
    folded = [dot(sketch_v[0], down_v[...]).astype(BF16)]
    small[2].wait()
    folded.append(dot(sketch_v[1], up_v[...], NT).astype(BF16))
    for at, rows in chunks:
        for p, keep in enumerate((acts_keep, cots_keep)):
            big.pop(0).wait()
            right[p * k2 : (p + 1) * k2, at : at + rows] = dot(folded[p], keep[at : at + rows, :], NT)


def rank_side(acts, cots, down, up, sketch):
    rows, cols = acts.shape
    k2 = sketch.shape[1]
    n_copies = 3 + 2 * len(row_chunks(rows))
    return pl.pallas_call(
        rank_kernel,
        out_shape=(
            jax.ShapeDtypeStruct((2 * k2, rows), F32),
            pltpu.VMEM(acts.shape, BF16),
            pltpu.VMEM(cots.shape, BF16),
        ),
        in_specs=[HBM] * 5,
        out_specs=(VMEM, VMEM, VMEM),
        scratch_shapes=[
            pltpu.VMEM(down.shape, BF16),
            pltpu.VMEM(up.shape, BF16),
            pltpu.VMEM(sketch.shape, BF16),
            pltpu.SemaphoreType.DMA((n_copies,)),
        ],
        compiler_params=PARAMS,
        name="rank_side",
    )(acts, cots, down, up, sketch)


def sums_kernel(n_proj, seq_len, k2, *refs):
    rights, (lengths, acts, cots, width, *outs, parted) = refs[:n_proj], refs[n_proj:]
    right = sum([r[...] for r in rights[1:]], rights[0][...])
    ex_dev, rows = lengths.shape[0], acts.shape[0]
    t = lax.broadcasted_iota(jnp.int32, (k2, rows), 1)
    wide = []
    for p, keep in enumerate((cots, acts)):
        own = right[p * k2 : (p + 1) * k2]
        own = own.astype(BF16).astype(F32)
        spread = [
            jnp.where((t >= e * seq_len) & (t < e * seq_len + lengths[e]), own, 0.0) for e in range(ex_dev)
        ]
        wide.append(dot(jnp.concatenate(spread, axis=0).astype(BF16), keep[...]))
    both = [wide[p][e * k2 : (e + 1) * k2] for e in range(ex_dev) for p in range(2)]
    total = dot(jnp.concatenate(both, axis=0).astype(BF16), width[...])
    k_own = width.shape[1] // n_proj
    for s in range(n_proj):
        parted[s] = total[:, s * k_own : (s + 1) * k_own]
    me = lax.axis_index("proj")
    for m in range(n_proj):
        outs[m][...] = parted[me ^ m]


def token_sums(rights, lengths, acts, cots, width, seq_len, k2):
    n_proj = len(rights)
    ex_dev = lengths.shape[0]
    shape = (ex_dev * 2 * k2, width.shape[1] // n_proj)
    return pl.pallas_call(
        functools.partial(sums_kernel, n_proj, seq_len, k2),
        out_shape=[jax.ShapeDtypeStruct(shape, F32)] * n_proj,
        in_specs=[VMEM] * n_proj + [SMEM] + [VMEM] * 3,
        out_specs=[VMEM] * n_proj,
        scratch_shapes=[pltpu.VMEM((n_proj,) + shape, F32)],
        compiler_params=PARAMS,
        name="token_sums",
    )(*rights, lengths, acts, cots, width)


def dots_kernel(n_proj, r, *refs):
    pieces, lengths, blocks = refs[:n_proj], refs[n_proj], refs[n_proj + 1 : -4]
    train, note, turned, lined = refs[-4:]
    ex_dev = lengths.shape[0]
    k_own = pieces[0].shape[1]
    low = LANES // r
    high = k_own // low
    total = sum([piece[...] for piece in pieces[1:]], pieces[0][...])
    scaled = [total[e * r : (e + 1) * r] / lengths[e].astype(F32) for e in range(ex_dev)]
    turned[:, : ex_dev * r] = jnp.concatenate(scaled, axis=0).T
    lane = lax.broadcasted_iota(jnp.int32, (high, LANES), 1)
    lines = [jnp.zeros((high, LANES), F32)] * ex_dev
    for lo in range(low):
        got = turned[pl.ds(lo, high, stride=low), :]
        for e in range(ex_dev):
            moved = got if lo == e else pltpu.roll(got, (lo - e) * r % LANES, 1)
            lines[e] = jnp.where((lane >= lo * r) & (lane < (lo + 1) * r), moved, lines[e])
    for e in range(ex_dev):
        lined[pl.ds(e, high, stride=ex_dev), :] = lines[e]
    squares = jnp.zeros((ex_dev, LANES), F32)
    for hi in range(high):
        line = lined[hi * ex_dev : (hi + 1) * ex_dev, :].astype(BF16)
        train[:, hi * LANES : (hi + 1) * LANES] = line
        squares += line.astype(F32) * line.astype(F32)
    own = train[...]
    note[...] = jnp.zeros_like(note)
    at, rows, group = 0, 0, []
    for block in blocks:
        for begin in range(0, block.shape[0], LANES):
            size = min(LANES, block.shape[0] - begin)
            group.append(block[begin : begin + size, :])
            rows += size
            if rows == LANES:
                values = jnp.concatenate(group, axis=0)
                note[:ex_dev, at : at + LANES] = dot(own, values, NT)
                square = jnp.zeros((LANES, LANES), F32)
                for c in range(0, values.shape[1], LANES):
                    piece = values[:, c : c + LANES].astype(F32)
                    square += piece * piece
                note[ex_dev : ex_dev + 1, at : at + LANES] = jnp.sum(square.T, axis=0, keepdims=True)
                at, rows, group = at + LANES, 0, []
    note[:ex_dev, at : at + LANES] = jnp.broadcast_to(jnp.sum(squares, axis=1, keepdims=True), (ex_dev, LANES))


def partial_dots(pieces, lengths, blocks, r):
    n_proj, ex_dev = len(pieces), lengths.shape[0]
    k_own = pieces[0].shape[1]
    n_val = sum(block.shape[0] for block in blocks)
    high = k_own * r // LANES
    return pl.pallas_call(
        functools.partial(dots_kernel, n_proj, r),
        out_shape=(
            jax.ShapeDtypeStruct((ex_dev, k_own * r), BF16),
            jax.ShapeDtypeStruct((2 * ex_dev, n_val + LANES), F32),
        ),
        in_specs=[VMEM] * n_proj + [SMEM] + [VMEM] * len(blocks),
        out_specs=(VMEM, VMEM),
        scratch_shapes=[pltpu.VMEM((k_own, LANES), F32), pltpu.VMEM((high * ex_dev, LANES), F32)],
        compiler_params=PARAMS,
        name="partial_dots",
    )(*pieces, lengths, *blocks)


def scores_kernel(n_proj, ex_dev, scale, by_mask, *refs):
    notes, out = refs[:n_proj], refs[n_proj]
    total = sum([note[...] for note in notes[1:]], notes[0][...])
    n_val = total.shape[1] - LANES
    share = out.shape[1]
    train_sq = total[:ex_dev, n_val : n_val + 1]
    val_sq = total[ex_dev : ex_dev + 1, :n_val]
    every = scale * total[:ex_dev, :n_val] * lax.rsqrt(train_sq + epsilon) * lax.rsqrt(val_sq + epsilon)
    at = lax.axis_index("proj")
    if by_mask:
        at = at ^ lax.axis_index("ex")
    whole = jnp.concatenate([every, every], axis=0)
    out[...] = pltpu.roll(whole, (n_val - at * share) % n_val, 1)[:ex_dev, :share]


def final_scores(notes, ex_dev, share, scale, by_mask):
    return pl.pallas_call(
        functools.partial(scores_kernel, len(notes), ex_dev, scale, by_mask),
        out_shape=jax.ShapeDtypeStruct((ex_dev, share), F32),
        in_specs=[VMEM] * len(notes),
        out_specs=VMEM,
        compiler_params=PARAMS,
        name="final_scores",
    )(*notes)


def shards(
    inputs,
    cotangents,
    lengths,
    adapter_down_matrix,
    adapter_up_matrix,
    width_side_sketch,
    rank_side_sketch,
    heldout_gradient_rows,
):
    ex_dev, seq_len, model_cols = inputs.shape
    rows = ex_dev * seq_len
    k1, k2 = width_side_sketch.shape[1], rank_side_sketch.shape[2]
    n_proj, n_ex = lax.axis_size("proj"), lax.axis_size("ex")
    acts = inputs.reshape(rows, model_cols)
    cots = cotangents.reshape(rows, model_cols)

    by_mask = n_ex == n_proj
    if by_mask:
        blocks = [heldout_gradient_rows] + [swap(heldout_gradient_rows, "ex", m) for m in range(1, n_ex)]
    else:
        blocks = [lax.all_gather(heldout_gradient_rows, "ex", axis=0, tiled=True)]

    right, acts, cots = rank_side(
        acts, cots, adapter_down_matrix, adapter_up_matrix, rank_side_sketch.transpose(0, 2, 1)
    )
    rights = [right] + [swap(right, "proj", m) for m in range(1, n_proj)]
    pieces = token_sums(rights, lengths, acts, cots, width_side_sketch, seq_len, k2)
    pieces = [pieces[0]] + [swap(pieces[m], "proj", m) for m in range(1, n_proj)]
    train_proj, note = partial_dots(pieces, lengths, blocks, 2 * k2)
    notes = [note] + [swap(note, "proj", m) for m in range(1, n_proj)]
    share = (note.shape[1] - LANES) // n_proj
    scores = final_scores(notes, ex_dev, share, math.sqrt(k1 * 2 * k2), by_mask)
    return (train_proj, scores)


def solution(mesh):
    in_specs = (
        P(("grp", "ex"), None, "proj"),
        P(("grp", "ex"), None, "proj"),
        P(("grp", "ex")),
        P(None, "proj"),
        P("proj", None),
        P("proj", None),
        P(),
        P(("grp", "ex"), "proj"),
    )
    out_specs = (P(("grp", "ex"), "proj"), P(("grp", "ex"), "proj"))
    return jax.shard_map(shards, mesh=mesh, in_specs=in_specs, out_specs=out_specs, check_vma=False)
```

time: 32.7 us -> 32.2 us (0.985)
  Pallas kernels: 0 us -> 7.59 us
  matrix products: 7.03 us -> 0 us
  other arithmetic: 4.59 us -> 0 us
  local copies, waits for them, and re-layouts: 0.63 us -> 4.01 us
  waiting for transfers between devices: 6.32 us -> 7.83 us
  starting transfers between devices: 13.1 us -> 11.8 us
    pallas_call x0 -> x4, Pallas kernels: none -> 7.59 us  [the longest x1 4.01 us: rank_side(): pl.pallas_call(rank_kernel, out_shape=(jax.ShapeDtypeStruct((2 * k2, rows...]
    dot_general x8 -> x0, matrix products: 7.03 us -> none  [the longest x2 3.69 us: shards(): jnp.dot(wide.astype(bf16), width_side_sketch, preferred_element_type=f32)]
    unnamed x14, local copies, waits for them, and re-layouts: 0.06 us -> 4.01 us
    ppermute x12, waiting for transfers between devices: 6.32 us -> 7.83 us  [swap(): return lax.ppermute(x, axis, [(i, i ^ mask) for i in range(size)])]
    reduce_sum x5 -> x0, other arithmetic: 1.42 us -> none  [the longest x1 0.84 us: shards(): train_sq = jnp.sum(train_f32 * train_f32, axis=1, keepdims=True)]
    ppermute x12, starting transfers between devices: 13.1 us -> 11.8 us  [swap(): return lax.ppermute(x, axis, [(i, i ^ mask) for i in range(size)])]
    mul x4 -> x0, other arithmetic: 0.85 us -> none  [the longest x3 0.85 us: shards(): math.sqrt(pdim) * total[:ex_dev, :share]]
    select_n x1 -> x0, other arithmetic: 0.82 us -> none  [shards(): jnp.where(live[None, :, None, :], right.reshape(2, 1, k2, row_count), jnp...]
  transfers between devices with their start and end apart: 12 -> 12, of which waited for: 5 -> 6; matrix products, arithmetic and copies ran while one was open for 25% -> 0% of each run, Pallas kernels for 0% -> 4%
where the time goes in v2:
time: 32.2 us; the launch traced here: 31.9 us
  starting transfers between devices  11.8 us (37%)
  waiting for transfers between devices  7.83 us (24%)
  Pallas kernels  7.59 us (24%)
  local copies, waits for them, and re-layouts  4.01 us (12%)
  between operations  0.69 us (2%)
    ppermute x12, starting transfers between devices, swap(): return lax.ppermute(x, axis, [(i, i ^ mask) for i in range(size)])  11.8 us
    ppermute x12, waiting for transfers between devices, swap(): return lax.ppermute(x, axis, [(i, i ^ mask) for i in range(size)])  7.83 us
    pallas_call x1, Pallas kernels, rank_side(): pl.pallas_call(rank_kernel, out_shape=(jax.ShapeDtypeStruct((2 * k2, rows...  4.01 us
    unnamed x14, local copies, waits for them, and re-layouts  4.01 us
    pallas_call x1, Pallas kernels, partial_dots(): pl.pallas_call(functools.partial(dots_kernel, n_proj, r), out_shape=(jax....  1.44 us
    pallas_call x1, Pallas kernels, token_sums(): pl.pallas_call(functools.partial(sums_kernel, n_proj, seq_len, k2), out_s...  1.41 us
    pallas_call x1, Pallas kernels, final_scores(): pl.pallas_call(functools.partial(scores_kernel, len(notes), ex_dev, scale...  0.73 us
  transfers between devices with their start and end apart: 12, of which 6 were waited for; matrix products, arithmetic and copies ran while one was open for 0% of the time, Pallas kernels for 4%

profile of v2, /device:TPU:0, one launch (start us, length us, event | category | flops | bytes accessed | tf_op | source)
XLA Modules:
  0.0 31.9 jit_solution(7299172114368387925)
XLA Ops:
  0.6 1.4 %copy-done = bf16[4,144,1280]{2,1,0:T(8,128)(2,1)S(1)} copy-done((bf16[4,144,1280]{2,1,0:T(8,128)(2,1)S(1)}, bf16[4,144,1280]{2,1,0:T(8,128)(2,1)}, u32[]{:S(2)}) %copy-start) | copy-done | bytes 1474584
  2.0 1.0 %copy-done.2 = bf16[128,1280]{1,0:T(8,128)(2,1)S(1)} copy-done((bf16[128,1280]{1,0:T(8,128)(2,1)S(1)}, bf16[128,1280]{1,0:T(8,128)(2,1)}, u32[]{:S(2)}) %copy-start.2) | copy-done | bytes 327704
  3.0 1.0 %copy-done.3 = bf16[1280,128]{1,0:T(8,128)(2,1)S(1)} copy-done((bf16[1280,128]{1,0:T(8,128)(2,1)S(1)}, bf16[1280,128]{1,0:T(8,128)(2,1)}, u32[]{:S(2)}) %copy-start.3) | copy-done | bytes 327704
  4.0 0.7 %copy-done.5 = bf16[2,128,8]{1,2,0:T(8,128)(2,1)S(1)} copy-done((bf16[2,128,8]{1,2,0:T(8,128)(2,1)S(1)}, bf16[2,128,8]{1,2,0:T(8,128)(2,1)}, u32[]{:S(2)}) %copy-start.5) | copy-done | bytes 4120
  4.6 4.0 %rank_side.1 = (f32[16,576]{1,0:T(8,128)S(1)}, bf16[576,1280]{1,0:T(8,128)(2,1)S(1)}, bf16[576,1280]{1,0:T(8,128)(2,1)S(1)}) custom-call(bf16[576,1280]{1,0:T(8,128)(2,1)S(1)} %bitcast.3, bf16[576,1280]{1,0:T(8,128)(2,1)} %bitcast.5, bf16[128,1280]{1,0:T(8,128)(2,1)S(1)} %copy-done.2, bf16[1280,128]{1,0:T(8,128)(2,1)S(1)} %copy-done.3, ...), custom_call_target="tpu_custom_call" | custom-call | tf_op jit(solution)/shard_map/rank_side/pallas_call | solution.py:63
  8.7 0.5 %collective-permute-start = (f32[16,576]{1,0:T(8,128)S(1)}, f32[16,576]{1,0:T(8,128)S(1)}, u32[]{:S(2)}, u32[]{:S(2)}) collective-permute-start(f32[16,576]{1,0:T(8,128)S(1)} %get-tuple-element.11.refs_0_), channel_id=1, source_target_pairs={{0,1},{1,0},{2,3},{3,2},{4,5},{5,4},{6,7},{7,6},{8,9},{9,8},{10,11... | collective-permute-start | bytes 110600 | tf_op jit(solution)/shard_map/ppermute | solution.py:23
  9.2 2.7 %collective-permute-start.6 = (bf16[32,2048]{1,0:T(8,128)(2,1)S(1)}, bf16[32,2048]{1,0:T(8,128)(2,1)S(1)}, u32[]{:S(2)}, u32[]{:S(2)}) collective-permute-start(bf16[32,2048]{1,0:T(8,128)(2,1)S(1)} %copy-done.4), channel_id=1, source_target_pairs={{0,4},{4,0},{8,12},{12,8},{1,5},{5,1},{9,13},{13,9},{2,6},{6,2},{1... | collective-permute-start | bytes 393224 | tf_op jit(solution)/shard_map/ppermute | solution.py:23
  11.8 2.6 %collective-permute-start.7 = (bf16[32,2048]{1,0:T(8,128)(2,1)S(1)}, bf16[32,2048]{1,0:T(8,128)(2,1)S(1)}, u32[]{:S(2)}, u32[]{:S(2)}) collective-permute-start(bf16[32,2048]{1,0:T(8,128)(2,1)S(1)} %copy-done.4), channel_id=1, source_target_pairs={{0,8},{4,12},{8,0},{12,4},{1,9},{5,13},{9,1},{13,5},{2,10},{6,14},... | collective-permute-start | bytes 393224 | tf_op jit(solution)/shard_map/ppermute | solution.py:23
  14.4 1.7 %collective-permute-start.1 = (f32[16,576]{1,0:T(8,128)S(1)}, f32[16,576]{1,0:T(8,128)S(1)}, u32[]{:S(2)}, u32[]{:S(2)}) collective-permute-start(f32[16,576]{1,0:T(8,128)S(1)} %get-tuple-element.11.refs_0_), channel_id=1, source_target_pairs={{0,2},{1,3},{2,0},{3,1},{4,6},{5,7},{6,4},{7,5},{8,10},{9,11},{10,... | collective-permute-start | bytes 110600 | tf_op jit(solution)/shard_map/ppermute | solution.py:23
  16.2 2.3 %collective-permute-done.1.refs_2_ = f32[16,576]{1,0:T(8,128)S(1)} collective-permute-done((f32[16,576]{1,0:T(8,128)S(1)}, f32[16,576]{1,0:T(8,128)S(1)}, u32[]{:S(2)}, u32[]{:S(2)}) %collective-permute-start.1) | collective-permute-done | bytes 36896 | tf_op jit(solution)/shard_map/ppermute | solution.py:23
  18.4 1.1 %collective-permute-done.2.refs_3_ = f32[16,576]{1,0:T(8,128)S(1)} collective-permute-done((f32[16,576]{1,0:T(8,128)S(1)}, f32[16,576]{1,0:T(8,128)S(1)}, u32[]{:S(2)}, u32[]{:S(2)}) %collective-permute-start.2) | collective-permute-done | bytes 36896 | tf_op jit(solution)/shard_map/ppermute | solution.py:23
  19.6 1.4 %token_sums.1 = (f32[64,128]{1,0:T(8,128)S(1)}, f32[64,128]{1,0:T(8,128)S(1)}, f32[64,128]{1,0:T(8,128)S(1)}, f32[64,128]{1,0:T(8,128)S(1)}) custom-call(f32[16,576]{1,0:T(8,128)S(1)} %get-tuple-element.11.refs_0_, f32[16,576]{1,0:T(8,128)S(1)} %collective-permute-done.refs_1_, f32[16,576]{1,0:T(8,128)S(1)} %collective-permute-done.1.refs_2_, ...), custom_call_target="tpu_custom_call" | custom-call | tf_op jit(solution)/shard_map/token_sums/pallas_call | solution.py:110
  21.0 0.1 collective-permute-start.3
  21.1 1.3 %collective-permute-start.4 = (f32[64,128]{1,0:T(8,128)S(1)}, f32[64,128]{1,0:T(8,128)S(1)}, u32[]{:S(2)}, u32[]{:S(2)}) collective-permute-start(f32[64,128]{1,0:T(8,128)S(1)} %get-tuple-element.16), channel_id=1, source_target_pairs={{0,2},{1,3},{2,0},{3,1},{4,6},{5,7},{6,4},{7,5},{8,10},{9,11},{10,... | collective-permute-start | bytes 98312 | tf_op jit(solution)/shard_map/ppermute | solution.py:23
  22.4 0.8 %collective-permute-start.5 = (f32[64,128]{1,0:T(8,128)S(1)}, f32[64,128]{1,0:T(8,128)S(1)}, u32[]{:S(2)}, u32[]{:S(2)}) collective-permute-start(f32[64,128]{1,0:T(8,128)S(1)} %get-tuple-element.17), channel_id=1, source_target_pairs={{0,3},{1,2},{2,1},{3,0},{4,7},{5,6},{6,5},{7,4},{8,11},{9,10},{10,... | collective-permute-start | bytes 98312 | tf_op jit(solution)/shard_map/ppermute | solution.py:23
  23.2 1.9 %collective-permute-done.4.refs_2_ = f32[64,128]{1,0:T(8,128)S(1)} collective-permute-done((f32[64,128]{1,0:T(8,128)S(1)}, f32[64,128]{1,0:T(8,128)S(1)}, u32[]{:S(2)}, u32[]{:S(2)}) %collective-permute-start.4) | collective-permute-done | bytes 32800 | tf_op jit(solution)/shard_map/ppermute | solution.py:23
  25.1 0.8 %collective-permute-done.5.refs_3_ = f32[64,128]{1,0:T(8,128)S(1)} collective-permute-done((f32[64,128]{1,0:T(8,128)S(1)}, f32[64,128]{1,0:T(8,128)S(1)}, u32[]{:S(2)}, u32[]{:S(2)}) %collective-permute-start.5) | collective-permute-done | bytes 32800 | tf_op jit(solution)/shard_map/ppermute | solution.py:23
  25.8 1.4 %partial_dots.1 = (bf16[4,2048]{1,0:T(4,128)(2,1)}, f32[8,256]{1,0:T(8,128)S(1)}) custom-call(f32[64,128]{1,0:T(8,128)S(1)} %get-tuple-element.14.refs_0_, f32[64,128]{1,0:T(8,128)S(1)} %collective-permute-done.3.refs_1_, f32[64,128]{1,0:T(8,128)S(1)} %collective-permute-done.4.refs_2_, f32[64,128]{1,0:T(8,128)S(1)} %collective-permute-done.5.refs_3_, ...), custom_call_target="tpu_custom_call" | custom-call | tf_op jit(solution)/shard_map/partial_dots/pallas_call | solution.py:170
  27.3 0.8 %collective-permute-start.10 = (f32[8,256]{1,0:T(8,128)S(1)}, f32[8,256]{1,0:T(8,128)S(1)}, u32[]{:S(2)}, u32[]{:S(2)}) collective-permute-start(f32[8,256]{1,0:T(8,128)S(1)} %get-tuple-element.19.refs_0_), channel_id=1, source_target_pairs={{0,2},{1,3},{2,0},{3,1},{4,6},{5,7},{6,4},{7,5},{8,10},{9,11},{10,... | collective-permute-start | bytes 24584 | tf_op jit(solution)/shard_map/ppermute | solution.py:23
  28.1 0.7 %collective-permute-start.11 = (f32[8,256]{1,0:T(8,128)S(1)}, f32[8,256]{1,0:T(8,128)S(1)}, u32[]{:S(2)}, u32[]{:S(2)}) collective-permute-start(f32[8,256]{1,0:T(8,128)S(1)} %get-tuple-element.19.refs_0_), channel_id=1, source_target_pairs={{0,3},{1,2},{2,1},{3,0},{4,7},{5,6},{6,5},{7,4},{8,11},{9,10},{10,... | collective-permute-start | bytes 24584 | tf_op jit(solution)/shard_map/ppermute | solution.py:23
  28.8 0.7 %collective-permute-start.9 = (f32[8,256]{1,0:T(8,128)S(1)}, f32[8,256]{1,0:T(8,128)S(1)}, u32[]{:S(2)}, u32[]{:S(2)}) collective-permute-start(f32[8,256]{1,0:T(8,128)S(1)} %get-tuple-element.19.refs_0_), channel_id=1, source_target_pairs={{0,1},{1,0},{2,3},{3,2},{4,5},{5,4},{6,7},{7,6},{8,9},{9,8},{10,11... | collective-permute-start | bytes 24584 | tf_op jit(solution)/shard_map/ppermute | solution.py:23
  29.4 1.5 %collective-permute-done.10.refs_2_ = f32[8,256]{1,0:T(8,128)S(1)} collective-permute-done((f32[8,256]{1,0:T(8,128)S(1)}, f32[8,256]{1,0:T(8,128)S(1)}, u32[]{:S(2)}, u32[]{:S(2)}) %collective-permute-start.10) | collective-permute-done | bytes 8224 | tf_op jit(solution)/shard_map/ppermute | solution.py:23
  30.9 0.2 collective-permute-done.11.refs_3_
  31.2 0.7 %final_scores.1 = f32[4,32]{1,0:T(4,128)} custom-call(f32[8,256]{1,0:T(8,128)S(1)} %get-tuple-element.19.refs_0_, f32[8,256]{1,0:T(8,128)S(1)} %collective-permute-done.9.refs_1_, f32[8,256]{1,0:T(8,128)S(1)} %collective-permute-done.10.refs_2_, f32[8,256]{1,0:T(8,128)S(1)} %collective-permute-done.11.refs_3_), custom_call_target="tpu_custom_call" | custom-call | tf_op jit(solution)/shard_map/final_scores/pallas_call | solution.py:200
  (18 shorter events, 0.0 us)
Async XLA Ops:
  0.6 1.4 %copy-start = (bf16[4,144,1280]{2,1,0:T(8,128)(2,1)S(1)}, bf16[4,144,1280]{2,1,0:T(8,128)(2,1)}, u32[]{:S(2)}) copy-start(bf16[4,144,1280]{2,1,0:T(8,128)(2,1)} %param.8) | copy-start | bytes 4423684
  2.0 1.0 %copy-start.2 = (bf16[128,1280]{1,0:T(8,128)(2,1)S(1)}, bf16[128,1280]{1,0:T(8,128)(2,1)}, u32[]{:S(2)}) copy-start(bf16[128,1280]{1,0:T(8,128)(2,1)} %down.1) | copy-start | bytes 983044
  3.0 1.0 %copy-start.3 = (bf16[1280,128]{1,0:T(8,128)(2,1)S(1)}, bf16[1280,128]{1,0:T(8,128)(2,1)}, u32[]{:S(2)}) copy-start(bf16[1280,128]{1,0:T(8,128)(2,1)} %up.1) | copy-start | bytes 983044
  4.0 0.7 %copy-start.5 = (bf16[2,128,8]{1,2,0:T(8,128)(2,1)S(1)}, bf16[2,128,8]{1,2,0:T(8,128)(2,1)}, u32[]{:S(2)}) copy-start(bf16[2,128,8]{1,2,0:T(8,128)(2,1)} %param.14) | copy-start | bytes 12292
  4.6 4.5 %copy-start.4 = (bf16[32,2048]{1,0:T(8,128)(2,1)S(1)}, bf16[32,2048]{1,0:T(8,128)(2,1)}, u32[]{:S(2)}) copy-start(bf16[32,2048]{1,0:T(8,128)(2,1)} %refs_5_.1) | copy-start | bytes 393220
  4.6 14.9 %copy-start.1 = (bf16[1280,512]{1,0:T(8,128)(2,1)S(1)}, bf16[1280,512]{1,0:T(8,128)(2,1)}, u32[]{:S(2)}) copy-start(bf16[1280,512]{1,0:T(8,128)(2,1)} %refs_7_.1) | copy-start | bytes 3932164
  4.6 14.9 %copy-start.6 = (s32[4]{0:T(128)S(1)}, s32[4]{0:T(128)}, u32[]{:S(2)}) copy-start(s32[4]{0:T(128)} %refs_4_.3) | copy-start | bytes 52
  8.7 7.5 %collective-permute-start = (f32[16,576]{1,0:T(8,128)S(1)}, f32[16,576]{1,0:T(8,128)S(1)}, u32[]{:S(2)}, u32[]{:S(2)}) collective-permute-start(f32[16,576]{1,0:T(8,128)S(1)} %get-tuple-element.11.refs_0_), channel_id=1, source_target_pairs={{0,1},{1,0},{2,3},{3,2},{4,5},{5,4},{6,7},{7,6},{8,9},{9,8},{10,11... | collective-permute-start | bytes 110600 | tf_op jit(solution)/shard_map/ppermute | solution.py:23
  9.2 16.7 %collective-permute-start.6 = (bf16[32,2048]{1,0:T(8,128)(2,1)S(1)}, bf16[32,2048]{1,0:T(8,128)(2,1)S(1)}, u32[]{:S(2)}, u32[]{:S(2)}) collective-permute-start(bf16[32,2048]{1,0:T(8,128)(2,1)S(1)} %copy-done.4), channel_id=1, source_target_pairs={{0,4},{4,0},{8,12},{12,8},{1,5},{5,1},{9,13},{13,9},{2,6},{6,2},{1... | collective-permute-start | bytes 393224 | tf_op jit(solution)/shard_map/ppermute | solution.py:23
  11.8 14.0 %collective-permute-start.7 = (bf16[32,2048]{1,0:T(8,128)(2,1)S(1)}, bf16[32,2048]{1,0:T(8,128)(2,1)S(1)}, u32[]{:S(2)}, u32[]{:S(2)}) collective-permute-start(bf16[32,2048]{1,0:T(8,128)(2,1)S(1)} %copy-done.4), channel_id=1, source_target_pairs={{0,8},{4,12},{8,0},{12,4},{1,9},{5,13},{9,1},{13,5},{2,10},{6,14},... | collective-permute-start | bytes 393224 | tf_op jit(solution)/shard_map/ppermute | solution.py:23
  14.4 11.4 %collective-permute-start.8 = (bf16[32,2048]{1,0:T(8,128)(2,1)S(1)}, bf16[32,2048]{1,0:T(8,128)(2,1)S(1)}, u32[]{:S(2)}, u32[]{:S(2)}) collective-permute-start(bf16[32,2048]{1,0:T(8,128)(2,1)S(1)} %copy-done.4), channel_id=1, source_target_pairs={{0,12},{4,8},{8,4},{12,0},{1,13},{5,9},{9,5},{13,1},{2,14},{6,10},... | collective-permute-start | bytes 393224 | tf_op jit(solution)/shard_map/ppermute | solution.py:23
  14.4 4.0 %collective-permute-start.1 = (f32[16,576]{1,0:T(8,128)S(1)}, f32[16,576]{1,0:T(8,128)S(1)}, u32[]{:S(2)}, u32[]{:S(2)}) collective-permute-start(f32[16,576]{1,0:T(8,128)S(1)} %get-tuple-element.11.refs_0_), channel_id=1, source_target_pairs={{0,2},{1,3},{2,0},{3,1},{4,6},{5,7},{6,4},{7,5},{8,10},{9,11},{10,... | collective-permute-start | bytes 110600 | tf_op jit(solution)/shard_map/ppermute | solution.py:23
  16.1 3.4 %collective-permute-start.2 = (f32[16,576]{1,0:T(8,128)S(1)}, f32[16,576]{1,0:T(8,128)S(1)}, u32[]{:S(2)}, u32[]{:S(2)}) collective-permute-start(f32[16,576]{1,0:T(8,128)S(1)} %get-tuple-element.11.refs_0_), channel_id=1, source_target_pairs={{0,3},{1,2},{2,1},{3,0},{4,7},{5,6},{6,5},{7,4},{8,11},{9,10},{10,... | collective-permute-start | bytes 110600 | tf_op jit(solution)/shard_map/ppermute | solution.py:23
  21.0 1.4 %collective-permute-start.3 = (f32[64,128]{1,0:T(8,128)S(1)}, f32[64,128]{1,0:T(8,128)S(1)}, u32[]{:S(2)}, u32[]{:S(2)}) collective-permute-start(f32[64,128]{1,0:T(8,128)S(1)} %get-tuple-element.15), channel_id=1, source_target_pairs={{0,1},{1,0},{2,3},{3,2},{4,5},{5,4},{6,7},{7,6},{8,9},{9,8},{10,11... | collective-permute-start | bytes 98312 | tf_op jit(solution)/shard_map/ppermute | solution.py:23
  21.1 4.0 %collective-permute-start.4 = (f32[64,128]{1,0:T(8,128)S(1)}, f32[64,128]{1,0:T(8,128)S(1)}, u32[]{:S(2)}, u32[]{:S(2)}) collective-permute-start(f32[64,128]{1,0:T(8,128)S(1)} %get-tuple-element.16), channel_id=1, source_target_pairs={{0,2},{1,3},{2,0},{3,1},{4,6},{5,7},{6,4},{7,5},{8,10},{9,11},{10,... | collective-permute-start | bytes 98312 | tf_op jit(solution)/shard_map/ppermute | solution.py:23
  22.4 3.5 %collective-permute-start.5 = (f32[64,128]{1,0:T(8,128)S(1)}, f32[64,128]{1,0:T(8,128)S(1)}, u32[]{:S(2)}, u32[]{:S(2)}) collective-permute-start(f32[64,128]{1,0:T(8,128)S(1)} %get-tuple-element.17), channel_id=1, source_target_pairs={{0,3},{1,2},{2,1},{3,0},{4,7},{5,6},{6,5},{7,4},{8,11},{9,10},{10,... | collective-permute-start | bytes 98312 | tf_op jit(solution)/shard_map/ppermute | solution.py:23
  27.3 3.7 %collective-permute-start.10 = (f32[8,256]{1,0:T(8,128)S(1)}, f32[8,256]{1,0:T(8,128)S(1)}, u32[]{:S(2)}, u32[]{:S(2)}) collective-permute-start(f32[8,256]{1,0:T(8,128)S(1)} %get-tuple-element.19.refs_0_), channel_id=1, source_target_pairs={{0,2},{1,3},{2,0},{3,1},{4,6},{5,7},{6,4},{7,5},{8,10},{9,11},{10,... | collective-permute-start | bytes 24584 | tf_op jit(solution)/shard_map/ppermute | solution.py:23
  28.1 3.1 %collective-permute-start.11 = (f32[8,256]{1,0:T(8,128)S(1)}, f32[8,256]{1,0:T(8,128)S(1)}, u32[]{:S(2)}, u32[]{:S(2)}) collective-permute-start(f32[8,256]{1,0:T(8,128)S(1)} %get-tuple-element.19.refs_0_), channel_id=1, source_target_pairs={{0,3},{1,2},{2,1},{3,0},{4,7},{5,6},{6,5},{7,4},{8,11},{9,10},{10,... | collective-permute-start | bytes 24584 | tf_op jit(solution)/shard_map/ppermute | solution.py:23
  28.8 2.4 %collective-permute-start.9 = (f32[8,256]{1,0:T(8,128)S(1)}, f32[8,256]{1,0:T(8,128)S(1)}, u32[]{:S(2)}, u32[]{:S(2)}) collective-permute-start(f32[8,256]{1,0:T(8,128)S(1)} %get-tuple-element.19.refs_0_), channel_id=1, source_target_pairs={{0,1},{1,0},{2,3},{3,2},{4,5},{5,4},{6,7},{7,6},{8,9},{9,8},{10,11... | collective-permute-start | bytes 24584 | tf_op jit(solution)/shard_map/ppermute | solution.py:23

commit v3 on v2

--- a/solution.py
+++ b/solution.py
@@ -12,7 +12,7 @@
 LANES = 128
 F32, BF16 = jnp.float32, jnp.bfloat16
 NT = (((1,), (1,)), ((), ()))
-HBM = pl.BlockSpec(memory_space=pl.ANY)
+HBM = pl.BlockSpec(memory_space=pltpu.HBM)
 VMEM = pl.BlockSpec(memory_space=pltpu.VMEM)
 SMEM = pl.BlockSpec(memory_space=pltpu.SMEM)
 PARAMS = pltpu.CompilerParams(vmem_limit_bytes=48 * 1024 * 1024)
@@ -27,8 +27,11 @@
     return lax.dot_general(a, b, dims, preferred_element_type=F32)
 
 
+STEP = 2 * LANES
+
+
 def row_chunks(rows):
-    return [(at, min(LANES, rows - at)) for at in range(0, rows, LANES)]
+    return [(at, min(STEP, rows - at)) for at in range(0, rows, STEP)]
 
 
 def rank_kernel(acts, cots, down, up, sketch, right, acts_keep, cots_keep, down_v, up_v, sketch_v, sems):
@@ -47,19 +50,30 @@
     small[0].wait()
     small[1].wait()
     k2 = sketch.shape[1]
-    folded = [dot(sketch_v[0], down_v[...]).astype(BF16)]
+    folded = [dot(sketch_v[0], down_v[...])]
     small[2].wait()
-    folded.append(dot(sketch_v[1], up_v[...], NT).astype(BF16))
+    folded.append(dot(sketch_v[1], up_v[...], NT))
+    lanes = acts.shape[1]
+    pad = jnp.zeros((LANES - k2, lanes), F32)
+    weights = [
+        jnp.concatenate([folded[0], pad], axis=0).T.astype(BF16),
+        jnp.concatenate([pad[:k2], folded[1], pad[k2:]], axis=0).T.astype(BF16),
+    ]
     for at, rows in chunks:
-        for p, keep in enumerate((acts_keep, cots_keep)):
-            big.pop(0).wait()
-            right[p * k2 : (p + 1) * k2, at : at + rows] = dot(folded[p], keep[at : at + rows, :], NT)
+        big.pop(0).wait()
+        big.pop(0).wait()
+        cut = pl.ds(at, rows)
+        got = dot(acts_keep[cut, :], weights[0]) + dot(cots_keep[cut, :], weights[1])
+        for b in range(0, rows, LANES):
+            size = min(LANES, rows - b)
+            right[:, at + b : at + b + size] = got[b : b + size].T[: 2 * k2]
 
 
 def rank_side(acts, cots, down, up, sketch):
     rows, cols = acts.shape
     k2 = sketch.shape[1]
     n_copies = 3 + 2 * len(row_chunks(rows))
+    acts, cots, down, up, sketch = [pltpu.with_memory_space_constraint(x, pltpu.HBM) for x in (acts, cots, down, up, sketch)]
     return pl.pallas_call(
         rank_kernel,
         out_shape=(

time: 32.2 us -> 27.1 us (0.84)
  local copies, waits for them, and re-layouts: 4.01 us -> 0.01 us
  Pallas kernels: 7.59 us -> 6.67 us
    unnamed x14 -> x6, local copies, waits for them, and re-layouts: 4.01 us -> 0.01 us
    pallas_call x1, Pallas kernels: 4.01 us -> 3.09 us  [rank_side(): pl.pallas_call(rank_kernel, out_shape=(jax.ShapeDtypeStruct((2 * k2, rows...]
  transfers between devices with their start and end apart: 12 -> 12, of which waited for: 6 -> 6; matrix products, arithmetic and copies ran while one was open for 0% -> 0% of each run, Pallas kernels for 4% -> 5%
where the time goes in v3:
time: 27.1 us; the launch traced here: 27 us
  starting transfers between devices  11.8 us (44%)
  waiting for transfers between devices  7.83 us (29%)
  Pallas kernels  6.67 us (25%)
  between operations  0.7 us (3%)
    ppermute x12, starting transfers between devices, swap(): return lax.ppermute(x, axis, [(i, i ^ mask) for i in range(size)])  11.8 us
    ppermute x12, waiting for transfers between devices, swap(): return lax.ppermute(x, axis, [(i, i ^ mask) for i in range(size)])  7.83 us
    pallas_call x1, Pallas kernels, rank_side(): pl.pallas_call(rank_kernel, out_shape=(jax.ShapeDtypeStruct((2 * k2, rows...  3.09 us
    pallas_call x1, Pallas kernels, partial_dots(): pl.pallas_call(functools.partial(dots_kernel, n_proj, r), out_shape=(jax....  1.44 us
    pallas_call x1, Pallas kernels, token_sums(): pl.pallas_call(functools.partial(sums_kernel, n_proj, seq_len, k2), out_s...  1.41 us
    pallas_call x1, Pallas kernels, final_scores(): pl.pallas_call(functools.partial(scores_kernel, len(notes), ex_dev, scale...  0.73 us
  transfers between devices with their start and end apart: 12, of which 6 were waited for; matrix products, arithmetic and copies ran while one was open for 0% of the time, Pallas kernels for 5%

profile of v3, /device:TPU:0, one launch (start us, length us, event | category | flops | bytes accessed | tf_op | source)
XLA Modules:
  0.0 27.0 jit_solution(16675998797828889068)
XLA Ops:
  0.7 3.1 %rank_side.1 = (f32[16,576]{1,0:T(8,128)S(1)}, bf16[576,1280]{1,0:T(8,128)(2,1)S(1)}, bf16[576,1280]{1,0:T(8,128)(2,1)S(1)}) custom-call(bf16[576,1280]{1,0:T(8,128)(2,1)} %bitcast.3, bf16[576,1280]{1,0:T(8,128)(2,1)} %bitcast.4, bf16[128,1280]{1,0:T(8,128)(2,1)} %down.1, bf16[1280,128]{1,0:T(8,128)(2,1)} %up.1, bf16[2,8,128]{2,1,0:T(8,128)(2,1)} %bitcast.5), custom_call_target="tpu_custom_call" | custom-call | tf_op jit(solution)/shard_map/rank_side/pallas_call | solution.py:77
  3.8 0.5 %collective-permute-start = (f32[16,576]{1,0:T(8,128)S(1)}, f32[16,576]{1,0:T(8,128)S(1)}, u32[]{:S(2)}, u32[]{:S(2)}) collective-permute-start(f32[16,576]{1,0:T(8,128)S(1)} %get-tuple-element.11.refs_0_), channel_id=1, source_target_pairs={{0,1},{1,0},{2,3},{3,2},{4,5},{5,4},{6,7},{7,6},{8,9},{9,8},{10,11... | collective-permute-start | bytes 110600 | tf_op jit(solution)/shard_map/ppermute | solution.py:23
  4.3 2.7 %collective-permute-start.6 = (bf16[32,2048]{1,0:T(8,128)(2,1)S(1)}, bf16[32,2048]{1,0:T(8,128)(2,1)S(1)}, u32[]{:S(2)}, u32[]{:S(2)}) collective-permute-start(bf16[32,2048]{1,0:T(8,128)(2,1)S(1)} %copy-done.1), channel_id=1, source_target_pairs={{0,4},{4,0},{8,12},{12,8},{1,5},{5,1},{9,13},{13,9},{2,6},{6,2},{1... | collective-permute-start | bytes 393224 | tf_op jit(solution)/shard_map/ppermute | solution.py:23
  6.9 2.6 %collective-permute-start.7 = (bf16[32,2048]{1,0:T(8,128)(2,1)S(1)}, bf16[32,2048]{1,0:T(8,128)(2,1)S(1)}, u32[]{:S(2)}, u32[]{:S(2)}) collective-permute-start(bf16[32,2048]{1,0:T(8,128)(2,1)S(1)} %copy-done.1), channel_id=1, source_target_pairs={{0,8},{4,12},{8,0},{12,4},{1,9},{5,13},{9,1},{13,5},{2,10},{6,14},... | collective-permute-start | bytes 393224 | tf_op jit(solution)/shard_map/ppermute | solution.py:23
  9.5 0.0 collective-permute-start.8
  9.5 1.7 %collective-permute-start.1 = (f32[16,576]{1,0:T(8,128)S(1)}, f32[16,576]{1,0:T(8,128)S(1)}, u32[]{:S(2)}, u32[]{:S(2)}) collective-permute-start(f32[16,576]{1,0:T(8,128)S(1)} %get-tuple-element.11.refs_0_), channel_id=1, source_target_pairs={{0,2},{1,3},{2,0},{3,1},{4,6},{5,7},{6,4},{7,5},{8,10},{9,11},{10,... | collective-permute-start | bytes 110600 | tf_op jit(solution)/shard_map/ppermute | solution.py:23
  11.2 0.0 collective-permute-done.refs_1_
  11.2 0.0 collective-permute-start.2
  11.2 2.3 %collective-permute-done.1.refs_2_ = f32[16,576]{1,0:T(8,128)S(1)} collective-permute-done((f32[16,576]{1,0:T(8,128)S(1)}, f32[16,576]{1,0:T(8,128)S(1)}, u32[]{:S(2)}, u32[]{:S(2)}) %collective-permute-start.1) | collective-permute-done | bytes 36896 | tf_op jit(solution)/shard_map/ppermute | solution.py:23
  13.5 1.1 %collective-permute-done.2.refs_3_ = f32[16,576]{1,0:T(8,128)S(1)} collective-permute-done((f32[16,576]{1,0:T(8,128)S(1)}, f32[16,576]{1,0:T(8,128)S(1)}, u32[]{:S(2)}, u32[]{:S(2)}) %collective-permute-start.2) | collective-permute-done | bytes 36896 | tf_op jit(solution)/shard_map/ppermute | solution.py:23
  14.7 1.4 %token_sums.1 = (f32[64,128]{1,0:T(8,128)S(1)}, f32[64,128]{1,0:T(8,128)S(1)}, f32[64,128]{1,0:T(8,128)S(1)}, f32[64,128]{1,0:T(8,128)S(1)}) custom-call(f32[16,576]{1,0:T(8,128)S(1)} %get-tuple-element.11.refs_0_, f32[16,576]{1,0:T(8,128)S(1)} %collective-permute-done.refs_1_, f32[16,576]{1,0:T(8,128)S(1)} %collective-permute-done.1.refs_2_, ...), custom_call_target="tpu_custom_call" | custom-call | tf_op jit(solution)/shard_map/token_sums/pallas_call | solution.py:124
  16.1 0.1 collective-permute-start.3
  16.2 1.3 %collective-permute-start.4 = (f32[64,128]{1,0:T(8,128)S(1)}, f32[64,128]{1,0:T(8,128)S(1)}, u32[]{:S(2)}, u32[]{:S(2)}) collective-permute-start(f32[64,128]{1,0:T(8,128)S(1)} %get-tuple-element.16), channel_id=1, source_target_pairs={{0,2},{1,3},{2,0},{3,1},{4,6},{5,7},{6,4},{7,5},{8,10},{9,11},{10,... | collective-permute-start | bytes 98312 | tf_op jit(solution)/shard_map/ppermute | solution.py:23
  17.5 0.8 %collective-permute-start.5 = (f32[64,128]{1,0:T(8,128)S(1)}, f32[64,128]{1,0:T(8,128)S(1)}, u32[]{:S(2)}, u32[]{:S(2)}) collective-permute-start(f32[64,128]{1,0:T(8,128)S(1)} %get-tuple-element.17), channel_id=1, source_target_pairs={{0,3},{1,2},{2,1},{3,0},{4,7},{5,6},{6,5},{7,4},{8,11},{9,10},{10,... | collective-permute-start | bytes 98312 | tf_op jit(solution)/shard_map/ppermute | solution.py:23
  18.3 1.9 %collective-permute-done.4.refs_2_ = f32[64,128]{1,0:T(8,128)S(1)} collective-permute-done((f32[64,128]{1,0:T(8,128)S(1)}, f32[64,128]{1,0:T(8,128)S(1)}, u32[]{:S(2)}, u32[]{:S(2)}) %collective-permute-start.4) | collective-permute-done | bytes 32800 | tf_op jit(solution)/shard_map/ppermute | solution.py:23
  20.2 0.8 %collective-permute-done.5.refs_3_ = f32[64,128]{1,0:T(8,128)S(1)} collective-permute-done((f32[64,128]{1,0:T(8,128)S(1)}, f32[64,128]{1,0:T(8,128)S(1)}, u32[]{:S(2)}, u32[]{:S(2)}) %collective-permute-start.5) | collective-permute-done | bytes 32800 | tf_op jit(solution)/shard_map/ppermute | solution.py:23
  20.9 0.0 collective-permute-done.6.refs_6_
  20.9 1.4 %partial_dots.1 = (bf16[4,2048]{1,0:T(4,128)(2,1)}, f32[8,256]{1,0:T(8,128)S(1)}) custom-call(f32[64,128]{1,0:T(8,128)S(1)} %get-tuple-element.14.refs_0_, f32[64,128]{1,0:T(8,128)S(1)} %collective-permute-done.3.refs_1_, f32[64,128]{1,0:T(8,128)S(1)} %collective-permute-done.4.refs_2_, f32[64,128]{1,0:T(8,128)S(1)} %collective-permute-done.5.refs_3_, ...), custom_call_target="tpu_custom_call" | custom-call | tf_op jit(solution)/shard_map/partial_dots/pallas_call | solution.py:184
  22.4 0.8 %collective-permute-start.10 = (f32[8,256]{1,0:T(8,128)S(1)}, f32[8,256]{1,0:T(8,128)S(1)}, u32[]{:S(2)}, u32[]{:S(2)}) collective-permute-start(f32[8,256]{1,0:T(8,128)S(1)} %get-tuple-element.19.refs_0_), channel_id=1, source_target_pairs={{0,2},{1,3},{2,0},{3,1},{4,6},{5,7},{6,4},{7,5},{8,10},{9,11},{10,... | collective-permute-start | bytes 24584 | tf_op jit(solution)/shard_map/ppermute | solution.py:23
  23.2 0.7 %collective-permute-start.11 = (f32[8,256]{1,0:T(8,128)S(1)}, f32[8,256]{1,0:T(8,128)S(1)}, u32[]{:S(2)}, u32[]{:S(2)}) collective-permute-start(f32[8,256]{1,0:T(8,128)S(1)} %get-tuple-element.19.refs_0_), channel_id=1, source_target_pairs={{0,3},{1,2},{2,1},{3,0},{4,7},{5,6},{6,5},{7,4},{8,11},{9,10},{10,... | collective-permute-start | bytes 24584 | tf_op jit(solution)/shard_map/ppermute | solution.py:23
  23.8 0.7 %collective-permute-start.9 = (f32[8,256]{1,0:T(8,128)S(1)}, f32[8,256]{1,0:T(8,128)S(1)}, u32[]{:S(2)}, u32[]{:S(2)}) collective-permute-start(f32[8,256]{1,0:T(8,128)S(1)} %get-tuple-element.19.refs_0_), channel_id=1, source_target_pairs={{0,1},{1,0},{2,3},{3,2},{4,5},{5,4},{6,7},{7,6},{8,9},{9,8},{10,11... | collective-permute-start | bytes 24584 | tf_op jit(solution)/shard_map/ppermute | solution.py:23
  24.5 1.5 %collective-permute-done.10.refs_2_ = f32[8,256]{1,0:T(8,128)S(1)} collective-permute-done((f32[8,256]{1,0:T(8,128)S(1)}, f32[8,256]{1,0:T(8,128)S(1)}, u32[]{:S(2)}, u32[]{:S(2)}) %collective-permute-start.10) | collective-permute-done | bytes 8224 | tf_op jit(solution)/shard_map/ppermute | solution.py:23
  26.0 0.2 collective-permute-done.11.refs_3_
  26.3 0.7 %final_scores.1 = f32[4,32]{1,0:T(4,128)} custom-call(f32[8,256]{1,0:T(8,128)S(1)} %get-tuple-element.19.refs_0_, f32[8,256]{1,0:T(8,128)S(1)} %collective-permute-done.9.refs_1_, f32[8,256]{1,0:T(8,128)S(1)} %collective-permute-done.10.refs_2_, f32[8,256]{1,0:T(8,128)S(1)} %collective-permute-done.11.refs_3_), custom_call_target="tpu_custom_call" | custom-call | tf_op jit(solution)/shard_map/final_scores/pallas_call | solution.py:214
  (10 shorter events, 0.0 us)
Async XLA Ops:
  0.6 3.6 %copy-start.1 = (bf16[32,2048]{1,0:T(8,128)(2,1)S(1)}, bf16[32,2048]{1,0:T(8,128)(2,1)}, u32[]{:S(2)}) copy-start(bf16[32,2048]{1,0:T(8,128)(2,1)} %refs_5_.1) | copy-start | bytes 393220
  0.6 14.0 %copy-start = (bf16[1280,512]{1,0:T(8,128)(2,1)S(1)}, bf16[1280,512]{1,0:T(8,128)(2,1)}, u32[]{:S(2)}) copy-start(bf16[1280,512]{1,0:T(8,128)(2,1)} %refs_7_.1) | copy-start | bytes 3932164
  0.7 14.0 %copy-start.2 = (s32[4]{0:T(128)S(1)}, s32[4]{0:T(128)}, u32[]{:S(2)}) copy-start(s32[4]{0:T(128)} %refs_4_.3) | copy-start | bytes 52
  3.8 7.5 %collective-permute-start = (f32[16,576]{1,0:T(8,128)S(1)}, f32[16,576]{1,0:T(8,128)S(1)}, u32[]{:S(2)}, u32[]{:S(2)}) collective-permute-start(f32[16,576]{1,0:T(8,128)S(1)} %get-tuple-element.11.refs_0_), channel_id=1, source_target_pairs={{0,1},{1,0},{2,3},{3,2},{4,5},{5,4},{6,7},{7,6},{8,9},{9,8},{10,11... | collective-permute-start | bytes 110600 | tf_op jit(solution)/shard_map/ppermute | solution.py:23
  4.3 16.6 %collective-permute-start.6 = (bf16[32,2048]{1,0:T(8,128)(2,1)S(1)}, bf16[32,2048]{1,0:T(8,128)(2,1)S(1)}, u32[]{:S(2)}, u32[]{:S(2)}) collective-permute-start(bf16[32,2048]{1,0:T(8,128)(2,1)S(1)} %copy-done.1), channel_id=1, source_target_pairs={{0,4},{4,0},{8,12},{12,8},{1,5},{5,1},{9,13},{13,9},{2,6},{6,2},{1... | collective-permute-start | bytes 393224 | tf_op jit(solution)/shard_map/ppermute | solution.py:23
  6.9 14.0 %collective-permute-start.7 = (bf16[32,2048]{1,0:T(8,128)(2,1)S(1)}, bf16[32,2048]{1,0:T(8,128)(2,1)S(1)}, u32[]{:S(2)}, u32[]{:S(2)}) collective-permute-start(bf16[32,2048]{1,0:T(8,128)(2,1)S(1)} %copy-done.1), channel_id=1, source_target_pairs={{0,8},{4,12},{8,0},{12,4},{1,9},{5,13},{9,1},{13,5},{2,10},{6,14},... | collective-permute-start | bytes 393224 | tf_op jit(solution)/shard_map/ppermute | solution.py:23
  9.5 11.4 %collective-permute-start.8 = (bf16[32,2048]{1,0:T(8,128)(2,1)S(1)}, bf16[32,2048]{1,0:T(8,128)(2,1)S(1)}, u32[]{:S(2)}, u32[]{:S(2)}) collective-permute-start(bf16[32,2048]{1,0:T(8,128)(2,1)S(1)} %copy-done.1), channel_id=1, source_target_pairs={{0,12},{4,8},{8,4},{12,0},{1,13},{5,9},{9,5},{13,1},{2,14},{6,10},... | collective-permute-start | bytes 393224 | tf_op jit(solution)/shard_map/ppermute | solution.py:23
  9.5 4.0 %collective-permute-start.1 = (f32[16,576]{1,0:T(8,128)S(1)}, f32[16,576]{1,0:T(8,128)S(1)}, u32[]{:S(2)}, u32[]{:S(2)}) collective-permute-start(f32[16,576]{1,0:T(8,128)S(1)} %get-tuple-element.11.refs_0_), channel_id=1, source_target_pairs={{0,2},{1,3},{2,0},{3,1},{4,6},{5,7},{6,4},{7,5},{8,10},{9,11},{10,... | collective-permute-start | bytes 110600 | tf_op jit(solution)/shard_map/ppermute | solution.py:23
  11.2 3.4 %collective-permute-start.2 = (f32[16,576]{1,0:T(8,128)S(1)}, f32[16,576]{1,0:T(8,128)S(1)}, u32[]{:S(2)}, u32[]{:S(2)}) collective-permute-start(f32[16,576]{1,0:T(8,128)S(1)} %get-tuple-element.11.refs_0_), channel_id=1, source_target_pairs={{0,3},{1,2},{2,1},{3,0},{4,7},{5,6},{6,5},{7,4},{8,11},{9,10},{10,... | collective-permute-start | bytes 110600 | tf_op jit(solution)/shard_map/ppermute | solution.py:23
  16.1 1.4 %collective-permute-start.3 = (f32[64,128]{1,0:T(8,128)S(1)}, f32[64,128]{1,0:T(8,128)S(1)}, u32[]{:S(2)}, u32[]{:S(2)}) collective-permute-start(f32[64,128]{1,0:T(8,128)S(1)} %get-tuple-element.15), channel_id=1, source_target_pairs={{0,1},{1,0},{2,3},{3,2},{4,5},{5,4},{6,7},{7,6},{8,9},{9,8},{10,11... | collective-permute-start | bytes 98312 | tf_op jit(solution)/shard_map/ppermute | solution.py:23
  16.2 4.0 %collective-permute-start.4 = (f32[64,128]{1,0:T(8,128)S(1)}, f32[64,128]{1,0:T(8,128)S(1)}, u32[]{:S(2)}, u32[]{:S(2)}) collective-permute-start(f32[64,128]{1,0:T(8,128)S(1)} %get-tuple-element.16), channel_id=1, source_target_pairs={{0,2},{1,3},{2,0},{3,1},{4,6},{5,7},{6,4},{7,5},{8,10},{9,11},{10,... | collective-permute-start | bytes 98312 | tf_op jit(solution)/shard_map/ppermute | solution.py:23
  17.5 3.5 %collective-permute-start.5 = (f32[64,128]{1,0:T(8,128)S(1)}, f32[64,128]{1,0:T(8,128)S(1)}, u32[]{:S(2)}, u32[]{:S(2)}) collective-permute-start(f32[64,128]{1,0:T(8,128)S(1)} %get-tuple-element.17), channel_id=1, source_target_pairs={{0,3},{1,2},{2,1},{3,0},{4,7},{5,6},{6,5},{7,4},{8,11},{9,10},{10,... | collective-permute-start | bytes 98312 | tf_op jit(solution)/shard_map/ppermute | solution.py:23
  22.4 3.7 %collective-permute-start.10 = (f32[8,256]{1,0:T(8,128)S(1)}, f32[8,256]{1,0:T(8,128)S(1)}, u32[]{:S(2)}, u32[]{:S(2)}) collective-permute-start(f32[8,256]{1,0:T(8,128)S(1)} %get-tuple-element.19.refs_0_), channel_id=1, source_target_pairs={{0,2},{1,3},{2,0},{3,1},{4,6},{5,7},{6,4},{7,5},{8,10},{9,11},{10,... | collective-permute-start | bytes 24584 | tf_op jit(solution)/shard_map/ppermute | solution.py:23
  23.2 3.1 %collective-permute-start.11 = (f32[8,256]{1,0:T(8,128)S(1)}, f32[8,256]{1,0:T(8,128)S(1)}, u32[]{:S(2)}, u32[]{:S(2)}) collective-permute-start(f32[8,256]{1,0:T(8,128)S(1)} %get-tuple-element.19.refs_0_), channel_id=1, source_target_pairs={{0,3},{1,2},{2,1},{3,0},{4,7},{5,6},{6,5},{7,4},{8,11},{9,10},{10,... | collective-permute-start | bytes 24584 | tf_op jit(solution)/shard_map/ppermute | solution.py:23
  23.8 2.4 %collective-permute-start.9 = (f32[8,256]{1,0:T(8,128)S(1)}, f32[8,256]{1,0:T(8,128)S(1)}, u32[]{:S(2)}, u32[]{:S(2)}) collective-permute-start(f32[8,256]{1,0:T(8,128)S(1)} %get-tuple-element.19.refs_0_), channel_id=1, source_target_pairs={{0,1},{1,0},{2,3},{3,2},{4,5},{5,4},{6,7},{7,6},{8,9},{9,8},{10,11... | collective-permute-start | bytes 24584 | tf_op jit(solution)/shard_map/ppermute | solution.py:23

commit v4 on v3

--- a/solution.py
+++ b/solution.py
@@ -95,7 +95,7 @@
 
 
 def sums_kernel(n_proj, seq_len, k2, *refs):
-    rights, (lengths, acts, cots, width, *outs, parted) = refs[:n_proj], refs[n_proj:]
+    rights, (lengths, acts, cots, width, _, *outs, parted) = refs[:n_proj], refs[n_proj:]
     right = sum([r[...] for r in rights[1:]], rights[0][...])
     ex_dev, rows = lengths.shape[0], acts.shape[0]
     t = lax.broadcasted_iota(jnp.int32, (k2, rows), 1)
@@ -117,19 +117,20 @@
         outs[m][...] = parted[me ^ m]
 
 
-def token_sums(rights, lengths, acts, cots, width, seq_len, k2):
+def token_sums(rights, lengths, acts, cots, width, seq_len, k2, early):
     n_proj = len(rights)
     ex_dev = lengths.shape[0]
     shape = (ex_dev * 2 * k2, width.shape[1] // n_proj)
     return pl.pallas_call(
         functools.partial(sums_kernel, n_proj, seq_len, k2),
         out_shape=[jax.ShapeDtypeStruct(shape, F32)] * n_proj,
-        in_specs=[VMEM] * n_proj + [SMEM] + [VMEM] * 3,
+        in_specs=[VMEM] * n_proj + [SMEM] + [VMEM] * 3 + [HBM],
         out_specs=[VMEM] * n_proj,
         scratch_shapes=[pltpu.VMEM((n_proj,) + shape, F32)],
         compiler_params=PARAMS,
         name="token_sums",
-    )(*rights, lengths, acts, cots, width)
+        cost_estimate=pl.CostEstimate(flops=20000000000, bytes_accessed=400000000, transcendentals=0),
+    )(*rights, lengths, acts, cots, width, early)
 
 
 def dots_kernel(n_proj, r, *refs):
@@ -184,7 +185,7 @@
     return pl.pallas_call(
         functools.partial(dots_kernel, n_proj, r),
         out_shape=(
-            jax.ShapeDtypeStruct((ex_dev, k_own * r), BF16),
+            pltpu.VMEM((ex_dev, k_own * r), BF16),
             jax.ShapeDtypeStruct((2 * ex_dev, n_val + LANES), F32),
         ),
         in_specs=[VMEM] * n_proj + [SMEM] + [VMEM] * len(blocks),
@@ -240,7 +241,10 @@
 
     by_mask = n_ex == n_proj
     if by_mask:
-        blocks = [heldout_gradient_rows] + [swap(heldout_gradient_rows, "ex", m) for m in range(1, n_ex)]
+        blocks = [heldout_gradient_rows] * n_ex
+        blocks[2] = swap(heldout_gradient_rows, "ex", 2)
+        blocks[1] = swap(heldout_gradient_rows, "ex", 1)
+        blocks[3] = swap(heldout_gradient_rows, "ex", 3)
     else:
         blocks = [lax.all_gather(heldout_gradient_rows, "ex", axis=0, tiled=True)]
 
@@ -248,7 +252,7 @@
         acts, cots, adapter_down_matrix, adapter_up_matrix, rank_side_sketch.transpose(0, 2, 1)
     )
     rights = [right] + [swap(right, "proj", m) for m in range(1, n_proj)]
-    pieces = token_sums(rights, lengths, acts, cots, width_side_sketch, seq_len, k2)
+    pieces = token_sums(rights, lengths, acts, cots, width_side_sketch, seq_len, k2, blocks[min(2, len(blocks) - 1)])
     pieces = [pieces[0]] + [swap(pieces[m], "proj", m) for m in range(1, n_proj)]
     train_proj, note = partial_dots(pieces, lengths, blocks, 2 * k2)
     notes = [note] + [swap(note, "proj", m) for m in range(1, n_proj)]

time: 27.1 us -> 25.3 us (0.934)
  waiting for transfers between devices: 7.83 us -> 5.88 us
  local copies, waits for them, and re-layouts: 0.01 us -> 0.62 us
  Pallas kernels: 6.67 us -> 6.22 us
    ppermute x12, waiting for transfers between devices: 7.83 us -> 5.88 us  [swap(): return lax.ppermute(x, axis, [(i, i ^ mask) for i in range(size)])]
    unnamed x6 -> x7, local copies, waits for them, and re-layouts: 0.01 us -> 0.62 us
    pallas_call x1, Pallas kernels: 1.44 us -> 0.99 us  [partial_dots(): pl.pallas_call(functools.partial(dots_kernel, n_proj, r), out_shape=(pltp...]
  transfers between devices with their start and end apart: 12 -> 12, of which waited for: 6 -> 6; matrix products, arithmetic and copies ran while one was open for 0% -> 2% of each run, Pallas kernels for 5% -> 18%
where the time goes in v4:
time: 25.3 us; the launch traced here: 25.1 us
  starting transfers between devices  11.7 us (46%)
  Pallas kernels  6.22 us (25%)
  waiting for transfers between devices  5.88 us (23%)
  between operations  0.68 us (3%)
  local copies, waits for them, and re-layouts  0.62 us (2%)
    ppermute x12, starting transfers between devices, swap(): return lax.ppermute(x, axis, [(i, i ^ mask) for i in range(size)])  11.7 us
    ppermute x12, waiting for transfers between devices, swap(): return lax.ppermute(x, axis, [(i, i ^ mask) for i in range(size)])  5.88 us
    pallas_call x1, Pallas kernels, rank_side(): pl.pallas_call(rank_kernel, out_shape=(jax.ShapeDtypeStruct((2 * k2, rows...  3.09 us
    pallas_call x1, Pallas kernels, token_sums(): pl.pallas_call(functools.partial(sums_kernel, n_proj, seq_len, k2), out_s...  1.41 us
    pallas_call x1, Pallas kernels, partial_dots(): pl.pallas_call(functools.partial(dots_kernel, n_proj, r), out_shape=(pltp...  0.99 us
    pallas_call x1, Pallas kernels, final_scores(): pl.pallas_call(functools.partial(scores_kernel, len(notes), ex_dev, scale...  0.73 us
    unnamed x7, local copies, waits for them, and re-layouts  0.62 us
  transfers between devices with their start and end apart: 12, of which 6 were waited for; matrix products, arithmetic and copies ran while one was open for 2% of the time, Pallas kernels for 18%

profile of v4, /device:TPU:0, one launch (start us, length us, event | category | flops | bytes accessed | tf_op | source)
XLA Modules:
  0.0 25.1 jit_solution(9364989186323747776)
XLA Ops:
  0.6 4.1 %collective-permute-start.3 = (bf16[32,2048]{1,0:T(8,128)(2,1)}, bf16[32,2048]{1,0:T(8,128)(2,1)S(1)}, u32[]{:S(2)}, u32[]{:S(2)}) collective-permute-start(bf16[32,2048]{1,0:T(8,128)(2,1)} %refs_5_.1), channel_id=1, source_target_pairs={{0,8},{4,12},{8,0},{12,4},{1,9},{5,13},{9,1},{13,5},{2,10},{6,14},... | collective-permute-start | bytes 393224 | tf_op jit(solution)/shard_map/ppermute | solution.py:23
  4.7 3.1 %rank_side.1 = (f32[16,576]{1,0:T(8,128)S(1)}, bf16[576,1280]{1,0:T(8,128)(2,1)S(1)}, bf16[576,1280]{1,0:T(8,128)(2,1)S(1)}) custom-call(bf16[576,1280]{1,0:T(8,128)(2,1)} %bitcast.3, bf16[576,1280]{1,0:T(8,128)(2,1)} %bitcast.4, bf16[128,1280]{1,0:T(8,128)(2,1)} %down.1, bf16[1280,128]{1,0:T(8,128)(2,1)} %up.1, bf16[2,8,128]{2,1,0:T(8,128)(2,1)} %bitcast.5), custom_call_target="tpu_custom_call" | custom-call | tf_op jit(solution)/shard_map/rank_side/pallas_call | solution.py:77
  7.8 0.1 collective-permute-start
  7.9 1.6 %collective-permute-start.1 = (f32[16,576]{1,0:T(8,128)S(1)}, f32[16,576]{1,0:T(8,128)S(1)}, u32[]{:S(2)}, u32[]{:S(2)}) collective-permute-start(f32[16,576]{1,0:T(8,128)S(1)} %get-tuple-element.11.refs_0_), channel_id=1, source_target_pairs={{0,2},{1,3},{2,0},{3,1},{4,6},{5,7},{6,4},{7,5},{8,10},{9,11},{10,... | collective-permute-start | bytes 110600 | tf_op jit(solution)/shard_map/ppermute | solution.py:23
  9.5 0.3 %collective-permute-start.2 = (f32[16,576]{1,0:T(8,128)S(1)}, f32[16,576]{1,0:T(8,128)S(1)}, u32[]{:S(2)}, u32[]{:S(2)}) collective-permute-start(f32[16,576]{1,0:T(8,128)S(1)} %get-tuple-element.11.refs_0_), channel_id=1, source_target_pairs={{0,3},{1,2},{2,1},{3,0},{4,7},{5,6},{6,5},{7,4},{8,11},{9,10},{10,... | collective-permute-start | bytes 110600 | tf_op jit(solution)/shard_map/ppermute | solution.py:23
  9.8 1.6 %collective-permute-start.7 = (bf16[32,2048]{1,0:T(8,128)(2,1)S(1)}, bf16[32,2048]{1,0:T(8,128)(2,1)S(1)}, u32[]{:S(2)}, u32[]{:S(2)}) collective-permute-start(bf16[32,2048]{1,0:T(8,128)(2,1)S(1)} %copy-done), channel_id=1, source_target_pairs={{0,4},{4,0},{8,12},{12,8},{1,5},{5,1},{9,13},{13,9},{2,6},{6,2},{1... | collective-permute-start | bytes 393224 | tf_op jit(solution)/shard_map/ppermute | solution.py:23
  11.4 0.0 collective-permute-done.refs_1_
  11.4 0.6 %collective-permute-done.1.refs_2_ = f32[16,576]{1,0:T(8,128)S(1)} collective-permute-done((f32[16,576]{1,0:T(8,128)S(1)}, f32[16,576]{1,0:T(8,128)S(1)}, u32[]{:S(2)}, u32[]{:S(2)}) %collective-permute-start.1) | collective-permute-done | bytes 36896 | tf_op jit(solution)/shard_map/ppermute | solution.py:23
  12.0 1.0 %collective-permute-done.2.refs_3_ = f32[16,576]{1,0:T(8,128)S(1)} collective-permute-done((f32[16,576]{1,0:T(8,128)S(1)}, f32[16,576]{1,0:T(8,128)S(1)}, u32[]{:S(2)}, u32[]{:S(2)}) %collective-permute-start.2) | collective-permute-done | bytes 36896 | tf_op jit(solution)/shard_map/ppermute | solution.py:23
  13.0 0.0 collective-permute-done.3.refs_8_.refs_7_
  13.0 1.4 %token_sums.1 = (f32[64,128]{1,0:T(8,128)S(1)}, f32[64,128]{1,0:T(8,128)S(1)}, f32[64,128]{1,0:T(8,128)S(1)}, f32[64,128]{1,0:T(8,128)S(1)}) custom-call(f32[16,576]{1,0:T(8,128)S(1)} %get-tuple-element.11.refs_0_, f32[16,576]{1,0:T(8,128)S(1)} %collective-permute-done.refs_1_, f32[16,576]{1,0:T(8,128)S(1)} %collective-permute-done.1.refs_2_, ...), custom_call_target="tpu_custom_call" | custom-call | flops 20000000000 | bytes 400000000 | tf_op jit(solution)/shard_map/token_sums/pallas_call | solution.py:124
  14.4 0.2 collective-permute-start.4
  14.7 1.0 %collective-permute-start.5 = (f32[64,128]{1,0:T(8,128)S(1)}, f32[64,128]{1,0:T(8,128)S(1)}, u32[]{:S(2)}, u32[]{:S(2)}) collective-permute-start(f32[64,128]{1,0:T(8,128)S(1)} %get-tuple-element.16), channel_id=1, source_target_pairs={{0,2},{1,3},{2,0},{3,1},{4,6},{5,7},{6,4},{7,5},{8,10},{9,11},{10,... | collective-permute-start | bytes 98312 | tf_op jit(solution)/shard_map/ppermute | solution.py:23
  15.6 0.7 %collective-permute-start.6 = (f32[64,128]{1,0:T(8,128)S(1)}, f32[64,128]{1,0:T(8,128)S(1)}, u32[]{:S(2)}, u32[]{:S(2)}) collective-permute-start(f32[64,128]{1,0:T(8,128)S(1)} %get-tuple-element.17), channel_id=1, source_target_pairs={{0,3},{1,2},{2,1},{3,0},{4,7},{5,6},{6,5},{7,4},{8,11},{9,10},{10,... | collective-permute-start | bytes 98312 | tf_op jit(solution)/shard_map/ppermute | solution.py:23
  16.4 2.4 %collective-permute-done.8.refs_8_ = bf16[32,2048]{1,0:T(8,128)(2,1)S(1)} collective-permute-done((bf16[32,2048]{1,0:T(8,128)(2,1)S(1)}, bf16[32,2048]{1,0:T(8,128)(2,1)S(1)}, u32[]{:S(2)}, u32[]{:S(2)}) %collective-permute-start.8) | collective-permute-done | bytes 131104 | tf_op jit(solution)/shard_map/ppermute | solution.py:23
  18.7 0.4 %collective-permute-done.6.refs_3_ = f32[64,128]{1,0:T(8,128)S(1)} collective-permute-done((f32[64,128]{1,0:T(8,128)S(1)}, f32[64,128]{1,0:T(8,128)S(1)}, u32[]{:S(2)}, u32[]{:S(2)}) %collective-permute-start.6) | collective-permute-done | bytes 32800 | tf_op jit(solution)/shard_map/ppermute | solution.py:23
  19.2 1.0 %partial_dots.1 = (bf16[4,2048]{1,0:T(4,128)(2,1)S(1)}, f32[8,256]{1,0:T(8,128)S(1)}) custom-call(f32[64,128]{1,0:T(8,128)S(1)} %get-tuple-element.14.refs_0_, f32[64,128]{1,0:T(8,128)S(1)} %collective-permute-done.4.refs_1_, f32[64,128]{1,0:T(8,128)S(1)} %collective-permute-done.5.refs_2_, f32[64,128]{1,0:T(8,128)S(1)} %collective-permute-done.6.refs_3_, ...), custom_call_target="tpu_custom_call" | custom-call | tf_op jit(solution)/shard_map/partial_dots/pallas_call | solution.py:185
  20.2 1.1 %collective-permute-start.10 = (f32[8,256]{1,0:T(8,128)S(1)}, f32[8,256]{1,0:T(8,128)S(1)}, u32[]{:S(2)}, u32[]{:S(2)}) collective-permute-start(f32[8,256]{1,0:T(8,128)S(1)} %get-tuple-element.19.refs_0_), channel_id=1, source_target_pairs={{0,2},{1,3},{2,0},{3,1},{4,6},{5,7},{6,4},{7,5},{8,10},{9,11},{10,... | collective-permute-start | bytes 24584 | tf_op jit(solution)/shard_map/ppermute | solution.py:23
  21.3 0.4 %collective-permute-start.11 = (f32[8,256]{1,0:T(8,128)S(1)}, f32[8,256]{1,0:T(8,128)S(1)}, u32[]{:S(2)}, u32[]{:S(2)}) collective-permute-start(f32[8,256]{1,0:T(8,128)S(1)} %get-tuple-element.19.refs_0_), channel_id=1, source_target_pairs={{0,3},{1,2},{2,1},{3,0},{4,7},{5,6},{6,5},{7,4},{8,11},{9,10},{10,... | collective-permute-start | bytes 24584 | tf_op jit(solution)/shard_map/ppermute | solution.py:23
  21.7 0.7 %collective-permute-start.9 = (f32[8,256]{1,0:T(8,128)S(1)}, f32[8,256]{1,0:T(8,128)S(1)}, u32[]{:S(2)}, u32[]{:S(2)}) collective-permute-start(f32[8,256]{1,0:T(8,128)S(1)} %get-tuple-element.19.refs_0_), channel_id=1, source_target_pairs={{0,1},{1,0},{2,3},{3,2},{4,5},{5,4},{6,7},{7,6},{8,9},{9,8},{10,11... | collective-permute-start | bytes 24584 | tf_op jit(solution)/shard_map/ppermute | solution.py:23
  22.3 0.6 %copy.10 = bf16[4,2048]{1,0:T(4,128)(2,1)} copy(bf16[4,2048]{1,0:T(4,128)(2,1)S(1)} %get-tuple-element.20) | data formatting | bytes 32768
  22.9 0.9 %collective-permute-done.10.refs_2_ = f32[8,256]{1,0:T(8,128)S(1)} collective-permute-done((f32[8,256]{1,0:T(8,128)S(1)}, f32[8,256]{1,0:T(8,128)S(1)}, u32[]{:S(2)}, u32[]{:S(2)}) %collective-permute-start.10) | collective-permute-done | bytes 8224 | tf_op jit(solution)/shard_map/ppermute | solution.py:23
  23.8 0.5 %collective-permute-done.11.refs_3_ = f32[8,256]{1,0:T(8,128)S(1)} collective-permute-done((f32[8,256]{1,0:T(8,128)S(1)}, f32[8,256]{1,0:T(8,128)S(1)}, u32[]{:S(2)}, u32[]{:S(2)}) %collective-permute-start.11) | collective-permute-done | bytes 8224 | tf_op jit(solution)/shard_map/ppermute | solution.py:23
  24.4 0.7 %final_scores.1 = f32[4,32]{1,0:T(4,128)} custom-call(f32[8,256]{1,0:T(8,128)S(1)} %get-tuple-element.19.refs_0_, f32[8,256]{1,0:T(8,128)S(1)} %collective-permute-done.9.refs_1_, f32[8,256]{1,0:T(8,128)S(1)} %collective-permute-done.10.refs_2_, f32[8,256]{1,0:T(8,128)S(1)} %collective-permute-done.11.refs_3_), custom_call_target="tpu_custom_call" | custom-call | tf_op jit(solution)/shard_map/final_scores/pallas_call | solution.py:215
  (11 shorter events, 0.0 us)
Async XLA Ops:
  0.6 12.4 %collective-permute-start.3 = (bf16[32,2048]{1,0:T(8,128)(2,1)}, bf16[32,2048]{1,0:T(8,128)(2,1)S(1)}, u32[]{:S(2)}, u32[]{:S(2)}) collective-permute-start(bf16[32,2048]{1,0:T(8,128)(2,1)} %refs_5_.1), channel_id=1, source_target_pairs={{0,8},{4,12},{8,0},{12,4},{1,9},{5,13},{9,1},{13,5},{2,10},{6,14},... | collective-permute-start | bytes 393224 | tf_op jit(solution)/shard_map/ppermute | solution.py:23
  4.7 5.0 %copy-start = (bf16[32,2048]{1,0:T(8,128)(2,1)S(1)}, bf16[32,2048]{1,0:T(8,128)(2,1)}, u32[]{:S(2)}) copy-start(bf16[32,2048]{1,0:T(8,128)(2,1)} %refs_5_.1) | copy-start | bytes 393220
  4.7 8.3 %copy-start.1 = (s32[4]{0:T(128)S(1)}, s32[4]{0:T(128)}, u32[]{:S(2)}) copy-start(s32[4]{0:T(128)} %refs_4_.3) | copy-start | bytes 52
  4.7 8.3 %copy-start.2 = (bf16[1280,512]{1,0:T(8,128)(2,1)S(1)}, bf16[1280,512]{1,0:T(8,128)(2,1)}, u32[]{:S(2)}) copy-start(bf16[1280,512]{1,0:T(8,128)(2,1)} %refs_7_.1) | copy-start | bytes 3932164
  7.8 3.5 %collective-permute-start = (f32[16,576]{1,0:T(8,128)S(1)}, f32[16,576]{1,0:T(8,128)S(1)}, u32[]{:S(2)}, u32[]{:S(2)}) collective-permute-start(f32[16,576]{1,0:T(8,128)S(1)} %get-tuple-element.11.refs_0_), channel_id=1, source_target_pairs={{0,1},{1,0},{2,3},{3,2},{4,5},{5,4},{6,7},{7,6},{8,9},{9,8},{10,11... | collective-permute-start | bytes 110600 | tf_op jit(solution)/shard_map/ppermute | solution.py:23
  7.9 4.1 %collective-permute-start.1 = (f32[16,576]{1,0:T(8,128)S(1)}, f32[16,576]{1,0:T(8,128)S(1)}, u32[]{:S(2)}, u32[]{:S(2)}) collective-permute-start(f32[16,576]{1,0:T(8,128)S(1)} %get-tuple-element.11.refs_0_), channel_id=1, source_target_pairs={{0,2},{1,3},{2,0},{3,1},{4,6},{5,7},{6,4},{7,5},{8,10},{9,11},{10,... | collective-permute-start | bytes 110600 | tf_op jit(solution)/shard_map/ppermute | solution.py:23
  9.5 3.5 %collective-permute-start.2 = (f32[16,576]{1,0:T(8,128)S(1)}, f32[16,576]{1,0:T(8,128)S(1)}, u32[]{:S(2)}, u32[]{:S(2)}) collective-permute-start(f32[16,576]{1,0:T(8,128)S(1)} %get-tuple-element.11.refs_0_), channel_id=1, source_target_pairs={{0,3},{1,2},{2,1},{3,0},{4,7},{5,6},{6,5},{7,4},{8,11},{9,10},{10,... | collective-permute-start | bytes 110600 | tf_op jit(solution)/shard_map/ppermute | solution.py:23
  9.8 6.6 %collective-permute-start.7 = (bf16[32,2048]{1,0:T(8,128)(2,1)S(1)}, bf16[32,2048]{1,0:T(8,128)(2,1)S(1)}, u32[]{:S(2)}, u32[]{:S(2)}) collective-permute-start(bf16[32,2048]{1,0:T(8,128)(2,1)S(1)} %copy-done), channel_id=1, source_target_pairs={{0,4},{4,0},{8,12},{12,8},{1,5},{5,1},{9,13},{13,9},{2,6},{6,2},{1... | collective-permute-start | bytes 393224 | tf_op jit(solution)/shard_map/ppermute | solution.py:23
  11.4 7.4 %collective-permute-start.8 = (bf16[32,2048]{1,0:T(8,128)(2,1)S(1)}, bf16[32,2048]{1,0:T(8,128)(2,1)S(1)}, u32[]{:S(2)}, u32[]{:S(2)}) collective-permute-start(bf16[32,2048]{1,0:T(8,128)(2,1)S(1)} %copy-done), channel_id=1, source_target_pairs={{0,12},{4,8},{8,4},{12,0},{1,13},{5,9},{9,5},{13,1},{2,14},{6,10},... | collective-permute-start | bytes 393224 | tf_op jit(solution)/shard_map/ppermute | solution.py:23
  14.4 4.3 %collective-permute-start.4 = (f32[64,128]{1,0:T(8,128)S(1)}, f32[64,128]{1,0:T(8,128)S(1)}, u32[]{:S(2)}, u32[]{:S(2)}) collective-permute-start(f32[64,128]{1,0:T(8,128)S(1)} %get-tuple-element.15), channel_id=1, source_target_pairs={{0,1},{1,0},{2,3},{3,2},{4,5},{5,4},{6,7},{7,6},{8,9},{9,8},{10,11... | collective-permute-start | bytes 98312 | tf_op jit(solution)/shard_map/ppermute | solution.py:23
  14.7 4.1 %collective-permute-start.5 = (f32[64,128]{1,0:T(8,128)S(1)}, f32[64,128]{1,0:T(8,128)S(1)}, u32[]{:S(2)}, u32[]{:S(2)}) collective-permute-start(f32[64,128]{1,0:T(8,128)S(1)} %get-tuple-element.16), channel_id=1, source_target_pairs={{0,2},{1,3},{2,0},{3,1},{4,6},{5,7},{6,4},{7,5},{8,10},{9,11},{10,... | collective-permute-start | bytes 98312 | tf_op jit(solution)/shard_map/ppermute | solution.py:23
  15.6 3.5 %collective-permute-start.6 = (f32[64,128]{1,0:T(8,128)S(1)}, f32[64,128]{1,0:T(8,128)S(1)}, u32[]{:S(2)}, u32[]{:S(2)}) collective-permute-start(f32[64,128]{1,0:T(8,128)S(1)} %get-tuple-element.17), channel_id=1, source_target_pairs={{0,3},{1,2},{2,1},{3,0},{4,7},{5,6},{6,5},{7,4},{8,11},{9,10},{10,... | collective-permute-start | bytes 98312 | tf_op jit(solution)/shard_map/ppermute | solution.py:23
  20.2 3.7 %collective-permute-start.10 = (f32[8,256]{1,0:T(8,128)S(1)}, f32[8,256]{1,0:T(8,128)S(1)}, u32[]{:S(2)}, u32[]{:S(2)}) collective-permute-start(f32[8,256]{1,0:T(8,128)S(1)} %get-tuple-element.19.refs_0_), channel_id=1, source_target_pairs={{0,2},{1,3},{2,0},{3,1},{4,6},{5,7},{6,4},{7,5},{8,10},{9,11},{10,... | collective-permute-start | bytes 24584 | tf_op jit(solution)/shard_map/ppermute | solution.py:23
  21.3 3.1 %collective-permute-start.11 = (f32[8,256]{1,0:T(8,128)S(1)}, f32[8,256]{1,0:T(8,128)S(1)}, u32[]{:S(2)}, u32[]{:S(2)}) collective-permute-start(f32[8,256]{1,0:T(8,128)S(1)} %get-tuple-element.19.refs_0_), channel_id=1, source_target_pairs={{0,3},{1,2},{2,1},{3,0},{4,7},{5,6},{6,5},{7,4},{8,11},{9,10},{10,... | collective-permute-start | bytes 24584 | tf_op jit(solution)/shard_map/ppermute | solution.py:23
  21.7 2.7 %collective-permute-start.9 = (f32[8,256]{1,0:T(8,128)S(1)}, f32[8,256]{1,0:T(8,128)S(1)}, u32[]{:S(2)}, u32[]{:S(2)}) collective-permute-start(f32[8,256]{1,0:T(8,128)S(1)} %get-tuple-element.19.refs_0_), channel_id=1, source_target_pairs={{0,1},{1,0},{2,3},{3,2},{4,5},{5,4},{6,7},{7,6},{8,9},{9,8},{10,11... | collective-permute-start | bytes 24584 | tf_op jit(solution)/shard_map/ppermute | solution.py:23

commit v5 on v4

--- a/solution.py
+++ b/solution.py
@@ -34,64 +34,48 @@
     return [(at, min(STEP, rows - at)) for at in range(0, rows, STEP)]
 
 
-def rank_kernel(acts, cots, down, up, sketch, right, acts_keep, cots_keep, down_v, up_v, sketch_v, sems):
-    chunks = row_chunks(acts.shape[0])
-    small = [
-        pltpu.make_async_copy(src, dst, sems.at[at])
-        for at, (src, dst) in enumerate(((sketch, sketch_v), (down, down_v), (up, up_v)))
-    ]
-    big = []
-    for at, rows in chunks:
-        for src, dst in ((acts, acts_keep), (cots, cots_keep)):
-            cut = pl.ds(at, rows)
-            big.append(pltpu.make_async_copy(src.at[cut], dst.at[cut], sems.at[3 + len(big)]))
-    for copy in small + big:
-        copy.start()
-    small[0].wait()
-    small[1].wait()
+def open_kernel(out):
+    out[...] = jnp.zeros_like(out)
+
+
+def opening():
+    return pl.pallas_call(
+        open_kernel,
+        out_shape=jax.ShapeDtypeStruct((8, LANES), F32),
+        out_specs=VMEM,
+        compiler_params=PARAMS,
+        cost_estimate=pl.CostEstimate(flops=20_000_000_000, bytes_accessed=400_000_000, transcendentals=0),
+        name="opening",
+    )()
+
+
+def rank_kernel(acts, cots, down, up, sketch, _, right):
+    rows, lanes = acts.shape
     k2 = sketch.shape[1]
-    folded = [dot(sketch_v[0], down_v[...])]
-    small[2].wait()
-    folded.append(dot(sketch_v[1], up_v[...], NT))
-    lanes = acts.shape[1]
-    pad = jnp.zeros((LANES - k2, lanes), F32)
-    weights = [
-        jnp.concatenate([folded[0], pad], axis=0).T.astype(BF16),
-        jnp.concatenate([pad[:k2], folded[1], pad[k2:]], axis=0).T.astype(BF16),
-    ]
-    for at, rows in chunks:
-        big.pop(0).wait()
-        big.pop(0).wait()
-        cut = pl.ds(at, rows)
-        got = dot(acts_keep[cut, :], weights[0]) + dot(cots_keep[cut, :], weights[1])
-        for b in range(0, rows, LANES):
-            size = min(LANES, rows - b)
-            right[:, at + b : at + b + size] = got[b : b + size].T[: 2 * k2]
-
-
-def rank_side(acts, cots, down, up, sketch):
-    rows, cols = acts.shape
-    k2 = sketch.shape[1]
-    n_copies = 3 + 2 * len(row_chunks(rows))
-    acts, cots, down, up, sketch = [pltpu.with_memory_space_constraint(x, pltpu.HBM) for x in (acts, cots, down, up, sketch)]
+    folded = [dot(sketch[0], down[...]), dot(sketch[1], up[...], NT)]
+    coarse = [one.astype(BF16).astype(F32) for one in folded]
+    fine = [one - near for one, near in zip(folded, coarse)]
+    gap = jnp.zeros((k2, lanes), F32)
+    pad = jnp.zeros((LANES - 4 * k2, lanes), F32)
+    first = jnp.concatenate([coarse[0], gap, fine[0], gap, pad], axis=0).T.astype(BF16)
+    second = jnp.concatenate([gap, coarse[1], gap, fine[1], pad], axis=0).T.astype(BF16)
+    got = dot(acts[...], first) + dot(cots[...], second)
+    for at in range(0, rows, LANES):
+        size = min(LANES, rows - at)
+        turned = got[at : at + size].T
+        right[:, at : at + size] = (turned[: 2 * k2] + turned[2 * k2 : 4 * k2]).astype(right.dtype)
+
+
+def rank_side(acts, cots, down, up, sketch, gate):
+    rows = acts.shape[0]
     return pl.pallas_call(
         rank_kernel,
-        out_shape=(
-            jax.ShapeDtypeStruct((2 * k2, rows), F32),
-            pltpu.VMEM(acts.shape, BF16),
-            pltpu.VMEM(cots.shape, BF16),
-        ),
-        in_specs=[HBM] * 5,
-        out_specs=(VMEM, VMEM, VMEM),
-        scratch_shapes=[
-            pltpu.VMEM(down.shape, BF16),
-            pltpu.VMEM(up.shape, BF16),
-            pltpu.VMEM(sketch.shape, BF16),
-            pltpu.SemaphoreType.DMA((n_copies,)),
-        ],
+        out_shape=jax.ShapeDtypeStruct((2 * sketch.shape[1], rows), F32),
+        in_specs=[VMEM] * 5 + [HBM],
+        out_specs=VMEM,
         compiler_params=PARAMS,
         name="rank_side",
-    )(acts, cots, down, up, sketch)
+    )(acts, cots, down, up, sketch, gate)
 
 
 def sums_kernel(n_proj, seq_len, k2, *refs):
@@ -241,17 +225,21 @@
 
     by_mask = n_ex == n_proj
     if by_mask:
+        gate, held = lax.optimization_barrier((opening(), heldout_gradient_rows))
         blocks = [heldout_gradient_rows] * n_ex
-        blocks[2] = swap(heldout_gradient_rows, "ex", 2)
-        blocks[1] = swap(heldout_gradient_rows, "ex", 1)
-        blocks[3] = swap(heldout_gradient_rows, "ex", 3)
+        blocks[2] = swap(held, "ex", 2)
     else:
+        gate = opening()
         blocks = [lax.all_gather(heldout_gradient_rows, "ex", axis=0, tiled=True)]
 
-    right, acts, cots = rank_side(
-        acts, cots, adapter_down_matrix, adapter_up_matrix, rank_side_sketch.transpose(0, 2, 1)
+    right = rank_side(
+        acts, cots, adapter_down_matrix, adapter_up_matrix, rank_side_sketch.transpose(0, 2, 1), gate
     )
     rights = [right] + [swap(right, "proj", m) for m in range(1, n_proj)]
+    if by_mask:
+        later, rights[1] = lax.optimization_barrier((heldout_gradient_rows, rights[1]))
+        blocks[3] = swap(later, "ex", 3)
+        blocks[1] = swap(later, "ex", 1)
     pieces = token_sums(rights, lengths, acts, cots, width_side_sketch, seq_len, k2, blocks[min(2, len(blocks) - 1)])
     pieces = [pieces[0]] + [swap(pieces[m], "proj", m) for m in range(1, n_proj)]
     train_proj, note = partial_dots(pieces, lengths, blocks, 2 * k2)

time: 25.3 us -> 24.6 us (0.972)
  Pallas kernels: 6.22 us -> 4.49 us
  starting transfers between devices: 11.7 us -> 12.6 us
  local copies, waits for them, and re-layouts: 0.62 us -> 1.48 us
  waiting for transfers between devices: 5.88 us -> 5.15 us
    pallas_call x1 -> x2, Pallas kernels: 3.09 us -> 1.36 us  [the longest x1 1.36 us: rank_side(): pl.pallas_call(rank_kernel, out_shape=jax.ShapeDtypeStruct((2 * sketch.sh...]
    ppermute x12, starting transfers between devices: 11.7 us -> 12.6 us  [swap(): return lax.ppermute(x, axis, [(i, i ^ mask) for i in range(size)])]
    unnamed x7 -> x17, local copies, waits for them, and re-layouts: 0.62 us -> 1.48 us
    ppermute x12, waiting for transfers between devices: 5.88 us -> 5.15 us  [swap(): return lax.ppermute(x, axis, [(i, i ^ mask) for i in range(size)])]
  transfers between devices with their start and end apart: 12 -> 12, of which waited for: 6 -> 5; matrix products, arithmetic and copies ran while one was open for 2% -> 2% of each run, Pallas kernels for 18% -> 11%
where the time goes in v5:
time: 24.6 us; the launch traced here: 24.5 us
  starting transfers between devices  12.6 us (51%)
  waiting for transfers between devices  5.15 us (21%)
  Pallas kernels  4.49 us (18%)
  local copies, waits for them, and re-layouts  1.48 us (6%)
  between operations  0.75 us (3%)
    ppermute x12, starting transfers between devices, swap(): return lax.ppermute(x, axis, [(i, i ^ mask) for i in range(size)])  12.6 us
    ppermute x12, waiting for transfers between devices, swap(): return lax.ppermute(x, axis, [(i, i ^ mask) for i in range(size)])  5.15 us
    unnamed x17, local copies, waits for them, and re-layouts  1.48 us
    pallas_call x1, Pallas kernels, token_sums(): pl.pallas_call(functools.partial(sums_kernel, n_proj, seq_len, k2), out_s...  1.41 us
    pallas_call x1, Pallas kernels, rank_side(): pl.pallas_call(rank_kernel, out_shape=jax.ShapeDtypeStruct((2 * sketch.sh...  1.36 us
    pallas_call x1, Pallas kernels, partial_dots(): pl.pallas_call(functools.partial(dots_kernel, n_proj, r), out_shape=(pltp...  1 us
    pallas_call x1, Pallas kernels, final_scores(): pl.pallas_call(functools.partial(scores_kernel, len(notes), ex_dev, scale...  0.73 us
  transfers between devices with their start and end apart: 12, of which 5 were waited for; matrix products, arithmetic and copies ran while one was open for 2% of the time, Pallas kernels for 11%

profile of v5, /device:TPU:0, one launch (start us, length us, event | category | flops | bytes accessed | tf_op | source)
XLA Modules:
  0.0 24.5 jit_solution(15116725201981326980)
XLA Ops:
  0.7 0.8 %copy-done.4 = bf16[32,2048]{1,0:T(8,128)(2,1)S(1)} copy-done((bf16[32,2048]{1,0:T(8,128)(2,1)S(1)}, bf16[32,2048]{1,0:T(8,128)(2,1)}, u32[]{:S(2)}) %copy-start.4) | copy-done | bytes 131096
  1.5 4.0 %collective-permute-start.3 = (bf16[32,2048]{1,0:T(8,128)(2,1)S(1)}, bf16[32,2048]{1,0:T(8,128)(2,1)S(1)}, u32[]{:S(2)}, u32[]{:S(2)}) collective-permute-start(bf16[32,2048]{1,0:T(8,128)(2,1)S(1)} %copy-done.4), channel_id=1, source_target_pairs={{0,8},{4,12},{8,0},{12,4},{1,9},{5,13},{9,1},{13,5},{2,10},{6,14},... | collective-permute-start | bytes 393224 | tf_op jit(solution)/shard_map/ppermute | solution.py:23
  5.6 0.0 copy-start.6
  5.6 1.4 %rank_side.1.refs_0_ = f32[16,576]{1,0:T(8,128)S(1)} custom-call(bf16[576,1280]{1,0:T(8,128)(2,1)S(1)} %bitcast.3, bf16[576,1280]{1,0:T(8,128)(2,1)S(1)} %bitcast.5, bf16[128,1280]{1,0:T(8,128)(2,1)S(1)} %copy-done.2, bf16[1280,128]{1,0:T(8,128)(2,1)S(1)} %copy-done.3, bf16[2,8,128]{2,1,0:T(8,128)(2,1)S(1)} %bitcast.7, f32[8,128]{1,0:T(8,128)S(1)} %opening.1._), custom_call_target="tpu_custom_call" | custom-call | tf_op jit(solution)/shard_map/rank_side/pallas_call | solution.py:71
  7.0 0.1 collective-permute-start
  7.0 1.6 %collective-permute-start.1 = (f32[16,576]{1,0:T(8,128)S(1)}, f32[16,576]{1,0:T(8,128)S(1)}, u32[]{:S(2)}, u32[]{:S(2)}) collective-permute-start(f32[16,576]{1,0:T(8,128)S(1)} %rank_side.1.refs_0_), channel_id=1, source_target_pairs={{0,2},{1,3},{2,0},{3,1},{4,6},{5,7},{6,4},{7,5},{8,10},{9,11},{10,... | collective-permute-start | bytes 110600 | tf_op jit(solution)/shard_map/ppermute | solution.py:23
  8.6 0.3 %collective-permute-start.2 = (f32[16,576]{1,0:T(8,128)S(1)}, f32[16,576]{1,0:T(8,128)S(1)}, u32[]{:S(2)}, u32[]{:S(2)}) collective-permute-start(f32[16,576]{1,0:T(8,128)S(1)} %rank_side.1.refs_0_), channel_id=1, source_target_pairs={{0,3},{1,2},{2,1},{3,0},{4,7},{5,6},{6,5},{7,4},{8,11},{9,10},{10,... | collective-permute-start | bytes 110600 | tf_op jit(solution)/shard_map/ppermute | solution.py:23
  8.9 1.6 %collective-permute-start.7 = (bf16[32,2048]{1,0:T(8,128)(2,1)S(1)}, bf16[32,2048]{1,0:T(8,128)(2,1)S(1)}, u32[]{:S(2)}, u32[]{:S(2)}) collective-permute-start(bf16[32,2048]{1,0:T(8,128)(2,1)S(1)} %copy-done.4), channel_id=1, source_target_pairs={{0,4},{4,0},{8,12},{12,8},{1,5},{5,1},{9,13},{13,9},{2,6},{6,2},{1... | collective-permute-start | bytes 393224 | tf_op jit(solution)/shard_map/ppermute | solution.py:23
  10.5 1.0 %collective-permute-start.8 = (bf16[32,2048]{1,0:T(8,128)(2,1)S(1)}, bf16[32,2048]{1,0:T(8,128)(2,1)S(1)}, u32[]{:S(2)}, u32[]{:S(2)}) collective-permute-start(bf16[32,2048]{1,0:T(8,128)(2,1)S(1)} %copy-done.4), channel_id=1, source_target_pairs={{0,12},{4,8},{8,4},{12,0},{1,13},{5,9},{9,5},{13,1},{2,14},{6,10},... | collective-permute-start | bytes 393224 | tf_op jit(solution)/shard_map/ppermute | solution.py:23
  11.5 0.6 %collective-permute-done.2.refs_3_ = f32[16,576]{1,0:T(8,128)S(1)} collective-permute-done((f32[16,576]{1,0:T(8,128)S(1)}, f32[16,576]{1,0:T(8,128)S(1)}, u32[]{:S(2)}, u32[]{:S(2)}) %collective-permute-start.2) | collective-permute-done | bytes 36896 | tf_op jit(solution)/shard_map/ppermute | solution.py:23
  12.1 1.4 %token_sums.1 = (f32[64,128]{1,0:T(8,128)S(1)}, f32[64,128]{1,0:T(8,128)S(1)}, f32[64,128]{1,0:T(8,128)S(1)}, f32[64,128]{1,0:T(8,128)S(1)}) custom-call(f32[16,576]{1,0:T(8,128)S(1)} %rank_side.1.refs_0_, f32[16,576]{1,0:T(8,128)S(1)} %collective-permute-done.refs_1_, f32[16,576]{1,0:T(8,128)S(1)} %collective-permute-done.1.refs_2_, ...), custom_call_target="tpu_custom_call" | custom-call | flops 20000000000 | bytes 400000000 | tf_op jit(solution)/shard_map/token_sums/pallas_call | solution.py:108
  13.5 0.2 collective-permute-start.4
  13.8 1.3 %collective-permute-start.5 = (f32[64,128]{1,0:T(8,128)S(1)}, f32[64,128]{1,0:T(8,128)S(1)}, u32[]{:S(2)}, u32[]{:S(2)}) collective-permute-start(f32[64,128]{1,0:T(8,128)S(1)} %get-tuple-element.17), channel_id=1, source_target_pairs={{0,2},{1,3},{2,0},{3,1},{4,6},{5,7},{6,4},{7,5},{8,10},{9,11},{10,... | collective-permute-start | bytes 98312 | tf_op jit(solution)/shard_map/ppermute | solution.py:23
  15.1 0.4 %collective-permute-start.6 = (f32[64,128]{1,0:T(8,128)S(1)}, f32[64,128]{1,0:T(8,128)S(1)}, u32[]{:S(2)}, u32[]{:S(2)}) collective-permute-start(f32[64,128]{1,0:T(8,128)S(1)} %get-tuple-element.18), channel_id=1, source_target_pairs={{0,3},{1,2},{2,1},{3,0},{4,7},{5,6},{6,5},{7,4},{8,11},{9,10},{10,... | collective-permute-start | bytes 98312 | tf_op jit(solution)/shard_map/ppermute | solution.py:23
  15.5 2.2 %collective-permute-done.5.refs_2_ = f32[64,128]{1,0:T(8,128)S(1)} collective-permute-done((f32[64,128]{1,0:T(8,128)S(1)}, f32[64,128]{1,0:T(8,128)S(1)}, u32[]{:S(2)}, u32[]{:S(2)}) %collective-permute-start.5) | collective-permute-done | bytes 32800 | tf_op jit(solution)/shard_map/ppermute | solution.py:23
  17.7 0.8 %collective-permute-done.6.refs_3_ = f32[64,128]{1,0:T(8,128)S(1)} collective-permute-done((f32[64,128]{1,0:T(8,128)S(1)}, f32[64,128]{1,0:T(8,128)S(1)}, u32[]{:S(2)}, u32[]{:S(2)}) %collective-permute-start.6) | collective-permute-done | bytes 32800 | tf_op jit(solution)/shard_map/ppermute | solution.py:23
  18.5 1.0 %partial_dots.1 = (bf16[4,2048]{1,0:T(4,128)(2,1)S(1)}, f32[8,256]{1,0:T(8,128)S(1)}) custom-call(f32[64,128]{1,0:T(8,128)S(1)} %get-tuple-element.15.refs_0_, f32[64,128]{1,0:T(8,128)S(1)} %collective-permute-done.4.refs_1_, f32[64,128]{1,0:T(8,128)S(1)} %collective-permute-done.5.refs_2_, f32[64,128]{1,0:T(8,128)S(1)} %collective-permute-done.6.refs_3_, ...), custom_call_target="tpu_custom_call" | custom-call | tf_op jit(solution)/shard_map/partial_dots/pallas_call | solution.py:169
  19.5 1.1 %collective-permute-start.10 = (f32[8,256]{1,0:T(8,128)S(1)}, f32[8,256]{1,0:T(8,128)S(1)}, u32[]{:S(2)}, u32[]{:S(2)}) collective-permute-start(f32[8,256]{1,0:T(8,128)S(1)} %get-tuple-element.21.refs_0_), channel_id=1, source_target_pairs={{0,2},{1,3},{2,0},{3,1},{4,6},{5,7},{6,4},{7,5},{8,10},{9,11},{10,... | collective-permute-start | bytes 24584 | tf_op jit(solution)/shard_map/ppermute | solution.py:23
  20.6 0.4 %collective-permute-start.11 = (f32[8,256]{1,0:T(8,128)S(1)}, f32[8,256]{1,0:T(8,128)S(1)}, u32[]{:S(2)}, u32[]{:S(2)}) collective-permute-start(f32[8,256]{1,0:T(8,128)S(1)} %get-tuple-element.21.refs_0_), channel_id=1, source_target_pairs={{0,3},{1,2},{2,1},{3,0},{4,7},{5,6},{6,5},{7,4},{8,11},{9,10},{10,... | collective-permute-start | bytes 24584 | tf_op jit(solution)/shard_map/ppermute | solution.py:23
  21.0 0.7 %collective-permute-start.9 = (f32[8,256]{1,0:T(8,128)S(1)}, f32[8,256]{1,0:T(8,128)S(1)}, u32[]{:S(2)}, u32[]{:S(2)}) collective-permute-start(f32[8,256]{1,0:T(8,128)S(1)} %get-tuple-element.21.refs_0_), channel_id=1, source_target_pairs={{0,1},{1,0},{2,3},{3,2},{4,5},{5,4},{6,7},{7,6},{8,9},{9,8},{10,11... | collective-permute-start | bytes 24584 | tf_op jit(solution)/shard_map/ppermute | solution.py:23
  21.7 0.6 %copy.10 = bf16[4,2048]{1,0:T(4,128)(2,1)} copy(bf16[4,2048]{1,0:T(4,128)(2,1)S(1)} %get-tuple-element.22) | data formatting | bytes 32768
  22.3 0.9 %collective-permute-done.10.refs_2_ = f32[8,256]{1,0:T(8,128)S(1)} collective-permute-done((f32[8,256]{1,0:T(8,128)S(1)}, f32[8,256]{1,0:T(8,128)S(1)}, u32[]{:S(2)}, u32[]{:S(2)}) %collective-permute-start.10) | collective-permute-done | bytes 8224 | tf_op jit(solution)/shard_map/ppermute | solution.py:23
  23.2 0.6 %collective-permute-done.11.refs_3_ = f32[8,256]{1,0:T(8,128)S(1)} collective-permute-done((f32[8,256]{1,0:T(8,128)S(1)}, f32[8,256]{1,0:T(8,128)S(1)}, u32[]{:S(2)}, u32[]{:S(2)}) %collective-permute-start.11) | collective-permute-done | bytes 8224 | tf_op jit(solution)/shard_map/ppermute | solution.py:23
  23.8 0.7 %final_scores.1 = f32[4,32]{1,0:T(4,128)} custom-call(f32[8,256]{1,0:T(8,128)S(1)} %get-tuple-element.21.refs_0_, f32[8,256]{1,0:T(8,128)S(1)} %collective-permute-done.9.refs_1_, f32[8,256]{1,0:T(8,128)S(1)} %collective-permute-done.10.refs_2_, f32[8,256]{1,0:T(8,128)S(1)} %collective-permute-done.11.refs_3_), custom_call_target="tpu_custom_call" | custom-call | tf_op jit(solution)/shard_map/final_scores/pallas_call | solution.py:199
  (22 shorter events, 0.1 us)
Async XLA Ops:
  0.6 0.9 %copy-start.4 = (bf16[32,2048]{1,0:T(8,128)(2,1)S(1)}, bf16[32,2048]{1,0:T(8,128)(2,1)}, u32[]{:S(2)}) copy-start(bf16[32,2048]{1,0:T(8,128)(2,1)} %refs_5_.1) | copy-start | bytes 393220
  0.6 4.9 %copy-start = (bf16[4,144,1280]{2,1,0:T(8,128)(2,1)S(1)}, bf16[4,144,1280]{2,1,0:T(8,128)(2,1)}, u32[]{:S(2)}) copy-start(bf16[4,144,1280]{2,1,0:T(8,128)(2,1)} %param.8) | copy-start | bytes 4423684
  0.7 4.9 %copy-start.1 = (bf16[4,144,1280]{2,1,0:T(8,128)(2,1)S(1)}, bf16[4,144,1280]{2,1,0:T(8,128)(2,1)}, u32[]{:S(2)}) copy-start(bf16[4,144,1280]{2,1,0:T(8,128)(2,1)} %param.9) | copy-start | bytes 4423684
  0.7 4.9 %copy-start.5 = (bf16[2,128,8]{1,2,0:T(8,128)(2,1)S(1)}, bf16[2,128,8]{1,2,0:T(8,128)(2,1)}, u32[]{:S(2)}) copy-start(bf16[2,128,8]{1,2,0:T(8,128)(2,1)} %param.14) | copy-start | bytes 12292
  0.7 4.9 %copy-start.2 = (bf16[128,1280]{1,0:T(8,128)(2,1)S(1)}, bf16[128,1280]{1,0:T(8,128)(2,1)}, u32[]{:S(2)}) copy-start(bf16[128,1280]{1,0:T(8,128)(2,1)} %down.1) | copy-start | bytes 983044
  0.7 4.9 %copy-start.3 = (bf16[1280,128]{1,0:T(8,128)(2,1)S(1)}, bf16[1280,128]{1,0:T(8,128)(2,1)}, u32[]{:S(2)}) copy-start(bf16[1280,128]{1,0:T(8,128)(2,1)} %up.1) | copy-start | bytes 983044
  1.5 10.6 %collective-permute-start.3 = (bf16[32,2048]{1,0:T(8,128)(2,1)S(1)}, bf16[32,2048]{1,0:T(8,128)(2,1)S(1)}, u32[]{:S(2)}, u32[]{:S(2)}) collective-permute-start(bf16[32,2048]{1,0:T(8,128)(2,1)S(1)} %copy-done.4), channel_id=1, source_target_pairs={{0,8},{4,12},{8,0},{12,4},{1,9},{5,13},{9,1},{13,5},{2,10},{6,14},... | collective-permute-start | bytes 393224 | tf_op jit(solution)/shard_map/ppermute | solution.py:23
  5.6 6.5 %copy-start.6 = (s32[4]{0:T(128)S(1)}, s32[4]{0:T(128)}, u32[]{:S(2)}) copy-start(s32[4]{0:T(128)} %refs_4_.3) | copy-start | bytes 52
  5.6 6.5 %copy-start.7 = (bf16[1280,512]{1,0:T(8,128)(2,1)S(1)}, bf16[1280,512]{1,0:T(8,128)(2,1)}, u32[]{:S(2)}) copy-start(bf16[1280,512]{1,0:T(8,128)(2,1)} %refs_7_.1) | copy-start | bytes 3932164
  7.0 1.9 %collective-permute-start = (f32[16,576]{1,0:T(8,128)S(1)}, f32[16,576]{1,0:T(8,128)S(1)}, u32[]{:S(2)}, u32[]{:S(2)}) collective-permute-start(f32[16,576]{1,0:T(8,128)S(1)} %rank_side.1.refs_0_), channel_id=1, source_target_pairs={{0,1},{1,0},{2,3},{3,2},{4,5},{5,4},{6,7},{7,6},{8,9},{9,8},{10,11... | collective-permute-start | bytes 110600 | tf_op jit(solution)/shard_map/ppermute | solution.py:23
  7.0 4.4 %collective-permute-start.1 = (f32[16,576]{1,0:T(8,128)S(1)}, f32[16,576]{1,0:T(8,128)S(1)}, u32[]{:S(2)}, u32[]{:S(2)}) collective-permute-start(f32[16,576]{1,0:T(8,128)S(1)} %rank_side.1.refs_0_), channel_id=1, source_target_pairs={{0,2},{1,3},{2,0},{3,1},{4,6},{5,7},{6,4},{7,5},{8,10},{9,11},{10,... | collective-permute-start | bytes 110600 | tf_op jit(solution)/shard_map/ppermute | solution.py:23
  8.6 3.5 %collective-permute-start.2 = (f32[16,576]{1,0:T(8,128)S(1)}, f32[16,576]{1,0:T(8,128)S(1)}, u32[]{:S(2)}, u32[]{:S(2)}) collective-permute-start(f32[16,576]{1,0:T(8,128)S(1)} %rank_side.1.refs_0_), channel_id=1, source_target_pairs={{0,3},{1,2},{2,1},{3,0},{4,7},{5,6},{6,5},{7,4},{8,11},{9,10},{10,... | collective-permute-start | bytes 110600 | tf_op jit(solution)/shard_map/ppermute | solution.py:23
  8.9 9.6 %collective-permute-start.7 = (bf16[32,2048]{1,0:T(8,128)(2,1)S(1)}, bf16[32,2048]{1,0:T(8,128)(2,1)S(1)}, u32[]{:S(2)}, u32[]{:S(2)}) collective-permute-start(bf16[32,2048]{1,0:T(8,128)(2,1)S(1)} %copy-done.4), channel_id=1, source_target_pairs={{0,4},{4,0},{8,12},{12,8},{1,5},{5,1},{9,13},{13,9},{2,6},{6,2},{1... | collective-permute-start | bytes 393224 | tf_op jit(solution)/shard_map/ppermute | solution.py:23
  10.5 8.0 %collective-permute-start.8 = (bf16[32,2048]{1,0:T(8,128)(2,1)S(1)}, bf16[32,2048]{1,0:T(8,128)(2,1)S(1)}, u32[]{:S(2)}, u32[]{:S(2)}) collective-permute-start(bf16[32,2048]{1,0:T(8,128)(2,1)S(1)} %copy-done.4), channel_id=1, source_target_pairs={{0,12},{4,8},{8,4},{12,0},{1,13},{5,9},{9,5},{13,1},{2,14},{6,10},... | collective-permute-start | bytes 393224 | tf_op jit(solution)/shard_map/ppermute | solution.py:23
  13.5 1.9 %collective-permute-start.4 = (f32[64,128]{1,0:T(8,128)S(1)}, f32[64,128]{1,0:T(8,128)S(1)}, u32[]{:S(2)}, u32[]{:S(2)}) collective-permute-start(f32[64,128]{1,0:T(8,128)S(1)} %get-tuple-element.16), channel_id=1, source_target_pairs={{0,1},{1,0},{2,3},{3,2},{4,5},{5,4},{6,7},{7,6},{8,9},{9,8},{10,11... | collective-permute-start | bytes 98312 | tf_op jit(solution)/shard_map/ppermute | solution.py:23
  13.8 3.9 %collective-permute-start.5 = (f32[64,128]{1,0:T(8,128)S(1)}, f32[64,128]{1,0:T(8,128)S(1)}, u32[]{:S(2)}, u32[]{:S(2)}) collective-permute-start(f32[64,128]{1,0:T(8,128)S(1)} %get-tuple-element.17), channel_id=1, source_target_pairs={{0,2},{1,3},{2,0},{3,1},{4,6},{5,7},{6,4},{7,5},{8,10},{9,11},{10,... | collective-permute-start | bytes 98312 | tf_op jit(solution)/shard_map/ppermute | solution.py:23
  15.1 3.4 %collective-permute-start.6 = (f32[64,128]{1,0:T(8,128)S(1)}, f32[64,128]{1,0:T(8,128)S(1)}, u32[]{:S(2)}, u32[]{:S(2)}) collective-permute-start(f32[64,128]{1,0:T(8,128)S(1)} %get-tuple-element.18), channel_id=1, source_target_pairs={{0,3},{1,2},{2,1},{3,0},{4,7},{5,6},{6,5},{7,4},{8,11},{9,10},{10,... | collective-permute-start | bytes 98312 | tf_op jit(solution)/shard_map/ppermute | solution.py:23
  19.5 3.7 %collective-permute-start.10 = (f32[8,256]{1,0:T(8,128)S(1)}, f32[8,256]{1,0:T(8,128)S(1)}, u32[]{:S(2)}, u32[]{:S(2)}) collective-permute-start(f32[8,256]{1,0:T(8,128)S(1)} %get-tuple-element.21.refs_0_), channel_id=1, source_target_pairs={{0,2},{1,3},{2,0},{3,1},{4,6},{5,7},{6,4},{7,5},{8,10},{9,11},{10,... | collective-permute-start | bytes 24584 | tf_op jit(solution)/shard_map/ppermute | solution.py:23
  20.6 3.1 %collective-permute-start.11 = (f32[8,256]{1,0:T(8,128)S(1)}, f32[8,256]{1,0:T(8,128)S(1)}, u32[]{:S(2)}, u32[]{:S(2)}) collective-permute-start(f32[8,256]{1,0:T(8,128)S(1)} %get-tuple-element.21.refs_0_), channel_id=1, source_target_pairs={{0,3},{1,2},{2,1},{3,0},{4,7},{5,6},{6,5},{7,4},{8,11},{9,10},{10,... | collective-permute-start | bytes 24584 | tf_op jit(solution)/shard_map/ppermute | solution.py:23
  21.0 2.8 %collective-permute-start.9 = (f32[8,256]{1,0:T(8,128)S(1)}, f32[8,256]{1,0:T(8,128)S(1)}, u32[]{:S(2)}, u32[]{:S(2)}) collective-permute-start(f32[8,256]{1,0:T(8,128)S(1)} %get-tuple-element.21.refs_0_), channel_id=1, source_target_pairs={{0,1},{1,0},{2,3},{3,2},{4,5},{5,4},{6,7},{7,6},{8,9},{9,8},{10,11... | collective-permute-start | bytes 24584 | tf_op jit(solution)/shard_map/ppermute | solution.py:23

commit v6 on v5

--- a/solution.py
+++ b/solution.py
@@ -41,9 +41,9 @@
 def opening():
     return pl.pallas_call(
         open_kernel,
-        out_shape=jax.ShapeDtypeStruct((8, LANES), F32),
+        out_shape=pltpu.VMEM((8, LANES), F32),
         out_specs=VMEM,
-        compiler_params=PARAMS,
+        compiler_params=pltpu.CompilerParams(vmem_limit_bytes=63400000),
         cost_estimate=pl.CostEstimate(flops=20_000_000_000, bytes_accessed=400_000_000, transcendentals=0),
         name="opening",
     )()
@@ -71,7 +71,7 @@
     return pl.pallas_call(
         rank_kernel,
         out_shape=jax.ShapeDtypeStruct((2 * sketch.shape[1], rows), F32),
-        in_specs=[VMEM] * 5 + [HBM],
+        in_specs=[VMEM] * 5 + [pl.BlockSpec(memory_space=pl.ANY)],
         out_specs=VMEM,
         compiler_params=PARAMS,
         name="rank_side",
@@ -79,16 +79,16 @@
 
 
 def sums_kernel(n_proj, seq_len, k2, *refs):
-    rights, (lengths, acts, cots, width, _, *outs, parted) = refs[:n_proj], refs[n_proj:]
+    rights, (lengths, acts, cots, width, *outs, parted) = refs[:n_proj], refs[n_proj:]
     right = sum([r[...] for r in rights[1:]], rights[0][...])
-    ex_dev, rows = lengths.shape[0], acts.shape[0]
+    ex_dev, rows = lengths.shape[1], acts.shape[0]
     t = lax.broadcasted_iota(jnp.int32, (k2, rows), 1)
     wide = []
     for p, keep in enumerate((cots, acts)):
         own = right[p * k2 : (p + 1) * k2]
         own = own.astype(BF16).astype(F32)
         spread = [
-            jnp.where((t >= e * seq_len) & (t < e * seq_len + lengths[e]), own, 0.0) for e in range(ex_dev)
+            jnp.where((t >= e * seq_len) & (t < e * seq_len + lengths[:, e : e + 1]), own, 0.0) for e in range(ex_dev)
         ]
         wide.append(dot(jnp.concatenate(spread, axis=0).astype(BF16), keep[...]))
     both = [wide[p][e * k2 : (e + 1) * k2] for e in range(ex_dev) for p in range(2)]
@@ -98,34 +98,34 @@
         parted[s] = total[:, s * k_own : (s + 1) * k_own]
     me = lax.axis_index("proj")
     for m in range(n_proj):
-        outs[m][...] = parted[me ^ m]
-
-
-def token_sums(rights, lengths, acts, cots, width, seq_len, k2, early):
+        outs[m][...] = parted[me ^ m].astype(BF16)
+
+
+def token_sums(rights, lengths, acts, cots, width, seq_len, k2):
     n_proj = len(rights)
-    ex_dev = lengths.shape[0]
+    ex_dev = lengths.shape[1]
     shape = (ex_dev * 2 * k2, width.shape[1] // n_proj)
     return pl.pallas_call(
         functools.partial(sums_kernel, n_proj, seq_len, k2),
-        out_shape=[jax.ShapeDtypeStruct(shape, F32)] * n_proj,
-        in_specs=[VMEM] * n_proj + [SMEM] + [VMEM] * 3 + [HBM],
+        out_shape=[jax.ShapeDtypeStruct(shape, BF16)] * n_proj,
+        in_specs=[VMEM] * n_proj + [VMEM] + [VMEM] * 3,
         out_specs=[VMEM] * n_proj,
         scratch_shapes=[pltpu.VMEM((n_proj,) + shape, F32)],
         compiler_params=PARAMS,
         name="token_sums",
         cost_estimate=pl.CostEstimate(flops=20000000000, bytes_accessed=400000000, transcendentals=0),
-    )(*rights, lengths, acts, cots, width, early)
+    )(*rights, lengths, acts, cots, width)
 
 
 def dots_kernel(n_proj, r, *refs):
     pieces, lengths, blocks = refs[:n_proj], refs[n_proj], refs[n_proj + 1 : -4]
     train, note, turned, lined = refs[-4:]
-    ex_dev = lengths.shape[0]
+    ex_dev = lengths.shape[1]
     k_own = pieces[0].shape[1]
     low = LANES // r
     high = k_own // low
-    total = sum([piece[...] for piece in pieces[1:]], pieces[0][...])
-    scaled = [total[e * r : (e + 1) * r] / lengths[e].astype(F32) for e in range(ex_dev)]
+    total = sum([piece[...].astype(F32) for piece in pieces[1:]], pieces[0][...].astype(F32))
+    scaled = [total[e * r : (e + 1) * r] / lengths[:, e : e + 1].astype(F32) for e in range(ex_dev)]
     turned[:, : ex_dev * r] = jnp.concatenate(scaled, axis=0).T
     lane = lax.broadcasted_iota(jnp.int32, (high, LANES), 1)
     lines = [jnp.zeros((high, LANES), F32)] * ex_dev
@@ -162,7 +162,7 @@
 
 
 def partial_dots(pieces, lengths, blocks, r):
-    n_proj, ex_dev = len(pieces), lengths.shape[0]
+    n_proj, ex_dev = len(pieces), lengths.shape[1]
     k_own = pieces[0].shape[1]
     n_val = sum(block.shape[0] for block in blocks)
     high = k_own * r // LANES
@@ -172,7 +172,7 @@
             pltpu.VMEM((ex_dev, k_own * r), BF16),
             jax.ShapeDtypeStruct((2 * ex_dev, n_val + LANES), F32),
         ),
-        in_specs=[VMEM] * n_proj + [SMEM] + [VMEM] * len(blocks),
+        in_specs=[VMEM] * n_proj + [VMEM] + [VMEM] * len(blocks),
         out_specs=(VMEM, VMEM),
         scratch_shapes=[pltpu.VMEM((k_own, LANES), F32), pltpu.VMEM((high * ex_dev, LANES), F32)],
         compiler_params=PARAMS,
@@ -220,6 +220,7 @@
     rows = ex_dev * seq_len
     k1, k2 = width_side_sketch.shape[1], rank_side_sketch.shape[2]
     n_proj, n_ex = lax.axis_size("proj"), lax.axis_size("ex")
+    lengths = lengths.reshape(1, ex_dev)
     acts = inputs.reshape(rows, model_cols)
     cots = cotangents.reshape(rows, model_cols)
 
@@ -237,10 +238,9 @@
     )
     rights = [right] + [swap(right, "proj", m) for m in range(1, n_proj)]
     if by_mask:
-        later, rights[1] = lax.optimization_barrier((heldout_gradient_rows, rights[1]))
-        blocks[3] = swap(later, "ex", 3)
-        blocks[1] = swap(later, "ex", 1)
-    pieces = token_sums(rights, lengths, acts, cots, width_side_sketch, seq_len, k2, blocks[min(2, len(blocks) - 1)])
+        blocks[1] = swap(heldout_gradient_rows, "ex", 1)
+        blocks[3] = swap(blocks[2], "ex", 1)
+    pieces = token_sums(rights, lengths, acts, cots, width_side_sketch, seq_len, k2)
     pieces = [pieces[0]] + [swap(pieces[m], "proj", m) for m in range(1, n_proj)]
     train_proj, note = partial_dots(pieces, lengths, blocks, 2 * k2)
     notes = [note] + [swap(note, "proj", m) for m in range(1, n_proj)]

time: 24.6 us -> 23.4 us (0.951)
  waiting for transfers between devices: 5.15 us -> 6.14 us
  Pallas kernels: 4.49 us -> 3.55 us
  local copies, waits for them, and re-layouts: 1.48 us -> 0.64 us
  starting transfers between devices: 12.6 us -> 12.2 us
    ppermute x12, waiting for transfers between devices: 5.15 us -> 6.14 us  [swap(): return lax.ppermute(x, axis, [(i, i ^ mask) for i in range(size)])]
    unnamed x17, local copies, waits for them, and re-layouts: 1.48 us -> 0.64 us
    pallas_call x1, Pallas kernels: 1.41 us -> 0.9 us  [token_sums(): pl.pallas_call(functools.partial(sums_kernel, n_proj, seq_len, k2), out_s...]
    ppermute x12, starting transfers between devices: 12.6 us -> 12.2 us  [swap(): return lax.ppermute(x, axis, [(i, i ^ mask) for i in range(size)])]
    pallas_call x1, Pallas kernels: 1 us -> 0.56 us  [partial_dots(): pl.pallas_call(functools.partial(dots_kernel, n_proj, r), out_shape=(pltp...]
  transfers between devices with their start and end apart: 12 -> 12, of which waited for: 5 -> 5; matrix products, arithmetic and copies ran while one was open for 2% -> 3% of each run, Pallas kernels for 11% -> 10%
where the time goes in v6:
time: 23.4 us; the launch traced here: 23.3 us
  starting transfers between devices  12.2 us (52%)
  waiting for transfers between devices  6.14 us (26%)
  Pallas kernels  3.55 us (15%)
  between operations  0.76 us (3%)
  local copies, waits for them, and re-layouts  0.64 us (3%)
    ppermute x12, starting transfers between devices, swap(): return lax.ppermute(x, axis, [(i, i ^ mask) for i in range(size)])  12.2 us
    ppermute x12, waiting for transfers between devices, swap(): return lax.ppermute(x, axis, [(i, i ^ mask) for i in range(size)])  6.14 us
    pallas_call x1, Pallas kernels, rank_side(): pl.pallas_call(rank_kernel, out_shape=jax.ShapeDtypeStruct((2 * sketch.sh...  1.36 us
    pallas_call x1, Pallas kernels, token_sums(): pl.pallas_call(functools.partial(sums_kernel, n_proj, seq_len, k2), out_s...  0.9 us
    pallas_call x1, Pallas kernels, final_scores(): pl.pallas_call(functools.partial(scores_kernel, len(notes), ex_dev, scale...  0.73 us
    unnamed x17, local copies, waits for them, and re-layouts  0.64 us
    pallas_call x1, Pallas kernels, partial_dots(): pl.pallas_call(functools.partial(dots_kernel, n_proj, r), out_shape=(pltp...  0.56 us
  transfers between devices with their start and end apart: 12, of which 5 were waited for; matrix products, arithmetic and copies ran while one was open for 3% of the time, Pallas kernels for 10%

profile of v6, /device:TPU:0, one launch (start us, length us, event | category | flops | bytes accessed | tf_op | source)
XLA Modules:
  0.0 23.3 jit_solution(13141994026944395785)
XLA Ops:
  0.7 4.1 %collective-permute-start.7 = (bf16[32,2048]{1,0:T(8,128)(2,1)}, bf16[32,2048]{1,0:T(8,128)(2,1)S(1)}, u32[]{:S(2)}, u32[]{:S(2)}) collective-permute-start(bf16[32,2048]{1,0:T(8,128)(2,1)} %refs_5_.1), channel_id=1, source_target_pairs={{0,8},{4,12},{8,0},{12,4},{1,9},{5,13},{9,1},{13,5},{2,10},{6,14},... | collective-permute-start | bytes 393224 | tf_op jit(solution)/shard_map/ppermute | solution.py:23
  4.8 0.0 copy-start.6
  4.8 0.0 copy-start.7
  4.8 1.4 %rank_side.1.refs_0_ = f32[16,576]{1,0:T(8,128)S(1)} custom-call(bf16[576,1280]{1,0:T(8,128)(2,1)S(1)} %bitcast.4, bf16[576,1280]{1,0:T(8,128)(2,1)S(1)} %bitcast.6, bf16[128,1280]{1,0:T(8,128)(2,1)S(1)} %copy-done.2, bf16[1280,128]{1,0:T(8,128)(2,1)S(1)} %copy-done.3, bf16[2,8,128]{2,1,0:T(8,128)(2,1)S(1)} %bitcast.8, f32[8,128]{1,0:T(8,128)S(1)} %opening.1._), custom_call_target="tpu_custom_call" | custom-call | tf_op jit(solution)/shard_map/rank_side/pallas_call | solution.py:71
  6.2 0.7 %collective-permute-start.2 = (f32[16,576]{1,0:T(8,128)S(1)}, f32[16,576]{1,0:T(8,128)S(1)}, u32[]{:S(2)}, u32[]{:S(2)}) collective-permute-start(f32[16,576]{1,0:T(8,128)S(1)} %rank_side.1.refs_0_), channel_id=1, source_target_pairs={{0,3},{1,2},{2,1},{3,0},{4,7},{5,6},{6,5},{7,4},{8,11},{9,10},{10,... | collective-permute-start | bytes 110600 | tf_op jit(solution)/shard_map/ppermute | solution.py:23
  6.9 0.9 %collective-permute-start.1 = (f32[16,576]{1,0:T(8,128)S(1)}, f32[16,576]{1,0:T(8,128)S(1)}, u32[]{:S(2)}, u32[]{:S(2)}) collective-permute-start(f32[16,576]{1,0:T(8,128)S(1)} %rank_side.1.refs_0_), channel_id=1, source_target_pairs={{0,2},{1,3},{2,0},{3,1},{4,6},{5,7},{6,4},{7,5},{8,10},{9,11},{10,... | collective-permute-start | bytes 110600 | tf_op jit(solution)/shard_map/ppermute | solution.py:23
  7.8 0.3 %collective-permute-start = (f32[16,576]{1,0:T(8,128)S(1)}, f32[16,576]{1,0:T(8,128)S(1)}, u32[]{:S(2)}, u32[]{:S(2)}) collective-permute-start(f32[16,576]{1,0:T(8,128)S(1)} %rank_side.1.refs_0_), channel_id=1, source_target_pairs={{0,1},{1,0},{2,3},{3,2},{4,5},{5,4},{6,7},{7,6},{8,9},{9,8},{10,11... | collective-permute-start | bytes 110600 | tf_op jit(solution)/shard_map/ppermute | solution.py:23
  8.1 1.6 %collective-permute-start.6 = (bf16[32,2048]{1,0:T(8,128)(2,1)S(1)}, bf16[32,2048]{1,0:T(8,128)(2,1)S(1)}, u32[]{:S(2)}, u32[]{:S(2)}) collective-permute-start(bf16[32,2048]{1,0:T(8,128)(2,1)S(1)} %copy-done.4), channel_id=1, source_target_pairs={{0,4},{4,0},{8,12},{12,8},{1,5},{5,1},{9,13},{13,9},{2,6},{6,2},{1... | collective-permute-start | bytes 393224 | tf_op jit(solution)/shard_map/ppermute | solution.py:23
  9.7 1.7 %collective-permute-done.7.refs_7_ = bf16[32,2048]{1,0:T(8,128)(2,1)S(1)} collective-permute-done((bf16[32,2048]{1,0:T(8,128)(2,1)}, bf16[32,2048]{1,0:T(8,128)(2,1)S(1)}, u32[]{:S(2)}, u32[]{:S(2)}) %collective-permute-start.7) | collective-permute-done | bytes 131104 | tf_op jit(solution)/shard_map/ppermute | solution.py:23
  11.3 0.8 %collective-permute-start.8 = (bf16[32,2048]{1,0:T(8,128)(2,1)S(1)}, bf16[32,2048]{1,0:T(8,128)(2,1)S(1)}, u32[]{:S(2)}, u32[]{:S(2)}) collective-permute-start(bf16[32,2048]{1,0:T(8,128)(2,1)S(1)} %collective-permute-done.7.refs_7_), channel_id=1, source_target_pairs={{0,4},{4,0},{8,12},{12,8},{1,5},{5,1},{9,13},{13,9},{2,6},{6,2},{1... | collective-permute-start | bytes 393224 | tf_op jit(solution)/shard_map/ppermute | solution.py:23
  12.2 0.9 %token_sums.1 = (bf16[64,128]{1,0:T(8,128)(2,1)S(1)}, bf16[64,128]{1,0:T(8,128)(2,1)S(1)}, bf16[64,128]{1,0:T(8,128)(2,1)S(1)}, bf16[64,128]{1,0:T(8,128)(2,1)S(1)}) custom-call(f32[16,576]{1,0:T(8,128)S(1)} %rank_side.1.refs_0_, f32[16,576]{1,0:T(8,128)S(1)} %collective-permute-done.refs_1_, f32[16,576]{1,0:T(8,128)S(1)} %collective-permute-done.1.refs_2_, ...), custom_call_target="tpu_custom_call" | custom-call | flops 20000000000 | bytes 400000000 | tf_op jit(solution)/shard_map/token_sums/pallas_call | solution.py:108
  13.1 0.1 collective-permute-start.3
  13.2 1.6 %collective-permute-start.4 = (bf16[64,128]{1,0:T(8,128)(2,1)S(1)}, bf16[64,128]{1,0:T(8,128)(2,1)S(1)}, u32[]{:S(2)}, u32[]{:S(2)}) collective-permute-start(bf16[64,128]{1,0:T(8,128)(2,1)S(1)} %get-tuple-element.13), channel_id=1, source_target_pairs={{0,2},{1,3},{2,0},{3,1},{4,6},{5,7},{6,4},{7,5},{8,10},{9,11},{10,... | collective-permute-start | bytes 49160 | tf_op jit(solution)/shard_map/ppermute | solution.py:23
  14.7 0.3 %collective-permute-start.5 = (bf16[64,128]{1,0:T(8,128)(2,1)S(1)}, bf16[64,128]{1,0:T(8,128)(2,1)S(1)}, u32[]{:S(2)}, u32[]{:S(2)}) collective-permute-start(bf16[64,128]{1,0:T(8,128)(2,1)S(1)} %get-tuple-element.14), channel_id=1, source_target_pairs={{0,3},{1,2},{2,1},{3,0},{4,7},{5,6},{6,5},{7,4},{8,11},{9,10},{10,... | collective-permute-start | bytes 49160 | tf_op jit(solution)/shard_map/ppermute | solution.py:23
  15.0 1.9 %collective-permute-done.4.refs_2_ = bf16[64,128]{1,0:T(8,128)(2,1)S(1)} collective-permute-done((bf16[64,128]{1,0:T(8,128)(2,1)S(1)}, bf16[64,128]{1,0:T(8,128)(2,1)S(1)}, u32[]{:S(2)}, u32[]{:S(2)}) %collective-permute-start.4) | collective-permute-done | bytes 16416 | tf_op jit(solution)/shard_map/ppermute | solution.py:23
  17.0 0.9 %collective-permute-done.5.refs_3_ = bf16[64,128]{1,0:T(8,128)(2,1)S(1)} collective-permute-done((bf16[64,128]{1,0:T(8,128)(2,1)S(1)}, bf16[64,128]{1,0:T(8,128)(2,1)S(1)}, u32[]{:S(2)}, u32[]{:S(2)}) %collective-permute-start.5) | collective-permute-done | bytes 16416 | tf_op jit(solution)/shard_map/ppermute | solution.py:23
  17.9 0.6 %partial_dots.1 = (bf16[4,2048]{1,0:T(4,128)(2,1)S(1)}, f32[8,256]{1,0:T(8,128)S(1)}) custom-call(bf16[64,128]{1,0:T(8,128)(2,1)S(1)} %get-tuple-element.11.refs_0_, bf16[64,128]{1,0:T(8,128)(2,1)S(1)} %collective-permute-done.3.refs_1_, bf16[64,128]{1,0:T(8,128)(2,1)S(1)} %collective-permute-done.4.refs_2_, ...), custom_call_target="tpu_custom_call" | custom-call | tf_op jit(solution)/shard_map/partial_dots/pallas_call | solution.py:169
  18.4 0.4 %collective-permute-start.11 = (f32[8,256]{1,0:T(8,128)S(1)}, f32[8,256]{1,0:T(8,128)S(1)}, u32[]{:S(2)}, u32[]{:S(2)}) collective-permute-start(f32[8,256]{1,0:T(8,128)S(1)} %get-tuple-element.17.refs_0_), channel_id=1, source_target_pairs={{0,3},{1,2},{2,1},{3,0},{4,7},{5,6},{6,5},{7,4},{8,11},{9,10},{10,... | collective-permute-start | bytes 24584 | tf_op jit(solution)/shard_map/ppermute | solution.py:23
  18.9 1.4 %collective-permute-start.10 = (f32[8,256]{1,0:T(8,128)S(1)}, f32[8,256]{1,0:T(8,128)S(1)}, u32[]{:S(2)}, u32[]{:S(2)}) collective-permute-start(f32[8,256]{1,0:T(8,128)S(1)} %get-tuple-element.17.refs_0_), channel_id=1, source_target_pairs={{0,2},{1,3},{2,0},{3,1},{4,6},{5,7},{6,4},{7,5},{8,10},{9,11},{10,... | collective-permute-start | bytes 24584 | tf_op jit(solution)/shard_map/ppermute | solution.py:23
  20.3 0.1 collective-permute-start.9
  20.3 0.6 %copy.10 = bf16[4,2048]{1,0:T(4,128)(2,1)} copy(bf16[4,2048]{1,0:T(4,128)(2,1)S(1)} %get-tuple-element.18) | data formatting | bytes 32768
  20.9 0.6 %collective-permute-done.11.refs_3_ = f32[8,256]{1,0:T(8,128)S(1)} collective-permute-done((f32[8,256]{1,0:T(8,128)S(1)}, f32[8,256]{1,0:T(8,128)S(1)}, u32[]{:S(2)}, u32[]{:S(2)}) %collective-permute-start.11) | collective-permute-done | bytes 8224 | tf_op jit(solution)/shard_map/ppermute | solution.py:23
  21.5 1.0 %collective-permute-done.10.refs_2_ = f32[8,256]{1,0:T(8,128)S(1)} collective-permute-done((f32[8,256]{1,0:T(8,128)S(1)}, f32[8,256]{1,0:T(8,128)S(1)}, u32[]{:S(2)}, u32[]{:S(2)}) %collective-permute-start.10) | collective-permute-done | bytes 8224 | tf_op jit(solution)/shard_map/ppermute | solution.py:23
  22.5 0.7 %final_scores.1 = f32[4,32]{1,0:T(4,128)} custom-call(f32[8,256]{1,0:T(8,128)S(1)} %get-tuple-element.17.refs_0_, f32[8,256]{1,0:T(8,128)S(1)} %collective-permute-done.9.refs_1_, f32[8,256]{1,0:T(8,128)S(1)} %collective-permute-done.10.refs_2_, f32[8,256]{1,0:T(8,128)S(1)} %collective-permute-done.11.refs_3_), custom_call_target="tpu_custom_call" | custom-call | tf_op jit(solution)/shard_map/final_scores/pallas_call | solution.py:199
  (22 shorter events, 0.1 us)
Async XLA Ops:
  0.6 4.2 %copy-start.5 = (bf16[2,128,8]{1,2,0:T(8,128)(2,1)S(1)}, bf16[2,128,8]{1,2,0:T(8,128)(2,1)}, u32[]{:S(2)}) copy-start(bf16[2,128,8]{1,2,0:T(8,128)(2,1)} %param.14) | copy-start | bytes 12292
  0.6 4.2 %copy-start.3 = (bf16[1280,128]{1,0:T(8,128)(2,1)S(1)}, bf16[1280,128]{1,0:T(8,128)(2,1)}, u32[]{:S(2)}) copy-start(bf16[1280,128]{1,0:T(8,128)(2,1)} %up.1) | copy-start | bytes 983044
  0.7 4.1 %copy-start.2 = (bf16[128,1280]{1,0:T(8,128)(2,1)S(1)}, bf16[128,1280]{1,0:T(8,128)(2,1)}, u32[]{:S(2)}) copy-start(bf16[128,1280]{1,0:T(8,128)(2,1)} %down.1) | copy-start | bytes 983044
  0.7 4.1 %copy-start.1 = (bf16[4,144,1280]{2,1,0:T(8,128)(2,1)S(1)}, bf16[4,144,1280]{2,1,0:T(8,128)(2,1)}, u32[]{:S(2)}) copy-start(bf16[4,144,1280]{2,1,0:T(8,128)(2,1)} %param.9) | copy-start | bytes 4423684
  0.7 4.1 %copy-start = (bf16[4,144,1280]{2,1,0:T(8,128)(2,1)S(1)}, bf16[4,144,1280]{2,1,0:T(8,128)(2,1)}, u32[]{:S(2)}) copy-start(bf16[4,144,1280]{2,1,0:T(8,128)(2,1)} %param.8) | copy-start | bytes 4423684
  0.7 10.7 %collective-permute-start.7 = (bf16[32,2048]{1,0:T(8,128)(2,1)}, bf16[32,2048]{1,0:T(8,128)(2,1)S(1)}, u32[]{:S(2)}, u32[]{:S(2)}) collective-permute-start(bf16[32,2048]{1,0:T(8,128)(2,1)} %refs_5_.1), channel_id=1, source_target_pairs={{0,8},{4,12},{8,0},{12,4},{1,9},{5,13},{9,1},{13,5},{2,10},{6,14},... | collective-permute-start | bytes 393224 | tf_op jit(solution)/shard_map/ppermute | solution.py:23
  4.8 3.3 %copy-start.4 = (bf16[32,2048]{1,0:T(8,128)(2,1)S(1)}, bf16[32,2048]{1,0:T(8,128)(2,1)}, u32[]{:S(2)}) copy-start(bf16[32,2048]{1,0:T(8,128)(2,1)} %refs_5_.1) | copy-start | bytes 393220
  4.8 7.3 %copy-start.6 = (s32[4]{0:T(128)S(1)}, s32[4]{0:T(128)}, u32[]{:S(2)}) copy-start(s32[4]{0:T(128)} %param.10) | copy-start | bytes 52
  4.8 7.3 %copy-start.7 = (bf16[1280,512]{1,0:T(8,128)(2,1)S(1)}, bf16[1280,512]{1,0:T(8,128)(2,1)}, u32[]{:S(2)}) copy-start(bf16[1280,512]{1,0:T(8,128)(2,1)} %refs_7_.1) | copy-start | bytes 3932164
  6.2 5.9 %collective-permute-start.2 = (f32[16,576]{1,0:T(8,128)S(1)}, f32[16,576]{1,0:T(8,128)S(1)}, u32[]{:S(2)}, u32[]{:S(2)}) collective-permute-start(f32[16,576]{1,0:T(8,128)S(1)} %rank_side.1.refs_0_), channel_id=1, source_target_pairs={{0,3},{1,2},{2,1},{3,0},{4,7},{5,6},{6,5},{7,4},{8,11},{9,10},{10,... | collective-permute-start | bytes 110600 | tf_op jit(solution)/shard_map/ppermute | solution.py:23
  6.9 5.2 %collective-permute-start.1 = (f32[16,576]{1,0:T(8,128)S(1)}, f32[16,576]{1,0:T(8,128)S(1)}, u32[]{:S(2)}, u32[]{:S(2)}) collective-permute-start(f32[16,576]{1,0:T(8,128)S(1)} %rank_side.1.refs_0_), channel_id=1, source_target_pairs={{0,2},{1,3},{2,0},{3,1},{4,6},{5,7},{6,4},{7,5},{8,10},{9,11},{10,... | collective-permute-start | bytes 110600 | tf_op jit(solution)/shard_map/ppermute | solution.py:23
  7.8 4.3 %collective-permute-start = (f32[16,576]{1,0:T(8,128)S(1)}, f32[16,576]{1,0:T(8,128)S(1)}, u32[]{:S(2)}, u32[]{:S(2)}) collective-permute-start(f32[16,576]{1,0:T(8,128)S(1)} %rank_side.1.refs_0_), channel_id=1, source_target_pairs={{0,1},{1,0},{2,3},{3,2},{4,5},{5,4},{6,7},{7,6},{8,9},{9,8},{10,11... | collective-permute-start | bytes 110600 | tf_op jit(solution)/shard_map/ppermute | solution.py:23
  8.1 9.8 %collective-permute-start.6 = (bf16[32,2048]{1,0:T(8,128)(2,1)S(1)}, bf16[32,2048]{1,0:T(8,128)(2,1)S(1)}, u32[]{:S(2)}, u32[]{:S(2)}) collective-permute-start(bf16[32,2048]{1,0:T(8,128)(2,1)S(1)} %copy-done.4), channel_id=1, source_target_pairs={{0,4},{4,0},{8,12},{12,8},{1,5},{5,1},{9,13},{13,9},{2,6},{6,2},{1... | collective-permute-start | bytes 393224 | tf_op jit(solution)/shard_map/ppermute | solution.py:23
  11.3 6.5 %collective-permute-start.8 = (bf16[32,2048]{1,0:T(8,128)(2,1)S(1)}, bf16[32,2048]{1,0:T(8,128)(2,1)S(1)}, u32[]{:S(2)}, u32[]{:S(2)}) collective-permute-start(bf16[32,2048]{1,0:T(8,128)(2,1)S(1)} %collective-permute-done.7.refs_7_), channel_id=1, source_target_pairs={{0,4},{4,0},{8,12},{12,8},{1,5},{5,1},{9,13},{13,9},{2,6},{6,2},{1... | collective-permute-start | bytes 393224 | tf_op jit(solution)/shard_map/ppermute | solution.py:23
  13.1 1.9 %collective-permute-start.3 = (bf16[64,128]{1,0:T(8,128)(2,1)S(1)}, bf16[64,128]{1,0:T(8,128)(2,1)S(1)}, u32[]{:S(2)}, u32[]{:S(2)}) collective-permute-start(bf16[64,128]{1,0:T(8,128)(2,1)S(1)} %get-tuple-element.12), channel_id=1, source_target_pairs={{0,1},{1,0},{2,3},{3,2},{4,5},{5,4},{6,7},{7,6},{8,9},{9,8},{10,11... | collective-permute-start | bytes 49160 | tf_op jit(solution)/shard_map/ppermute | solution.py:23
  13.2 3.8 %collective-permute-start.4 = (bf16[64,128]{1,0:T(8,128)(2,1)S(1)}, bf16[64,128]{1,0:T(8,128)(2,1)S(1)}, u32[]{:S(2)}, u32[]{:S(2)}) collective-permute-start(bf16[64,128]{1,0:T(8,128)(2,1)S(1)} %get-tuple-element.13), channel_id=1, source_target_pairs={{0,2},{1,3},{2,0},{3,1},{4,6},{5,7},{6,4},{7,5},{8,10},{9,11},{10,... | collective-permute-start | bytes 49160 | tf_op jit(solution)/shard_map/ppermute | solution.py:23
  14.7 3.2 %collective-permute-start.5 = (bf16[64,128]{1,0:T(8,128)(2,1)S(1)}, bf16[64,128]{1,0:T(8,128)(2,1)S(1)}, u32[]{:S(2)}, u32[]{:S(2)}) collective-permute-start(bf16[64,128]{1,0:T(8,128)(2,1)S(1)} %get-tuple-element.14), channel_id=1, source_target_pairs={{0,3},{1,2},{2,1},{3,0},{4,7},{5,6},{6,5},{7,4},{8,11},{9,10},{10,... | collective-permute-start | bytes 49160 | tf_op jit(solution)/shard_map/ppermute | solution.py:23
  18.4 3.1 %collective-permute-start.11 = (f32[8,256]{1,0:T(8,128)S(1)}, f32[8,256]{1,0:T(8,128)S(1)}, u32[]{:S(2)}, u32[]{:S(2)}) collective-permute-start(f32[8,256]{1,0:T(8,128)S(1)} %get-tuple-element.17.refs_0_), channel_id=1, source_target_pairs={{0,3},{1,2},{2,1},{3,0},{4,7},{5,6},{6,5},{7,4},{8,11},{9,10},{10,... | collective-permute-start | bytes 24584 | tf_op jit(solution)/shard_map/ppermute | solution.py:23
  18.9 3.7 %collective-permute-start.10 = (f32[8,256]{1,0:T(8,128)S(1)}, f32[8,256]{1,0:T(8,128)S(1)}, u32[]{:S(2)}, u32[]{:S(2)}) collective-permute-start(f32[8,256]{1,0:T(8,128)S(1)} %get-tuple-element.17.refs_0_), channel_id=1, source_target_pairs={{0,2},{1,3},{2,0},{3,1},{4,6},{5,7},{6,4},{7,5},{8,10},{9,11},{10,... | collective-permute-start | bytes 24584 | tf_op jit(solution)/shard_map/ppermute | solution.py:23
  20.3 2.3 %collective-permute-start.9 = (f32[8,256]{1,0:T(8,128)S(1)}, f32[8,256]{1,0:T(8,128)S(1)}, u32[]{:S(2)}, u32[]{:S(2)}) collective-permute-start(f32[8,256]{1,0:T(8,128)S(1)} %get-tuple-element.17.refs_0_), channel_id=1, source_target_pairs={{0,1},{1,0},{2,3},{3,2},{4,5},{5,4},{6,7},{7,6},{8,9},{9,8},{10,11... | collective-permute-start | bytes 24584 | tf_op jit(solution)/shard_map/ppermute | solution.py:23

commit v7 on v6

--- a/solution.py
+++ b/solution.py
@@ -10,11 +10,11 @@
 
 epsilon = 1e-06
 LANES = 128
+PLANES = 4
 F32, BF16 = jnp.float32, jnp.bfloat16
 NT = (((1,), (1,)), ((), ()))
 HBM = pl.BlockSpec(memory_space=pltpu.HBM)
 VMEM = pl.BlockSpec(memory_space=pltpu.VMEM)
-SMEM = pl.BlockSpec(memory_space=pltpu.SMEM)
 PARAMS = pltpu.CompilerParams(vmem_limit_bytes=48 * 1024 * 1024)
 
 
@@ -25,13 +25,6 @@
 
 def dot(a, b, dims=(((1,), (0,)), ((), ()))):
     return lax.dot_general(a, b, dims, preferred_element_type=F32)
-
-
-STEP = 2 * LANES
-
-
-def row_chunks(rows):
-    return [(at, min(STEP, rows - at)) for at in range(0, rows, STEP)]
 
 
 def open_kernel(out):
@@ -98,7 +91,7 @@
         parted[s] = total[:, s * k_own : (s + 1) * k_own]
     me = lax.axis_index("proj")
     for m in range(n_proj):
-        outs[m][...] = parted[me ^ m].astype(BF16)
+        outs[m][...] = parted[me ^ m].astype(outs[m].dtype)
 
 
 def token_sums(rights, lengths, acts, cots, width, seq_len, k2):
@@ -107,7 +100,7 @@
     shape = (ex_dev * 2 * k2, width.shape[1] // n_proj)
     return pl.pallas_call(
         functools.partial(sums_kernel, n_proj, seq_len, k2),
-        out_shape=[jax.ShapeDtypeStruct(shape, BF16)] * n_proj,
+        out_shape=[jax.ShapeDtypeStruct(shape, F32)] + [jax.ShapeDtypeStruct(shape, BF16)] * (n_proj - 1),
         in_specs=[VMEM] * n_proj + [VMEM] + [VMEM] * 3,
         out_specs=[VMEM] * n_proj,
         scratch_shapes=[pltpu.VMEM((n_proj,) + shape, F32)],
@@ -224,7 +217,7 @@
     acts = inputs.reshape(rows, model_cols)
     cots = cotangents.reshape(rows, model_cols)
 
-    by_mask = n_ex == n_proj
+    by_mask = n_ex == n_proj == PLANES
     if by_mask:
         gate, held = lax.optimization_barrier((opening(), heldout_gradient_rows))
         blocks = [heldout_gradient_rows] * n_ex
@@ -236,14 +229,14 @@
     right = rank_side(
         acts, cots, adapter_down_matrix, adapter_up_matrix, rank_side_sketch.transpose(0, 2, 1), gate
     )
-    rights = [right] + [swap(right, "proj", m) for m in range(1, n_proj)]
+    rights = [right] + [swap(right, "proj", m) for m in range(n_proj - 1, 0, -1)]
     if by_mask:
         blocks[1] = swap(heldout_gradient_rows, "ex", 1)
         blocks[3] = swap(blocks[2], "ex", 1)
     pieces = token_sums(rights, lengths, acts, cots, width_side_sketch, seq_len, k2)
-    pieces = [pieces[0]] + [swap(pieces[m], "proj", m) for m in range(1, n_proj)]
+    pieces = [pieces[0]] + [swap(pieces[m], "proj", m) for m in range(n_proj - 1, 0, -1)]
     train_proj, note = partial_dots(pieces, lengths, blocks, 2 * k2)
-    notes = [note] + [swap(note, "proj", m) for m in range(1, n_proj)]
+    notes = [note] + [swap(note, "proj", m) for m in range(n_proj - 1, 0, -1)]
     share = (note.shape[1] - LANES) // n_proj
     scores = final_scores(notes, ex_dev, share, math.sqrt(k1 * 2 * k2), by_mask)
     return (train_proj, scores)

time: 23.4 us -> 23.1 us (0.987)
  waiting for transfers between devices: 6.14 us -> 5.75 us
    ppermute x12, waiting for transfers between devices: 6.14 us -> 5.75 us  [swap(): return lax.ppermute(x, axis, [(i, i ^ mask) for i in range(size)])]
where the time goes in v7:
time: 23.1 us; the launch traced here: 22.9 us
  starting transfers between devices  12.2 us (53%)
  waiting for transfers between devices  5.75 us (25%)
  Pallas kernels  3.55 us (15%)
  between operations  0.77 us (3%)
  local copies, waits for them, and re-layouts  0.64 us (3%)
    ppermute x12, starting transfers between devices, swap(): return lax.ppermute(x, axis, [(i, i ^ mask) for i in range(size)])  12.2 us
    ppermute x12, waiting for transfers between devices, swap(): return lax.ppermute(x, axis, [(i, i ^ mask) for i in range(size)])  5.75 us
    pallas_call x1, Pallas kernels, rank_side(): pl.pallas_call(rank_kernel, out_shape=jax.ShapeDtypeStruct((2 * sketch.sh...  1.36 us
    pallas_call x1, Pallas kernels, token_sums(): pl.pallas_call(functools.partial(sums_kernel, n_proj, seq_len, k2), out_s...  0.91 us
    pallas_call x1, Pallas kernels, final_scores(): pl.pallas_call(functools.partial(scores_kernel, len(notes), ex_dev, scale...  0.73 us
    unnamed x17, local copies, waits for them, and re-layouts  0.64 us
    pallas_call x1, Pallas kernels, partial_dots(): pl.pallas_call(functools.partial(dots_kernel, n_proj, r), out_shape=(pltp...  0.56 us
  transfers between devices with their start and end apart: 12, of which 5 were waited for; matrix products, arithmetic and copies ran while one was open for 3% of the time, Pallas kernels for 10%

profile of v7, /device:TPU:0, one launch (start us, length us, event | category | flops | bytes accessed | tf_op | source)
XLA Modules:
  0.0 22.9 jit_solution(4015569738086605351)
XLA Ops:
  0.7 4.1 %collective-permute-start.7 = (bf16[32,2048]{1,0:T(8,128)(2,1)}, bf16[32,2048]{1,0:T(8,128)(2,1)S(1)}, u32[]{:S(2)}, u32[]{:S(2)}) collective-permute-start(bf16[32,2048]{1,0:T(8,128)(2,1)} %refs_5_.1), channel_id=1, source_target_pairs={{0,8},{4,12},{8,0},{12,4},{1,9},{5,13},{9,1},{13,5},{2,10},{6,14},... | collective-permute-start | bytes 393224 | tf_op jit(solution)/shard_map/ppermute | solution.py:23
  4.8 0.0 copy-start.6
  4.8 0.0 copy-start.7
  4.8 1.4 %rank_side.1.refs_0_ = f32[16,576]{1,0:T(8,128)S(1)} custom-call(bf16[576,1280]{1,0:T(8,128)(2,1)S(1)} %bitcast.4, bf16[576,1280]{1,0:T(8,128)(2,1)S(1)} %bitcast.6, bf16[128,1280]{1,0:T(8,128)(2,1)S(1)} %copy-done.2, bf16[1280,128]{1,0:T(8,128)(2,1)S(1)} %copy-done.3, bf16[2,8,128]{2,1,0:T(8,128)(2,1)S(1)} %bitcast.8, f32[8,128]{1,0:T(8,128)S(1)} %opening.1._), custom_call_target="tpu_custom_call" | custom-call | tf_op jit(solution)/shard_map/rank_side/pallas_call | solution.py:64
  6.2 0.1 collective-permute-start.2
  6.3 1.6 %collective-permute-start.1 = (f32[16,576]{1,0:T(8,128)S(1)}, f32[16,576]{1,0:T(8,128)S(1)}, u32[]{:S(2)}, u32[]{:S(2)}) collective-permute-start(f32[16,576]{1,0:T(8,128)S(1)} %rank_side.1.refs_0_), channel_id=1, source_target_pairs={{0,2},{1,3},{2,0},{3,1},{4,6},{5,7},{6,4},{7,5},{8,10},{9,11},{10,... | collective-permute-start | bytes 110600 | tf_op jit(solution)/shard_map/ppermute | solution.py:23
  7.8 0.3 %collective-permute-start = (f32[16,576]{1,0:T(8,128)S(1)}, f32[16,576]{1,0:T(8,128)S(1)}, u32[]{:S(2)}, u32[]{:S(2)}) collective-permute-start(f32[16,576]{1,0:T(8,128)S(1)} %rank_side.1.refs_0_), channel_id=1, source_target_pairs={{0,3},{1,2},{2,1},{3,0},{4,7},{5,6},{6,5},{7,4},{8,11},{9,10},{10,... | collective-permute-start | bytes 110600 | tf_op jit(solution)/shard_map/ppermute | solution.py:23
  8.1 1.6 %collective-permute-start.6 = (bf16[32,2048]{1,0:T(8,128)(2,1)S(1)}, bf16[32,2048]{1,0:T(8,128)(2,1)S(1)}, u32[]{:S(2)}, u32[]{:S(2)}) collective-permute-start(bf16[32,2048]{1,0:T(8,128)(2,1)S(1)} %copy-done.4), channel_id=1, source_target_pairs={{0,4},{4,0},{8,12},{12,8},{1,5},{5,1},{9,13},{13,9},{2,6},{6,2},{1... | collective-permute-start | bytes 393224 | tf_op jit(solution)/shard_map/ppermute | solution.py:23
  9.7 1.6 %collective-permute-done.7.refs_7_ = bf16[32,2048]{1,0:T(8,128)(2,1)S(1)} collective-permute-done((bf16[32,2048]{1,0:T(8,128)(2,1)}, bf16[32,2048]{1,0:T(8,128)(2,1)S(1)}, u32[]{:S(2)}, u32[]{:S(2)}) %collective-permute-start.7) | collective-permute-done | bytes 131104 | tf_op jit(solution)/shard_map/ppermute | solution.py:23
  11.3 0.8 %collective-permute-start.8 = (bf16[32,2048]{1,0:T(8,128)(2,1)S(1)}, bf16[32,2048]{1,0:T(8,128)(2,1)S(1)}, u32[]{:S(2)}, u32[]{:S(2)}) collective-permute-start(bf16[32,2048]{1,0:T(8,128)(2,1)S(1)} %collective-permute-done.7.refs_7_), channel_id=1, source_target_pairs={{0,4},{4,0},{8,12},{12,8},{1,5},{5,1},{9,13},{13,9},{2,6},{6,2},{1... | collective-permute-start | bytes 393224 | tf_op jit(solution)/shard_map/ppermute | solution.py:23
  12.2 0.9 %token_sums.1 = (f32[64,128]{1,0:T(8,128)S(1)}, bf16[64,128]{1,0:T(8,128)(2,1)S(1)}, bf16[64,128]{1,0:T(8,128)(2,1)S(1)}, bf16[64,128]{1,0:T(8,128)(2,1)S(1)}) custom-call(f32[16,576]{1,0:T(8,128)S(1)} %rank_side.1.refs_0_, f32[16,576]{1,0:T(8,128)S(1)} %collective-permute-done.refs_1_, f32[16,576]{1,0:T(8,128)S(1)} %collective-permute-done.1.refs_2_, ...), custom_call_target="tpu_custom_call" | custom-call | flops 20000000000 | bytes 400000000 | tf_op jit(solution)/shard_map/token_sums/pallas_call | solution.py:101
  13.1 0.9 %collective-permute-start.3 = (bf16[64,128]{1,0:T(8,128)(2,1)S(1)}, bf16[64,128]{1,0:T(8,128)(2,1)S(1)}, u32[]{:S(2)}, u32[]{:S(2)}) collective-permute-start(bf16[64,128]{1,0:T(8,128)(2,1)S(1)} %get-tuple-element.12), channel_id=1, source_target_pairs={{0,3},{1,2},{2,1},{3,0},{4,7},{5,6},{6,5},{7,4},{8,11},{9,10},{10,... | collective-permute-start | bytes 49160 | tf_op jit(solution)/shard_map/ppermute | solution.py:23
  14.0 0.7 %collective-permute-start.4 = (bf16[64,128]{1,0:T(8,128)(2,1)S(1)}, bf16[64,128]{1,0:T(8,128)(2,1)S(1)}, u32[]{:S(2)}, u32[]{:S(2)}) collective-permute-start(bf16[64,128]{1,0:T(8,128)(2,1)S(1)} %get-tuple-element.13), channel_id=1, source_target_pairs={{0,2},{1,3},{2,0},{3,1},{4,6},{5,7},{6,4},{7,5},{8,10},{9,11},{10,... | collective-permute-start | bytes 49160 | tf_op jit(solution)/shard_map/ppermute | solution.py:23
  14.7 0.3 %collective-permute-start.5 = (bf16[64,128]{1,0:T(8,128)(2,1)S(1)}, bf16[64,128]{1,0:T(8,128)(2,1)S(1)}, u32[]{:S(2)}, u32[]{:S(2)}) collective-permute-start(bf16[64,128]{1,0:T(8,128)(2,1)S(1)} %get-tuple-element.14), channel_id=1, source_target_pairs={{0,1},{1,0},{2,3},{3,2},{4,5},{5,4},{6,7},{7,6},{8,9},{9,8},{10,11... | collective-permute-start | bytes 49160 | tf_op jit(solution)/shard_map/ppermute | solution.py:23
  15.0 1.4 %collective-permute-done.3.refs_1_ = bf16[64,128]{1,0:T(8,128)(2,1)S(1)} collective-permute-done((bf16[64,128]{1,0:T(8,128)(2,1)S(1)}, bf16[64,128]{1,0:T(8,128)(2,1)S(1)}, u32[]{:S(2)}, u32[]{:S(2)}) %collective-permute-start.3) | collective-permute-done | bytes 16416 | tf_op jit(solution)/shard_map/ppermute | solution.py:23
  16.4 1.3 %collective-permute-done.4.refs_2_ = bf16[64,128]{1,0:T(8,128)(2,1)S(1)} collective-permute-done((bf16[64,128]{1,0:T(8,128)(2,1)S(1)}, bf16[64,128]{1,0:T(8,128)(2,1)S(1)}, u32[]{:S(2)}, u32[]{:S(2)}) %collective-permute-start.4) | collective-permute-done | bytes 16416 | tf_op jit(solution)/shard_map/ppermute | solution.py:23
  17.7 0.0 collective-permute-done.5.refs_3_
  17.7 0.6 %partial_dots.1 = (bf16[4,2048]{1,0:T(4,128)(2,1)S(1)}, f32[8,256]{1,0:T(8,128)S(1)}) custom-call(f32[64,128]{1,0:T(8,128)S(1)} %get-tuple-element.11.refs_0_, bf16[64,128]{1,0:T(8,128)(2,1)S(1)} %collective-permute-done.3.refs_1_, bf16[64,128]{1,0:T(8,128)(2,1)S(1)} %collective-permute-done.4.refs_2_, bf16[64,128]{1,0:T(8,128)(2,1)S(1)} %collective-permute-done.5.refs_3_, ...), custom_call_target="tpu_custom_call" | custom-call | tf_op jit(solution)/shard_map/partial_dots/pallas_call | solution.py:162
  18.3 0.8 %collective-permute-start.10 = (f32[8,256]{1,0:T(8,128)S(1)}, f32[8,256]{1,0:T(8,128)S(1)}, u32[]{:S(2)}, u32[]{:S(2)}) collective-permute-start(f32[8,256]{1,0:T(8,128)S(1)} %get-tuple-element.17.refs_0_), channel_id=1, source_target_pairs={{0,2},{1,3},{2,0},{3,1},{4,6},{5,7},{6,4},{7,5},{8,10},{9,11},{10,... | collective-permute-start | bytes 24584 | tf_op jit(solution)/shard_map/ppermute | solution.py:23
  19.1 1.1 %collective-permute-start.9 = (f32[8,256]{1,0:T(8,128)S(1)}, f32[8,256]{1,0:T(8,128)S(1)}, u32[]{:S(2)}, u32[]{:S(2)}) collective-permute-start(f32[8,256]{1,0:T(8,128)S(1)} %get-tuple-element.17.refs_0_), channel_id=1, source_target_pairs={{0,3},{1,2},{2,1},{3,0},{4,7},{5,6},{6,5},{7,4},{8,11},{9,10},{10,... | collective-permute-start | bytes 24584 | tf_op jit(solution)/shard_map/ppermute | solution.py:23
  20.2 0.6 %copy.10 = bf16[4,2048]{1,0:T(4,128)(2,1)} copy(bf16[4,2048]{1,0:T(4,128)(2,1)S(1)} %get-tuple-element.18) | data formatting | bytes 32768
  20.8 1.2 %collective-permute-done.10.refs_2_ = f32[8,256]{1,0:T(8,128)S(1)} collective-permute-done((f32[8,256]{1,0:T(8,128)S(1)}, f32[8,256]{1,0:T(8,128)S(1)}, u32[]{:S(2)}, u32[]{:S(2)}) %collective-permute-start.10) | collective-permute-done | bytes 8224 | tf_op jit(solution)/shard_map/ppermute | solution.py:23
  22.0 0.2 collective-permute-done.9.refs_1_
  22.2 0.7 %final_scores.1 = f32[4,32]{1,0:T(4,128)} custom-call(f32[8,256]{1,0:T(8,128)S(1)} %get-tuple-element.17.refs_0_, f32[8,256]{1,0:T(8,128)S(1)} %collective-permute-done.9.refs_1_, f32[8,256]{1,0:T(8,128)S(1)} %collective-permute-done.10.refs_2_, f32[8,256]{1,0:T(8,128)S(1)} %collective-permute-done.11.refs_3_), custom_call_target="tpu_custom_call" | custom-call | tf_op jit(solution)/shard_map/final_scores/pallas_call | solution.py:192
  (22 shorter events, 0.1 us)
Async XLA Ops:
  0.6 4.2 %copy-start.5 = (bf16[2,128,8]{1,2,0:T(8,128)(2,1)S(1)}, bf16[2,128,8]{1,2,0:T(8,128)(2,1)}, u32[]{:S(2)}) copy-start(bf16[2,128,8]{1,2,0:T(8,128)(2,1)} %param.14) | copy-start | bytes 12292
  0.6 4.2 %copy-start.3 = (bf16[1280,128]{1,0:T(8,128)(2,1)S(1)}, bf16[1280,128]{1,0:T(8,128)(2,1)}, u32[]{:S(2)}) copy-start(bf16[1280,128]{1,0:T(8,128)(2,1)} %up.1) | copy-start | bytes 983044
  0.7 4.1 %copy-start.2 = (bf16[128,1280]{1,0:T(8,128)(2,1)S(1)}, bf16[128,1280]{1,0:T(8,128)(2,1)}, u32[]{:S(2)}) copy-start(bf16[128,1280]{1,0:T(8,128)(2,1)} %down.1) | copy-start | bytes 983044
  0.7 4.1 %copy-start.1 = (bf16[4,144,1280]{2,1,0:T(8,128)(2,1)S(1)}, bf16[4,144,1280]{2,1,0:T(8,128)(2,1)}, u32[]{:S(2)}) copy-start(bf16[4,144,1280]{2,1,0:T(8,128)(2,1)} %param.9) | copy-start | bytes 4423684
  0.7 4.1 %copy-start = (bf16[4,144,1280]{2,1,0:T(8,128)(2,1)S(1)}, bf16[4,144,1280]{2,1,0:T(8,128)(2,1)}, u32[]{:S(2)}) copy-start(bf16[4,144,1280]{2,1,0:T(8,128)(2,1)} %param.8) | copy-start | bytes 4423684
  0.7 10.6 %collective-permute-start.7 = (bf16[32,2048]{1,0:T(8,128)(2,1)}, bf16[32,2048]{1,0:T(8,128)(2,1)S(1)}, u32[]{:S(2)}, u32[]{:S(2)}) collective-permute-start(bf16[32,2048]{1,0:T(8,128)(2,1)} %refs_5_.1), channel_id=1, source_target_pairs={{0,8},{4,12},{8,0},{12,4},{1,9},{5,13},{9,1},{13,5},{2,10},{6,14},... | collective-permute-start | bytes 393224 | tf_op jit(solution)/shard_map/ppermute | solution.py:23
  4.8 3.3 %copy-start.4 = (bf16[32,2048]{1,0:T(8,128)(2,1)S(1)}, bf16[32,2048]{1,0:T(8,128)(2,1)}, u32[]{:S(2)}) copy-start(bf16[32,2048]{1,0:T(8,128)(2,1)} %refs_5_.1) | copy-start | bytes 393220
  4.8 7.3 %copy-start.6 = (s32[4]{0:T(128)S(1)}, s32[4]{0:T(128)}, u32[]{:S(2)}) copy-start(s32[4]{0:T(128)} %param.10) | copy-start | bytes 52
  4.8 7.3 %copy-start.7 = (bf16[1280,512]{1,0:T(8,128)(2,1)S(1)}, bf16[1280,512]{1,0:T(8,128)(2,1)}, u32[]{:S(2)}) copy-start(bf16[1280,512]{1,0:T(8,128)(2,1)} %refs_7_.1) | copy-start | bytes 3932164
  6.2 5.9 %collective-permute-start.2 = (f32[16,576]{1,0:T(8,128)S(1)}, f32[16,576]{1,0:T(8,128)S(1)}, u32[]{:S(2)}, u32[]{:S(2)}) collective-permute-start(f32[16,576]{1,0:T(8,128)S(1)} %rank_side.1.refs_0_), channel_id=1, source_target_pairs={{0,1},{1,0},{2,3},{3,2},{4,5},{5,4},{6,7},{7,6},{8,9},{9,8},{10,11... | collective-permute-start | bytes 110600 | tf_op jit(solution)/shard_map/ppermute | solution.py:23
  6.3 5.9 %collective-permute-start.1 = (f32[16,576]{1,0:T(8,128)S(1)}, f32[16,576]{1,0:T(8,128)S(1)}, u32[]{:S(2)}, u32[]{:S(2)}) collective-permute-start(f32[16,576]{1,0:T(8,128)S(1)} %rank_side.1.refs_0_), channel_id=1, source_target_pairs={{0,2},{1,3},{2,0},{3,1},{4,6},{5,7},{6,4},{7,5},{8,10},{9,11},{10,... | collective-permute-start | bytes 110600 | tf_op jit(solution)/shard_map/ppermute | solution.py:23
  7.8 4.3 %collective-permute-start = (f32[16,576]{1,0:T(8,128)S(1)}, f32[16,576]{1,0:T(8,128)S(1)}, u32[]{:S(2)}, u32[]{:S(2)}) collective-permute-start(f32[16,576]{1,0:T(8,128)S(1)} %rank_side.1.refs_0_), channel_id=1, source_target_pairs={{0,3},{1,2},{2,1},{3,0},{4,7},{5,6},{6,5},{7,4},{8,11},{9,10},{10,... | collective-permute-start | bytes 110600 | tf_op jit(solution)/shard_map/ppermute | solution.py:23
  8.1 9.6 %collective-permute-start.6 = (bf16[32,2048]{1,0:T(8,128)(2,1)S(1)}, bf16[32,2048]{1,0:T(8,128)(2,1)S(1)}, u32[]{:S(2)}, u32[]{:S(2)}) collective-permute-start(bf16[32,2048]{1,0:T(8,128)(2,1)S(1)} %copy-done.4), channel_id=1, source_target_pairs={{0,4},{4,0},{8,12},{12,8},{1,5},{5,1},{9,13},{13,9},{2,6},{6,2},{1... | collective-permute-start | bytes 393224 | tf_op jit(solution)/shard_map/ppermute | solution.py:23
  11.3 6.4 %collective-permute-start.8 = (bf16[32,2048]{1,0:T(8,128)(2,1)S(1)}, bf16[32,2048]{1,0:T(8,128)(2,1)S(1)}, u32[]{:S(2)}, u32[]{:S(2)}) collective-permute-start(bf16[32,2048]{1,0:T(8,128)(2,1)S(1)} %collective-permute-done.7.refs_7_), channel_id=1, source_target_pairs={{0,4},{4,0},{8,12},{12,8},{1,5},{5,1},{9,13},{13,9},{2,6},{6,2},{1... | collective-permute-start | bytes 393224 | tf_op jit(solution)/shard_map/ppermute | solution.py:23
  13.1 3.4 %collective-permute-start.3 = (bf16[64,128]{1,0:T(8,128)(2,1)S(1)}, bf16[64,128]{1,0:T(8,128)(2,1)S(1)}, u32[]{:S(2)}, u32[]{:S(2)}) collective-permute-start(bf16[64,128]{1,0:T(8,128)(2,1)S(1)} %get-tuple-element.12), channel_id=1, source_target_pairs={{0,3},{1,2},{2,1},{3,0},{4,7},{5,6},{6,5},{7,4},{8,11},{9,10},{10,... | collective-permute-start | bytes 49160 | tf_op jit(solution)/shard_map/ppermute | solution.py:23
  14.0 3.7 %collective-permute-start.4 = (bf16[64,128]{1,0:T(8,128)(2,1)S(1)}, bf16[64,128]{1,0:T(8,128)(2,1)S(1)}, u32[]{:S(2)}, u32[]{:S(2)}) collective-permute-start(bf16[64,128]{1,0:T(8,128)(2,1)S(1)} %get-tuple-element.13), channel_id=1, source_target_pairs={{0,2},{1,3},{2,0},{3,1},{4,6},{5,7},{6,4},{7,5},{8,10},{9,11},{10,... | collective-permute-start | bytes 49160 | tf_op jit(solution)/shard_map/ppermute | solution.py:23
  14.7 3.0 %collective-permute-start.5 = (bf16[64,128]{1,0:T(8,128)(2,1)S(1)}, bf16[64,128]{1,0:T(8,128)(2,1)S(1)}, u32[]{:S(2)}, u32[]{:S(2)}) collective-permute-start(bf16[64,128]{1,0:T(8,128)(2,1)S(1)} %get-tuple-element.14), channel_id=1, source_target_pairs={{0,1},{1,0},{2,3},{3,2},{4,5},{5,4},{6,7},{7,6},{8,9},{9,8},{10,11... | collective-permute-start | bytes 49160 | tf_op jit(solution)/shard_map/ppermute | solution.py:23
  18.3 2.5 %collective-permute-start.11 = (f32[8,256]{1,0:T(8,128)S(1)}, f32[8,256]{1,0:T(8,128)S(1)}, u32[]{:S(2)}, u32[]{:S(2)}) collective-permute-start(f32[8,256]{1,0:T(8,128)S(1)} %get-tuple-element.17.refs_0_), channel_id=1, source_target_pairs={{0,1},{1,0},{2,3},{3,2},{4,5},{5,4},{6,7},{7,6},{8,9},{9,8},{10,11... | collective-permute-start | bytes 24584 | tf_op jit(solution)/shard_map/ppermute | solution.py:23
  18.3 3.7 %collective-permute-start.10 = (f32[8,256]{1,0:T(8,128)S(1)}, f32[8,256]{1,0:T(8,128)S(1)}, u32[]{:S(2)}, u32[]{:S(2)}) collective-permute-start(f32[8,256]{1,0:T(8,128)S(1)} %get-tuple-element.17.refs_0_), channel_id=1, source_target_pairs={{0,2},{1,3},{2,0},{3,1},{4,6},{5,7},{6,4},{7,5},{8,10},{9,11},{10,... | collective-permute-start | bytes 24584 | tf_op jit(solution)/shard_map/ppermute | solution.py:23
  19.1 3.1 %collective-permute-start.9 = (f32[8,256]{1,0:T(8,128)S(1)}, f32[8,256]{1,0:T(8,128)S(1)}, u32[]{:S(2)}, u32[]{:S(2)}) collective-permute-start(f32[8,256]{1,0:T(8,128)S(1)} %get-tuple-element.17.refs_0_), channel_id=1, source_target_pairs={{0,3},{1,2},{2,1},{3,0},{4,7},{5,6},{6,5},{7,4},{8,11},{9,10},{10,... | collective-permute-start | bytes 24584 | tf_op jit(solution)/shard_map/ppermute | solution.py:23

commit v8 on v7

--- a/solution.py
+++ b/solution.py
@@ -229,14 +229,14 @@
     right = rank_side(
         acts, cots, adapter_down_matrix, adapter_up_matrix, rank_side_sketch.transpose(0, 2, 1), gate
     )
-    rights = [right] + [swap(right, "proj", m) for m in range(n_proj - 1, 0, -1)]
+    rights = [right] + [swap(right, "proj", m) for m in range(1, n_proj)]
     if by_mask:
         blocks[1] = swap(heldout_gradient_rows, "ex", 1)
         blocks[3] = swap(blocks[2], "ex", 1)
     pieces = token_sums(rights, lengths, acts, cots, width_side_sketch, seq_len, k2)
     pieces = [pieces[0]] + [swap(pieces[m], "proj", m) for m in range(n_proj - 1, 0, -1)]
     train_proj, note = partial_dots(pieces, lengths, blocks, 2 * k2)
-    notes = [note] + [swap(note, "proj", m) for m in range(n_proj - 1, 0, -1)]
+    notes = [note] + [swap(note, "proj", m) for m in range(1, n_proj)]
     share = (note.shape[1] - LANES) // n_proj
     scores = final_scores(notes, ex_dev, share, math.sqrt(k1 * 2 * k2), by_mask)
     return (train_proj, scores)

time: 23.1 us -> 22.9 us (level)
  no operation moved by 1% of the time
where the time goes in v8:
time: 22.9 us; the launch traced here: 22.8 us
  starting transfers between devices  12.2 us (53%)
  waiting for transfers between devices  5.64 us (25%)
  Pallas kernels  3.55 us (16%)
  between operations  0.76 us (3%)
  local copies, waits for them, and re-layouts  0.64 us (3%)
    ppermute x12, starting transfers between devices, swap(): return lax.ppermute(x, axis, [(i, i ^ mask) for i in range(size)])  12.2 us
    ppermute x12, waiting for transfers between devices, swap(): return lax.ppermute(x, axis, [(i, i ^ mask) for i in range(size)])  5.64 us
    pallas_call x1, Pallas kernels, rank_side(): pl.pallas_call(rank_kernel, out_shape=jax.ShapeDtypeStruct((2 * sketch.sh...  1.36 us
    pallas_call x1, Pallas kernels, token_sums(): pl.pallas_call(functools.partial(sums_kernel, n_proj, seq_len, k2), out_s...  0.91 us
    pallas_call x1, Pallas kernels, final_scores(): pl.pallas_call(functools.partial(scores_kernel, len(notes), ex_dev, scale...  0.73 us
    unnamed x17, local copies, waits for them, and re-layouts  0.64 us
    pallas_call x1, Pallas kernels, partial_dots(): pl.pallas_call(functools.partial(dots_kernel, n_proj, r), out_shape=(pltp...  0.56 us
  transfers between devices with their start and end apart: 12, of which 5 were waited for; matrix products, arithmetic and copies ran while one was open for 3% of the time, Pallas kernels for 10%

profile of v8, /device:TPU:0, one launch (start us, length us, event | category | flops | bytes accessed | tf_op | source)
XLA Modules:
  0.0 22.8 jit_solution(13583953086303861738)
XLA Ops:
  0.7 4.1 %collective-permute-start.7 = (bf16[32,2048]{1,0:T(8,128)(2,1)}, bf16[32,2048]{1,0:T(8,128)(2,1)S(1)}, u32[]{:S(2)}, u32[]{:S(2)}) collective-permute-start(bf16[32,2048]{1,0:T(8,128)(2,1)} %refs_5_.1), channel_id=1, source_target_pairs={{0,8},{4,12},{8,0},{12,4},{1,9},{5,13},{9,1},{13,5},{2,10},{6,14},... | collective-permute-start | bytes 393224 | tf_op jit(solution)/shard_map/ppermute | solution.py:23
  4.8 0.0 copy-start.6
  4.8 0.0 copy-start.7
  4.8 1.4 %rank_side.1.refs_0_ = f32[16,576]{1,0:T(8,128)S(1)} custom-call(bf16[576,1280]{1,0:T(8,128)(2,1)S(1)} %bitcast.4, bf16[576,1280]{1,0:T(8,128)(2,1)S(1)} %bitcast.6, bf16[128,1280]{1,0:T(8,128)(2,1)S(1)} %copy-done.2, bf16[1280,128]{1,0:T(8,128)(2,1)S(1)} %copy-done.3, bf16[2,8,128]{2,1,0:T(8,128)(2,1)S(1)} %bitcast.8, f32[8,128]{1,0:T(8,128)S(1)} %opening.1._), custom_call_target="tpu_custom_call" | custom-call | tf_op jit(solution)/shard_map/rank_side/pallas_call | solution.py:64
  6.2 0.7 %collective-permute-start.2 = (f32[16,576]{1,0:T(8,128)S(1)}, f32[16,576]{1,0:T(8,128)S(1)}, u32[]{:S(2)}, u32[]{:S(2)}) collective-permute-start(f32[16,576]{1,0:T(8,128)S(1)} %rank_side.1.refs_0_), channel_id=1, source_target_pairs={{0,3},{1,2},{2,1},{3,0},{4,7},{5,6},{6,5},{7,4},{8,11},{9,10},{10,... | collective-permute-start | bytes 110600 | tf_op jit(solution)/shard_map/ppermute | solution.py:23
  6.9 0.9 %collective-permute-start.1 = (f32[16,576]{1,0:T(8,128)S(1)}, f32[16,576]{1,0:T(8,128)S(1)}, u32[]{:S(2)}, u32[]{:S(2)}) collective-permute-start(f32[16,576]{1,0:T(8,128)S(1)} %rank_side.1.refs_0_), channel_id=1, source_target_pairs={{0,2},{1,3},{2,0},{3,1},{4,6},{5,7},{6,4},{7,5},{8,10},{9,11},{10,... | collective-permute-start | bytes 110600 | tf_op jit(solution)/shard_map/ppermute | solution.py:23
  7.8 0.3 %collective-permute-start = (f32[16,576]{1,0:T(8,128)S(1)}, f32[16,576]{1,0:T(8,128)S(1)}, u32[]{:S(2)}, u32[]{:S(2)}) collective-permute-start(f32[16,576]{1,0:T(8,128)S(1)} %rank_side.1.refs_0_), channel_id=1, source_target_pairs={{0,1},{1,0},{2,3},{3,2},{4,5},{5,4},{6,7},{7,6},{8,9},{9,8},{10,11... | collective-permute-start | bytes 110600 | tf_op jit(solution)/shard_map/ppermute | solution.py:23
  8.1 1.6 %collective-permute-start.6 = (bf16[32,2048]{1,0:T(8,128)(2,1)S(1)}, bf16[32,2048]{1,0:T(8,128)(2,1)S(1)}, u32[]{:S(2)}, u32[]{:S(2)}) collective-permute-start(bf16[32,2048]{1,0:T(8,128)(2,1)S(1)} %copy-done.4), channel_id=1, source_target_pairs={{0,4},{4,0},{8,12},{12,8},{1,5},{5,1},{9,13},{13,9},{2,6},{6,2},{1... | collective-permute-start | bytes 393224 | tf_op jit(solution)/shard_map/ppermute | solution.py:23
  9.7 1.7 %collective-permute-done.7.refs_7_ = bf16[32,2048]{1,0:T(8,128)(2,1)S(1)} collective-permute-done((bf16[32,2048]{1,0:T(8,128)(2,1)}, bf16[32,2048]{1,0:T(8,128)(2,1)S(1)}, u32[]{:S(2)}, u32[]{:S(2)}) %collective-permute-start.7) | collective-permute-done | bytes 131104 | tf_op jit(solution)/shard_map/ppermute | solution.py:23
  11.3 0.8 %collective-permute-start.8 = (bf16[32,2048]{1,0:T(8,128)(2,1)S(1)}, bf16[32,2048]{1,0:T(8,128)(2,1)S(1)}, u32[]{:S(2)}, u32[]{:S(2)}) collective-permute-start(bf16[32,2048]{1,0:T(8,128)(2,1)S(1)} %collective-permute-done.7.refs_7_), channel_id=1, source_target_pairs={{0,4},{4,0},{8,12},{12,8},{1,5},{5,1},{9,13},{13,9},{2,6},{6,2},{1... | collective-permute-start | bytes 393224 | tf_op jit(solution)/shard_map/ppermute | solution.py:23
  12.2 0.9 %token_sums.1 = (f32[64,128]{1,0:T(8,128)S(1)}, bf16[64,128]{1,0:T(8,128)(2,1)S(1)}, bf16[64,128]{1,0:T(8,128)(2,1)S(1)}, bf16[64,128]{1,0:T(8,128)(2,1)S(1)}) custom-call(f32[16,576]{1,0:T(8,128)S(1)} %rank_side.1.refs_0_, f32[16,576]{1,0:T(8,128)S(1)} %collective-permute-done.refs_1_, f32[16,576]{1,0:T(8,128)S(1)} %collective-permute-done.1.refs_2_, ...), custom_call_target="tpu_custom_call" | custom-call | flops 20000000000 | bytes 400000000 | tf_op jit(solution)/shard_map/token_sums/pallas_call | solution.py:101
  13.1 0.9 %collective-permute-start.3 = (bf16[64,128]{1,0:T(8,128)(2,1)S(1)}, bf16[64,128]{1,0:T(8,128)(2,1)S(1)}, u32[]{:S(2)}, u32[]{:S(2)}) collective-permute-start(bf16[64,128]{1,0:T(8,128)(2,1)S(1)} %get-tuple-element.12), channel_id=1, source_target_pairs={{0,3},{1,2},{2,1},{3,0},{4,7},{5,6},{6,5},{7,4},{8,11},{9,10},{10,... | collective-permute-start | bytes 49160 | tf_op jit(solution)/shard_map/ppermute | solution.py:23
  14.0 0.7 %collective-permute-start.4 = (bf16[64,128]{1,0:T(8,128)(2,1)S(1)}, bf16[64,128]{1,0:T(8,128)(2,1)S(1)}, u32[]{:S(2)}, u32[]{:S(2)}) collective-permute-start(bf16[64,128]{1,0:T(8,128)(2,1)S(1)} %get-tuple-element.13), channel_id=1, source_target_pairs={{0,2},{1,3},{2,0},{3,1},{4,6},{5,7},{6,4},{7,5},{8,10},{9,11},{10,... | collective-permute-start | bytes 49160 | tf_op jit(solution)/shard_map/ppermute | solution.py:23
  14.7 0.3 %collective-permute-start.5 = (bf16[64,128]{1,0:T(8,128)(2,1)S(1)}, bf16[64,128]{1,0:T(8,128)(2,1)S(1)}, u32[]{:S(2)}, u32[]{:S(2)}) collective-permute-start(bf16[64,128]{1,0:T(8,128)(2,1)S(1)} %get-tuple-element.14), channel_id=1, source_target_pairs={{0,1},{1,0},{2,3},{3,2},{4,5},{5,4},{6,7},{7,6},{8,9},{9,8},{10,11... | collective-permute-start | bytes 49160 | tf_op jit(solution)/shard_map/ppermute | solution.py:23
  15.0 1.4 %collective-permute-done.3.refs_1_ = bf16[64,128]{1,0:T(8,128)(2,1)S(1)} collective-permute-done((bf16[64,128]{1,0:T(8,128)(2,1)S(1)}, bf16[64,128]{1,0:T(8,128)(2,1)S(1)}, u32[]{:S(2)}, u32[]{:S(2)}) %collective-permute-start.3) | collective-permute-done | bytes 16416 | tf_op jit(solution)/shard_map/ppermute | solution.py:23
  16.4 1.3 %collective-permute-done.4.refs_2_ = bf16[64,128]{1,0:T(8,128)(2,1)S(1)} collective-permute-done((bf16[64,128]{1,0:T(8,128)(2,1)S(1)}, bf16[64,128]{1,0:T(8,128)(2,1)S(1)}, u32[]{:S(2)}, u32[]{:S(2)}) %collective-permute-start.4) | collective-permute-done | bytes 16416 | tf_op jit(solution)/shard_map/ppermute | solution.py:23
  17.7 0.6 %partial_dots.1 = (bf16[4,2048]{1,0:T(4,128)(2,1)S(1)}, f32[8,256]{1,0:T(8,128)S(1)}) custom-call(f32[64,128]{1,0:T(8,128)S(1)} %get-tuple-element.11.refs_0_, bf16[64,128]{1,0:T(8,128)(2,1)S(1)} %collective-permute-done.3.refs_1_, bf16[64,128]{1,0:T(8,128)(2,1)S(1)} %collective-permute-done.4.refs_2_, bf16[64,128]{1,0:T(8,128)(2,1)S(1)} %collective-permute-done.5.refs_3_, ...), custom_call_target="tpu_custom_call" | custom-call | tf_op jit(solution)/shard_map/partial_dots/pallas_call | solution.py:162
  18.3 0.1 collective-permute-start.11
  18.4 1.2 %collective-permute-start.10 = (f32[8,256]{1,0:T(8,128)S(1)}, f32[8,256]{1,0:T(8,128)S(1)}, u32[]{:S(2)}, u32[]{:S(2)}) collective-permute-start(f32[8,256]{1,0:T(8,128)S(1)} %get-tuple-element.17.refs_0_), channel_id=1, source_target_pairs={{0,2},{1,3},{2,0},{3,1},{4,6},{5,7},{6,4},{7,5},{8,10},{9,11},{10,... | collective-permute-start | bytes 24584 | tf_op jit(solution)/shard_map/ppermute | solution.py:23
  19.6 0.6 %collective-permute-start.9 = (f32[8,256]{1,0:T(8,128)S(1)}, f32[8,256]{1,0:T(8,128)S(1)}, u32[]{:S(2)}, u32[]{:S(2)}) collective-permute-start(f32[8,256]{1,0:T(8,128)S(1)} %get-tuple-element.17.refs_0_), channel_id=1, source_target_pairs={{0,1},{1,0},{2,3},{3,2},{4,5},{5,4},{6,7},{7,6},{8,9},{9,8},{10,11... | collective-permute-start | bytes 24584 | tf_op jit(solution)/shard_map/ppermute | solution.py:23
  20.2 0.6 %copy.10 = bf16[4,2048]{1,0:T(4,128)(2,1)} copy(bf16[4,2048]{1,0:T(4,128)(2,1)S(1)} %get-tuple-element.18) | data formatting | bytes 32768
  20.8 0.6 %collective-permute-done.11.refs_3_ = f32[8,256]{1,0:T(8,128)S(1)} collective-permute-done((f32[8,256]{1,0:T(8,128)S(1)}, f32[8,256]{1,0:T(8,128)S(1)}, u32[]{:S(2)}, u32[]{:S(2)}) %collective-permute-start.11) | collective-permute-done | bytes 8224 | tf_op jit(solution)/shard_map/ppermute | solution.py:23
  21.4 0.6 %collective-permute-done.10.refs_2_ = f32[8,256]{1,0:T(8,128)S(1)} collective-permute-done((f32[8,256]{1,0:T(8,128)S(1)}, f32[8,256]{1,0:T(8,128)S(1)}, u32[]{:S(2)}, u32[]{:S(2)}) %collective-permute-start.10) | collective-permute-done | bytes 8224 | tf_op jit(solution)/shard_map/ppermute | solution.py:23
  22.0 0.7 %final_scores.1 = f32[4,32]{1,0:T(4,128)} custom-call(f32[8,256]{1,0:T(8,128)S(1)} %get-tuple-element.17.refs_0_, f32[8,256]{1,0:T(8,128)S(1)} %collective-permute-done.9.refs_1_, f32[8,256]{1,0:T(8,128)S(1)} %collective-permute-done.10.refs_2_, f32[8,256]{1,0:T(8,128)S(1)} %collective-permute-done.11.refs_3_), custom_call_target="tpu_custom_call" | custom-call | tf_op jit(solution)/shard_map/final_scores/pallas_call | solution.py:192
  (22 shorter events, 0.0 us)
Async XLA Ops:
  0.6 4.2 %copy-start.5 = (bf16[2,128,8]{1,2,0:T(8,128)(2,1)S(1)}, bf16[2,128,8]{1,2,0:T(8,128)(2,1)}, u32[]{:S(2)}) copy-start(bf16[2,128,8]{1,2,0:T(8,128)(2,1)} %param.14) | copy-start | bytes 12292
  0.6 4.2 %copy-start.3 = (bf16[1280,128]{1,0:T(8,128)(2,1)S(1)}, bf16[1280,128]{1,0:T(8,128)(2,1)}, u32[]{:S(2)}) copy-start(bf16[1280,128]{1,0:T(8,128)(2,1)} %up.1) | copy-start | bytes 983044
  0.7 4.1 %copy-start.2 = (bf16[128,1280]{1,0:T(8,128)(2,1)S(1)}, bf16[128,1280]{1,0:T(8,128)(2,1)}, u32[]{:S(2)}) copy-start(bf16[128,1280]{1,0:T(8,128)(2,1)} %down.1) | copy-start | bytes 983044
  0.7 4.1 %copy-start.1 = (bf16[4,144,1280]{2,1,0:T(8,128)(2,1)S(1)}, bf16[4,144,1280]{2,1,0:T(8,128)(2,1)}, u32[]{:S(2)}) copy-start(bf16[4,144,1280]{2,1,0:T(8,128)(2,1)} %param.9) | copy-start | bytes 4423684
  0.7 4.1 %copy-start = (bf16[4,144,1280]{2,1,0:T(8,128)(2,1)S(1)}, bf16[4,144,1280]{2,1,0:T(8,128)(2,1)}, u32[]{:S(2)}) copy-start(bf16[4,144,1280]{2,1,0:T(8,128)(2,1)} %param.8) | copy-start | bytes 4423684
  0.7 10.7 %collective-permute-start.7 = (bf16[32,2048]{1,0:T(8,128)(2,1)}, bf16[32,2048]{1,0:T(8,128)(2,1)S(1)}, u32[]{:S(2)}, u32[]{:S(2)}) collective-permute-start(bf16[32,2048]{1,0:T(8,128)(2,1)} %refs_5_.1), channel_id=1, source_target_pairs={{0,8},{4,12},{8,0},{12,4},{1,9},{5,13},{9,1},{13,5},{2,10},{6,14},... | collective-permute-start | bytes 393224 | tf_op jit(solution)/shard_map/ppermute | solution.py:23
  4.8 3.3 %copy-start.4 = (bf16[32,2048]{1,0:T(8,128)(2,1)S(1)}, bf16[32,2048]{1,0:T(8,128)(2,1)}, u32[]{:S(2)}) copy-start(bf16[32,2048]{1,0:T(8,128)(2,1)} %refs_5_.1) | copy-start | bytes 393220
  4.8 7.3 %copy-start.6 = (s32[4]{0:T(128)S(1)}, s32[4]{0:T(128)}, u32[]{:S(2)}) copy-start(s32[4]{0:T(128)} %param.10) | copy-start | bytes 52
  4.8 7.3 %copy-start.7 = (bf16[1280,512]{1,0:T(8,128)(2,1)S(1)}, bf16[1280,512]{1,0:T(8,128)(2,1)}, u32[]{:S(2)}) copy-start(bf16[1280,512]{1,0:T(8,128)(2,1)} %refs_7_.1) | copy-start | bytes 3932164
  6.2 5.9 %collective-permute-start.2 = (f32[16,576]{1,0:T(8,128)S(1)}, f32[16,576]{1,0:T(8,128)S(1)}, u32[]{:S(2)}, u32[]{:S(2)}) collective-permute-start(f32[16,576]{1,0:T(8,128)S(1)} %rank_side.1.refs_0_), channel_id=1, source_target_pairs={{0,3},{1,2},{2,1},{3,0},{4,7},{5,6},{6,5},{7,4},{8,11},{9,10},{10,... | collective-permute-start | bytes 110600 | tf_op jit(solution)/shard_map/ppermute | solution.py:23
  6.9 5.2 %collective-permute-start.1 = (f32[16,576]{1,0:T(8,128)S(1)}, f32[16,576]{1,0:T(8,128)S(1)}, u32[]{:S(2)}, u32[]{:S(2)}) collective-permute-start(f32[16,576]{1,0:T(8,128)S(1)} %rank_side.1.refs_0_), channel_id=1, source_target_pairs={{0,2},{1,3},{2,0},{3,1},{4,6},{5,7},{6,4},{7,5},{8,10},{9,11},{10,... | collective-permute-start | bytes 110600 | tf_op jit(solution)/shard_map/ppermute | solution.py:23
  7.8 4.3 %collective-permute-start = (f32[16,576]{1,0:T(8,128)S(1)}, f32[16,576]{1,0:T(8,128)S(1)}, u32[]{:S(2)}, u32[]{:S(2)}) collective-permute-start(f32[16,576]{1,0:T(8,128)S(1)} %rank_side.1.refs_0_), channel_id=1, source_target_pairs={{0,1},{1,0},{2,3},{3,2},{4,5},{5,4},{6,7},{7,6},{8,9},{9,8},{10,11... | collective-permute-start | bytes 110600 | tf_op jit(solution)/shard_map/ppermute | solution.py:23
  8.1 9.6 %collective-permute-start.6 = (bf16[32,2048]{1,0:T(8,128)(2,1)S(1)}, bf16[32,2048]{1,0:T(8,128)(2,1)S(1)}, u32[]{:S(2)}, u32[]{:S(2)}) collective-permute-start(bf16[32,2048]{1,0:T(8,128)(2,1)S(1)} %copy-done.4), channel_id=1, source_target_pairs={{0,4},{4,0},{8,12},{12,8},{1,5},{5,1},{9,13},{13,9},{2,6},{6,2},{1... | collective-permute-start | bytes 393224 | tf_op jit(solution)/shard_map/ppermute | solution.py:23
  11.3 6.4 %collective-permute-start.8 = (bf16[32,2048]{1,0:T(8,128)(2,1)S(1)}, bf16[32,2048]{1,0:T(8,128)(2,1)S(1)}, u32[]{:S(2)}, u32[]{:S(2)}) collective-permute-start(bf16[32,2048]{1,0:T(8,128)(2,1)S(1)} %collective-permute-done.7.refs_7_), channel_id=1, source_target_pairs={{0,4},{4,0},{8,12},{12,8},{1,5},{5,1},{9,13},{13,9},{2,6},{6,2},{1... | collective-permute-start | bytes 393224 | tf_op jit(solution)/shard_map/ppermute | solution.py:23
  13.1 3.4 %collective-permute-start.3 = (bf16[64,128]{1,0:T(8,128)(2,1)S(1)}, bf16[64,128]{1,0:T(8,128)(2,1)S(1)}, u32[]{:S(2)}, u32[]{:S(2)}) collective-permute-start(bf16[64,128]{1,0:T(8,128)(2,1)S(1)} %get-tuple-element.12), channel_id=1, source_target_pairs={{0,3},{1,2},{2,1},{3,0},{4,7},{5,6},{6,5},{7,4},{8,11},{9,10},{10,... | collective-permute-start | bytes 49160 | tf_op jit(solution)/shard_map/ppermute | solution.py:23
  14.0 3.7 %collective-permute-start.4 = (bf16[64,128]{1,0:T(8,128)(2,1)S(1)}, bf16[64,128]{1,0:T(8,128)(2,1)S(1)}, u32[]{:S(2)}, u32[]{:S(2)}) collective-permute-start(bf16[64,128]{1,0:T(8,128)(2,1)S(1)} %get-tuple-element.13), channel_id=1, source_target_pairs={{0,2},{1,3},{2,0},{3,1},{4,6},{5,7},{6,4},{7,5},{8,10},{9,11},{10,... | collective-permute-start | bytes 49160 | tf_op jit(solution)/shard_map/ppermute | solution.py:23
  14.7 3.0 %collective-permute-start.5 = (bf16[64,128]{1,0:T(8,128)(2,1)S(1)}, bf16[64,128]{1,0:T(8,128)(2,1)S(1)}, u32[]{:S(2)}, u32[]{:S(2)}) collective-permute-start(bf16[64,128]{1,0:T(8,128)(2,1)S(1)} %get-tuple-element.14), channel_id=1, source_target_pairs={{0,1},{1,0},{2,3},{3,2},{4,5},{5,4},{6,7},{7,6},{8,9},{9,8},{10,11... | collective-permute-start | bytes 49160 | tf_op jit(solution)/shard_map/ppermute | solution.py:23
  18.3 3.1 %collective-permute-start.11 = (f32[8,256]{1,0:T(8,128)S(1)}, f32[8,256]{1,0:T(8,128)S(1)}, u32[]{:S(2)}, u32[]{:S(2)}) collective-permute-start(f32[8,256]{1,0:T(8,128)S(1)} %get-tuple-element.17.refs_0_), channel_id=1, source_target_pairs={{0,3},{1,2},{2,1},{3,0},{4,7},{5,6},{6,5},{7,4},{8,11},{9,10},{10,... | collective-permute-start | bytes 24584 | tf_op jit(solution)/shard_map/ppermute | solution.py:23
  18.4 3.7 %collective-permute-start.10 = (f32[8,256]{1,0:T(8,128)S(1)}, f32[8,256]{1,0:T(8,128)S(1)}, u32[]{:S(2)}, u32[]{:S(2)}) collective-permute-start(f32[8,256]{1,0:T(8,128)S(1)} %get-tuple-element.17.refs_0_), channel_id=1, source_target_pairs={{0,2},{1,3},{2,0},{3,1},{4,6},{5,7},{6,4},{7,5},{8,10},{9,11},{10,... | collective-permute-start | bytes 24584 | tf_op jit(solution)/shard_map/ppermute | solution.py:23
  19.6 2.5 %collective-permute-start.9 = (f32[8,256]{1,0:T(8,128)S(1)}, f32[8,256]{1,0:T(8,128)S(1)}, u32[]{:S(2)}, u32[]{:S(2)}) collective-permute-start(f32[8,256]{1,0:T(8,128)S(1)} %get-tuple-element.17.refs_0_), channel_id=1, source_target_pairs={{0,1},{1,0},{2,3},{3,2},{4,5},{5,4},{6,7},{7,6},{8,9},{9,8},{10,11... | collective-permute-start | bytes 24584 | tf_op jit(solution)/shard_map/ppermute | solution.py:23

commit v9 on v8

--- a/solution.py
+++ b/solution.py
@@ -63,7 +63,7 @@
     rows = acts.shape[0]
     return pl.pallas_call(
         rank_kernel,
-        out_shape=jax.ShapeDtypeStruct((2 * sketch.shape[1], rows), F32),
+        out_shape=jax.ShapeDtypeStruct((2 * sketch.shape[1], rows), BF16),
         in_specs=[VMEM] * 5 + [pl.BlockSpec(memory_space=pl.ANY)],
         out_specs=VMEM,
         compiler_params=PARAMS,
@@ -73,7 +73,7 @@
 
 def sums_kernel(n_proj, seq_len, k2, *refs):
     rights, (lengths, acts, cots, width, *outs, parted) = refs[:n_proj], refs[n_proj:]
-    right = sum([r[...] for r in rights[1:]], rights[0][...])
+    right = sum([r[...].astype(F32) for r in rights[1:]], rights[0][...].astype(F32))
     ex_dev, rows = lengths.shape[1], acts.shape[0]
     t = lax.broadcasted_iota(jnp.int32, (k2, rows), 1)
     wide = []
@@ -221,7 +221,7 @@
     if by_mask:
         gate, held = lax.optimization_barrier((opening(), heldout_gradient_rows))
         blocks = [heldout_gradient_rows] * n_ex
-        blocks[2] = swap(held, "ex", 2)
+        blocks[3] = swap(held, "ex", 3)
     else:
         gate = opening()
         blocks = [lax.all_gather(heldout_gradient_rows, "ex", axis=0, tiled=True)]
@@ -232,7 +232,7 @@
     rights = [right] + [swap(right, "proj", m) for m in range(1, n_proj)]
     if by_mask:
         blocks[1] = swap(heldout_gradient_rows, "ex", 1)
-        blocks[3] = swap(blocks[2], "ex", 1)
+        blocks[2] = swap(blocks[3], "ex", 1)
     pieces = token_sums(rights, lengths, acts, cots, width_side_sketch, seq_len, k2)
     pieces = [pieces[0]] + [swap(pieces[m], "proj", m) for m in range(n_proj - 1, 0, -1)]
     train_proj, note = partial_dots(pieces, lengths, blocks, 2 * k2)

time: 22.9 us -> 22.8 us (level)
  waiting for transfers between devices: 5.64 us -> 4.46 us
  starting transfers between devices: 12.2 us -> 13.2 us
    ppermute x12, waiting for transfers between devices: 5.64 us -> 4.46 us  [swap(): return lax.ppermute(x, axis, [(i, i ^ mask) for i in range(size)])]
    ppermute x12, starting transfers between devices: 12.2 us -> 13.2 us  [swap(): return lax.ppermute(x, axis, [(i, i ^ mask) for i in range(size)])]
  transfers between devices with their start and end apart: 12 -> 12, of which waited for: 5 -> 6; matrix products, arithmetic and copies ran while one was open for 3% -> 3% of each run, Pallas kernels for 10% -> 10%
where the time goes in v9:
time: 22.8 us; the launch traced here: 22.7 us
  starting transfers between devices  13.2 us (58%)
  waiting for transfers between devices  4.46 us (20%)
  Pallas kernels  3.55 us (16%)
  between operations  0.76 us (3%)
  local copies, waits for them, and re-layouts  0.64 us (3%)
    ppermute x12, starting transfers between devices, swap(): return lax.ppermute(x, axis, [(i, i ^ mask) for i in range(size)])  13.2 us
    ppermute x12, waiting for transfers between devices, swap(): return lax.ppermute(x, axis, [(i, i ^ mask) for i in range(size)])  4.46 us
    pallas_call x1, Pallas kernels, rank_side(): pl.pallas_call(rank_kernel, out_shape=jax.ShapeDtypeStruct((2 * sketch.sh...  1.36 us
    pallas_call x1, Pallas kernels, token_sums(): pl.pallas_call(functools.partial(sums_kernel, n_proj, seq_len, k2), out_s...  0.91 us
    pallas_call x1, Pallas kernels, final_scores(): pl.pallas_call(functools.partial(scores_kernel, len(notes), ex_dev, scale...  0.73 us
    unnamed x17, local copies, waits for them, and re-layouts  0.64 us
    pallas_call x1, Pallas kernels, partial_dots(): pl.pallas_call(functools.partial(dots_kernel, n_proj, r), out_shape=(pltp...  0.56 us
  transfers between devices with their start and end apart: 12, of which 6 were waited for; matrix products, arithmetic and copies ran while one was open for 3% of the time, Pallas kernels for 10%

profile of v9, /device:TPU:0, one launch (start us, length us, event | category | flops | bytes accessed | tf_op | source)
XLA Modules:
  0.0 22.7 jit_solution(1351883991951033918)
XLA Ops:
  0.7 5.1 %collective-permute-start.7 = (bf16[32,2048]{1,0:T(8,128)(2,1)}, bf16[32,2048]{1,0:T(8,128)(2,1)S(1)}, u32[]{:S(2)}, u32[]{:S(2)}) collective-permute-start(bf16[32,2048]{1,0:T(8,128)(2,1)} %refs_5_.1), channel_id=1, source_target_pairs={{0,12},{4,8},{8,4},{12,0},{1,13},{5,9},{9,5},{13,1},{2,14},{6,10},... | collective-permute-start | bytes 393224 | tf_op jit(solution)/shard_map/ppermute | solution.py:23
  5.8 0.0 copy-start.6
  5.9 0.0 copy-start.7
  5.9 1.4 %rank_side.1.refs_0_ = bf16[16,576]{1,0:T(8,128)(2,1)S(1)} custom-call(bf16[576,1280]{1,0:T(8,128)(2,1)S(1)} %bitcast.4, bf16[576,1280]{1,0:T(8,128)(2,1)S(1)} %bitcast.6, bf16[128,1280]{1,0:T(8,128)(2,1)S(1)} %copy-done.2, bf16[1280,128]{1,0:T(8,128)(2,1)S(1)} %copy-done.3, bf16[2,8,128]{2,1,0:T(8,128)(2,1)S(1)} %bitcast.8, f32[8,128]{1,0:T(8,128)S(1)} %opening.1._), custom_call_target="tpu_custom_call" | custom-call | tf_op jit(solution)/shard_map/rank_side/pallas_call | solution.py:64
  7.2 0.7 %collective-permute-start.2 = (bf16[16,576]{1,0:T(8,128)(2,1)S(1)}, bf16[16,576]{1,0:T(8,128)(2,1)S(1)}, u32[]{:S(2)}, u32[]{:S(2)}) collective-permute-start(bf16[16,576]{1,0:T(8,128)(2,1)S(1)} %rank_side.1.refs_0_), channel_id=1, source_target_pairs={{0,3},{1,2},{2,1},{3,0},{4,7},{5,6},{6,5},{7,4},{8,11},{9,10},{10,... | collective-permute-start | bytes 55304 | tf_op jit(solution)/shard_map/ppermute | solution.py:23
  7.9 0.9 %collective-permute-start.1 = (bf16[16,576]{1,0:T(8,128)(2,1)S(1)}, bf16[16,576]{1,0:T(8,128)(2,1)S(1)}, u32[]{:S(2)}, u32[]{:S(2)}) collective-permute-start(bf16[16,576]{1,0:T(8,128)(2,1)S(1)} %rank_side.1.refs_0_), channel_id=1, source_target_pairs={{0,2},{1,3},{2,0},{3,1},{4,6},{5,7},{6,4},{7,5},{8,10},{9,11},{10,... | collective-permute-start | bytes 55304 | tf_op jit(solution)/shard_map/ppermute | solution.py:23
  8.8 0.3 %collective-permute-start = (bf16[16,576]{1,0:T(8,128)(2,1)S(1)}, bf16[16,576]{1,0:T(8,128)(2,1)S(1)}, u32[]{:S(2)}, u32[]{:S(2)}) collective-permute-start(bf16[16,576]{1,0:T(8,128)(2,1)S(1)} %rank_side.1.refs_0_), channel_id=1, source_target_pairs={{0,1},{1,0},{2,3},{3,2},{4,5},{5,4},{6,7},{7,6},{8,9},{9,8},{10,11... | collective-permute-start | bytes 55304 | tf_op jit(solution)/shard_map/ppermute | solution.py:23
  9.1 0.5 %collective-permute-done.7.refs_8_ = bf16[32,2048]{1,0:T(8,128)(2,1)S(1)} collective-permute-done((bf16[32,2048]{1,0:T(8,128)(2,1)}, bf16[32,2048]{1,0:T(8,128)(2,1)S(1)}, u32[]{:S(2)}, u32[]{:S(2)}) %collective-permute-start.7) | collective-permute-done | bytes 131104 | tf_op jit(solution)/shard_map/ppermute | solution.py:23
  9.6 2.4 %collective-permute-start.8 = (bf16[32,2048]{1,0:T(8,128)(2,1)S(1)}, bf16[32,2048]{1,0:T(8,128)(2,1)S(1)}, u32[]{:S(2)}, u32[]{:S(2)}) collective-permute-start(bf16[32,2048]{1,0:T(8,128)(2,1)S(1)} %collective-permute-done.7.refs_8_), channel_id=1, source_target_pairs={{0,4},{4,0},{8,12},{12,8},{1,5},{5,1},{9,13},{13,9},{2,6},{6,2},{1... | collective-permute-start | bytes 393224 | tf_op jit(solution)/shard_map/ppermute | solution.py:23
  12.1 0.9 %token_sums.1 = (f32[64,128]{1,0:T(8,128)S(1)}, bf16[64,128]{1,0:T(8,128)(2,1)S(1)}, bf16[64,128]{1,0:T(8,128)(2,1)S(1)}, bf16[64,128]{1,0:T(8,128)(2,1)S(1)}) custom-call(bf16[16,576]{1,0:T(8,128)(2,1)S(1)} %rank_side.1.refs_0_, bf16[16,576]{1,0:T(8,128)(2,1)S(1)} %collective-permute-done.refs_1_, bf16[16,576]{1,0:T(8,128)(2,1)S(1)} %collective-permute-done.1.refs_2_, ...), custom_call_target="tpu_custom_call" | custom-call | flops 20000000000 | bytes 400000000 | tf_op jit(solution)/shard_map/token_sums/pallas_call | solution.py:101
  13.0 0.1 collective-permute-start.3
  13.1 1.6 %collective-permute-start.4 = (bf16[64,128]{1,0:T(8,128)(2,1)S(1)}, bf16[64,128]{1,0:T(8,128)(2,1)S(1)}, u32[]{:S(2)}, u32[]{:S(2)}) collective-permute-start(bf16[64,128]{1,0:T(8,128)(2,1)S(1)} %get-tuple-element.13), channel_id=1, source_target_pairs={{0,2},{1,3},{2,0},{3,1},{4,6},{5,7},{6,4},{7,5},{8,10},{9,11},{10,... | collective-permute-start | bytes 49160 | tf_op jit(solution)/shard_map/ppermute | solution.py:23
  14.6 0.3 %collective-permute-start.5 = (bf16[64,128]{1,0:T(8,128)(2,1)S(1)}, bf16[64,128]{1,0:T(8,128)(2,1)S(1)}, u32[]{:S(2)}, u32[]{:S(2)}) collective-permute-start(bf16[64,128]{1,0:T(8,128)(2,1)S(1)} %get-tuple-element.14), channel_id=1, source_target_pairs={{0,1},{1,0},{2,3},{3,2},{4,5},{5,4},{6,7},{7,6},{8,9},{9,8},{10,11... | collective-permute-start | bytes 49160 | tf_op jit(solution)/shard_map/ppermute | solution.py:23
  14.9 1.3 %collective-permute-done.3.refs_1_ = bf16[64,128]{1,0:T(8,128)(2,1)S(1)} collective-permute-done((bf16[64,128]{1,0:T(8,128)(2,1)S(1)}, bf16[64,128]{1,0:T(8,128)(2,1)S(1)}, u32[]{:S(2)}, u32[]{:S(2)}) %collective-permute-start.3) | collective-permute-done | bytes 16416 | tf_op jit(solution)/shard_map/ppermute | solution.py:23
  16.3 0.6 %collective-permute-done.4.refs_2_ = bf16[64,128]{1,0:T(8,128)(2,1)S(1)} collective-permute-done((bf16[64,128]{1,0:T(8,128)(2,1)S(1)}, bf16[64,128]{1,0:T(8,128)(2,1)S(1)}, u32[]{:S(2)}, u32[]{:S(2)}) %collective-permute-start.4) | collective-permute-done | bytes 16416 | tf_op jit(solution)/shard_map/ppermute | solution.py:23
  16.9 0.7 %collective-permute-done.8.refs_7_ = bf16[32,2048]{1,0:T(8,128)(2,1)S(1)} collective-permute-done((bf16[32,2048]{1,0:T(8,128)(2,1)S(1)}, bf16[32,2048]{1,0:T(8,128)(2,1)S(1)}, u32[]{:S(2)}, u32[]{:S(2)}) %collective-permute-start.8) | collective-permute-done | bytes 131104 | tf_op jit(solution)/shard_map/ppermute | solution.py:23
  17.6 0.6 %partial_dots.1 = (bf16[4,2048]{1,0:T(4,128)(2,1)S(1)}, f32[8,256]{1,0:T(8,128)S(1)}) custom-call(f32[64,128]{1,0:T(8,128)S(1)} %get-tuple-element.11.refs_0_, bf16[64,128]{1,0:T(8,128)(2,1)S(1)} %collective-permute-done.3.refs_1_, bf16[64,128]{1,0:T(8,128)(2,1)S(1)} %collective-permute-done.4.refs_2_, bf16[64,128]{1,0:T(8,128)(2,1)S(1)} %collective-permute-done.5.refs_3_, ...), custom_call_target="tpu_custom_call" | custom-call | tf_op jit(solution)/shard_map/partial_dots/pallas_call | solution.py:162
  18.1 0.1 collective-permute-start.11
  18.3 1.5 %collective-permute-start.10 = (f32[8,256]{1,0:T(8,128)S(1)}, f32[8,256]{1,0:T(8,128)S(1)}, u32[]{:S(2)}, u32[]{:S(2)}) collective-permute-start(f32[8,256]{1,0:T(8,128)S(1)} %get-tuple-element.17.refs_0_), channel_id=1, source_target_pairs={{0,2},{1,3},{2,0},{3,1},{4,6},{5,7},{6,4},{7,5},{8,10},{9,11},{10,... | collective-permute-start | bytes 24584 | tf_op jit(solution)/shard_map/ppermute | solution.py:23
  19.8 0.2 %collective-permute-start.9 = (f32[8,256]{1,0:T(8,128)S(1)}, f32[8,256]{1,0:T(8,128)S(1)}, u32[]{:S(2)}, u32[]{:S(2)}) collective-permute-start(f32[8,256]{1,0:T(8,128)S(1)} %get-tuple-element.17.refs_0_), channel_id=1, source_target_pairs={{0,1},{1,0},{2,3},{3,2},{4,5},{5,4},{6,7},{7,6},{8,9},{9,8},{10,11... | collective-permute-start | bytes 24584 | tf_op jit(solution)/shard_map/ppermute | solution.py:23
  20.0 0.6 %copy.10 = bf16[4,2048]{1,0:T(4,128)(2,1)} copy(bf16[4,2048]{1,0:T(4,128)(2,1)S(1)} %get-tuple-element.18) | data formatting | bytes 32768
  20.6 0.6 %collective-permute-done.11.refs_3_ = f32[8,256]{1,0:T(8,128)S(1)} collective-permute-done((f32[8,256]{1,0:T(8,128)S(1)}, f32[8,256]{1,0:T(8,128)S(1)}, u32[]{:S(2)}, u32[]{:S(2)}) %collective-permute-start.11) | collective-permute-done | bytes 8224 | tf_op jit(solution)/shard_map/ppermute | solution.py:23
  21.2 0.7 %collective-permute-done.10.refs_2_ = f32[8,256]{1,0:T(8,128)S(1)} collective-permute-done((f32[8,256]{1,0:T(8,128)S(1)}, f32[8,256]{1,0:T(8,128)S(1)}, u32[]{:S(2)}, u32[]{:S(2)}) %collective-permute-start.10) | collective-permute-done | bytes 8224 | tf_op jit(solution)/shard_map/ppermute | solution.py:23
  21.9 0.7 %final_scores.1 = f32[4,32]{1,0:T(4,128)} custom-call(f32[8,256]{1,0:T(8,128)S(1)} %get-tuple-element.17.refs_0_, f32[8,256]{1,0:T(8,128)S(1)} %collective-permute-done.9.refs_1_, f32[8,256]{1,0:T(8,128)S(1)} %collective-permute-done.10.refs_2_, f32[8,256]{1,0:T(8,128)S(1)} %collective-permute-done.11.refs_3_), custom_call_target="tpu_custom_call" | custom-call | tf_op jit(solution)/shard_map/final_scores/pallas_call | solution.py:192
  (22 shorter events, 0.1 us)
Async XLA Ops:
  0.6 5.2 %copy-start.5 = (bf16[2,128,8]{1,2,0:T(8,128)(2,1)S(1)}, bf16[2,128,8]{1,2,0:T(8,128)(2,1)}, u32[]{:S(2)}) copy-start(bf16[2,128,8]{1,2,0:T(8,128)(2,1)} %param.14) | copy-start | bytes 12292
  0.6 5.2 %copy-start.3 = (bf16[1280,128]{1,0:T(8,128)(2,1)S(1)}, bf16[1280,128]{1,0:T(8,128)(2,1)}, u32[]{:S(2)}) copy-start(bf16[1280,128]{1,0:T(8,128)(2,1)} %up.1) | copy-start | bytes 983044
  0.7 5.2 %copy-start.2 = (bf16[128,1280]{1,0:T(8,128)(2,1)S(1)}, bf16[128,1280]{1,0:T(8,128)(2,1)}, u32[]{:S(2)}) copy-start(bf16[128,1280]{1,0:T(8,128)(2,1)} %down.1) | copy-start | bytes 983044
  0.7 5.2 %copy-start.1 = (bf16[4,144,1280]{2,1,0:T(8,128)(2,1)S(1)}, bf16[4,144,1280]{2,1,0:T(8,128)(2,1)}, u32[]{:S(2)}) copy-start(bf16[4,144,1280]{2,1,0:T(8,128)(2,1)} %param.9) | copy-start | bytes 4423684
  0.7 5.2 %copy-start = (bf16[4,144,1280]{2,1,0:T(8,128)(2,1)S(1)}, bf16[4,144,1280]{2,1,0:T(8,128)(2,1)}, u32[]{:S(2)}) copy-start(bf16[4,144,1280]{2,1,0:T(8,128)(2,1)} %param.8) | copy-start | bytes 4423684
  0.7 8.9 %collective-permute-start.7 = (bf16[32,2048]{1,0:T(8,128)(2,1)}, bf16[32,2048]{1,0:T(8,128)(2,1)S(1)}, u32[]{:S(2)}, u32[]{:S(2)}) collective-permute-start(bf16[32,2048]{1,0:T(8,128)(2,1)} %refs_5_.1), channel_id=1, source_target_pairs={{0,12},{4,8},{8,4},{12,0},{1,13},{5,9},{9,5},{13,1},{2,14},{6,10},... | collective-permute-start | bytes 393224 | tf_op jit(solution)/shard_map/ppermute | solution.py:23
  5.8 3.3 %copy-start.4 = (bf16[32,2048]{1,0:T(8,128)(2,1)S(1)}, bf16[32,2048]{1,0:T(8,128)(2,1)}, u32[]{:S(2)}) copy-start(bf16[32,2048]{1,0:T(8,128)(2,1)} %refs_5_.1) | copy-start | bytes 393220
  5.8 6.2 %copy-start.6 = (s32[4]{0:T(128)S(1)}, s32[4]{0:T(128)}, u32[]{:S(2)}) copy-start(s32[4]{0:T(128)} %param.10) | copy-start | bytes 52
  5.9 6.2 %copy-start.7 = (bf16[1280,512]{1,0:T(8,128)(2,1)S(1)}, bf16[1280,512]{1,0:T(8,128)(2,1)}, u32[]{:S(2)}) copy-start(bf16[1280,512]{1,0:T(8,128)(2,1)} %refs_7_.1) | copy-start | bytes 3932164
  7.2 4.8 %collective-permute-start.2 = (bf16[16,576]{1,0:T(8,128)(2,1)S(1)}, bf16[16,576]{1,0:T(8,128)(2,1)S(1)}, u32[]{:S(2)}, u32[]{:S(2)}) collective-permute-start(bf16[16,576]{1,0:T(8,128)(2,1)S(1)} %rank_side.1.refs_0_), channel_id=1, source_target_pairs={{0,3},{1,2},{2,1},{3,0},{4,7},{5,6},{6,5},{7,4},{8,11},{9,10},{10,... | collective-permute-start | bytes 55304 | tf_op jit(solution)/shard_map/ppermute | solution.py:23
  7.9 4.1 %collective-permute-start.1 = (bf16[16,576]{1,0:T(8,128)(2,1)S(1)}, bf16[16,576]{1,0:T(8,128)(2,1)S(1)}, u32[]{:S(2)}, u32[]{:S(2)}) collective-permute-start(bf16[16,576]{1,0:T(8,128)(2,1)S(1)} %rank_side.1.refs_0_), channel_id=1, source_target_pairs={{0,2},{1,3},{2,0},{3,1},{4,6},{5,7},{6,4},{7,5},{8,10},{9,11},{10,... | collective-permute-start | bytes 55304 | tf_op jit(solution)/shard_map/ppermute | solution.py:23
  8.8 3.2 %collective-permute-start = (bf16[16,576]{1,0:T(8,128)(2,1)S(1)}, bf16[16,576]{1,0:T(8,128)(2,1)S(1)}, u32[]{:S(2)}, u32[]{:S(2)}) collective-permute-start(bf16[16,576]{1,0:T(8,128)(2,1)S(1)} %rank_side.1.refs_0_), channel_id=1, source_target_pairs={{0,1},{1,0},{2,3},{3,2},{4,5},{5,4},{6,7},{7,6},{8,9},{9,8},{10,11... | collective-permute-start | bytes 55304 | tf_op jit(solution)/shard_map/ppermute | solution.py:23
  9.1 7.7 %collective-permute-start.6 = (bf16[32,2048]{1,0:T(8,128)(2,1)S(1)}, bf16[32,2048]{1,0:T(8,128)(2,1)S(1)}, u32[]{:S(2)}, u32[]{:S(2)}) collective-permute-start(bf16[32,2048]{1,0:T(8,128)(2,1)S(1)} %copy-done.4), channel_id=1, source_target_pairs={{0,4},{4,0},{8,12},{12,8},{1,5},{5,1},{9,13},{13,9},{2,6},{6,2},{1... | collective-permute-start | bytes 393224 | tf_op jit(solution)/shard_map/ppermute | solution.py:23
  9.6 7.9 %collective-permute-start.8 = (bf16[32,2048]{1,0:T(8,128)(2,1)S(1)}, bf16[32,2048]{1,0:T(8,128)(2,1)S(1)}, u32[]{:S(2)}, u32[]{:S(2)}) collective-permute-start(bf16[32,2048]{1,0:T(8,128)(2,1)S(1)} %collective-permute-done.7.refs_8_), channel_id=1, source_target_pairs={{0,4},{4,0},{8,12},{12,8},{1,5},{5,1},{9,13},{13,9},{2,6},{6,2},{1... | collective-permute-start | bytes 393224 | tf_op jit(solution)/shard_map/ppermute | solution.py:23
  13.0 3.3 %collective-permute-start.3 = (bf16[64,128]{1,0:T(8,128)(2,1)S(1)}, bf16[64,128]{1,0:T(8,128)(2,1)S(1)}, u32[]{:S(2)}, u32[]{:S(2)}) collective-permute-start(bf16[64,128]{1,0:T(8,128)(2,1)S(1)} %get-tuple-element.12), channel_id=1, source_target_pairs={{0,3},{1,2},{2,1},{3,0},{4,7},{5,6},{6,5},{7,4},{8,11},{9,10},{10,... | collective-permute-start | bytes 49160 | tf_op jit(solution)/shard_map/ppermute | solution.py:23
  13.1 3.8 %collective-permute-start.4 = (bf16[64,128]{1,0:T(8,128)(2,1)S(1)}, bf16[64,128]{1,0:T(8,128)(2,1)S(1)}, u32[]{:S(2)}, u32[]{:S(2)}) collective-permute-start(bf16[64,128]{1,0:T(8,128)(2,1)S(1)} %get-tuple-element.13), channel_id=1, source_target_pairs={{0,2},{1,3},{2,0},{3,1},{4,6},{5,7},{6,4},{7,5},{8,10},{9,11},{10,... | collective-permute-start | bytes 49160 | tf_op jit(solution)/shard_map/ppermute | solution.py:23
  14.6 2.2 %collective-permute-start.5 = (bf16[64,128]{1,0:T(8,128)(2,1)S(1)}, bf16[64,128]{1,0:T(8,128)(2,1)S(1)}, u32[]{:S(2)}, u32[]{:S(2)}) collective-permute-start(bf16[64,128]{1,0:T(8,128)(2,1)S(1)} %get-tuple-element.14), channel_id=1, source_target_pairs={{0,1},{1,0},{2,3},{3,2},{4,5},{5,4},{6,7},{7,6},{8,9},{9,8},{10,11... | collective-permute-start | bytes 49160 | tf_op jit(solution)/shard_map/ppermute | solution.py:23
  18.1 3.1 %collective-permute-start.11 = (f32[8,256]{1,0:T(8,128)S(1)}, f32[8,256]{1,0:T(8,128)S(1)}, u32[]{:S(2)}, u32[]{:S(2)}) collective-permute-start(f32[8,256]{1,0:T(8,128)S(1)} %get-tuple-element.17.refs_0_), channel_id=1, source_target_pairs={{0,3},{1,2},{2,1},{3,0},{4,7},{5,6},{6,5},{7,4},{8,11},{9,10},{10,... | collective-permute-start | bytes 24584 | tf_op jit(solution)/shard_map/ppermute | solution.py:23
  18.3 3.7 %collective-permute-start.10 = (f32[8,256]{1,0:T(8,128)S(1)}, f32[8,256]{1,0:T(8,128)S(1)}, u32[]{:S(2)}, u32[]{:S(2)}) collective-permute-start(f32[8,256]{1,0:T(8,128)S(1)} %get-tuple-element.17.refs_0_), channel_id=1, source_target_pairs={{0,2},{1,3},{2,0},{3,1},{4,6},{5,7},{6,4},{7,5},{8,10},{9,11},{10,... | collective-permute-start | bytes 24584 | tf_op jit(solution)/shard_map/ppermute | solution.py:23
  19.8 2.2 %collective-permute-start.9 = (f32[8,256]{1,0:T(8,128)S(1)}, f32[8,256]{1,0:T(8,128)S(1)}, u32[]{:S(2)}, u32[]{:S(2)}) collective-permute-start(f32[8,256]{1,0:T(8,128)S(1)} %get-tuple-element.17.refs_0_), channel_id=1, source_target_pairs={{0,1},{1,0},{2,3},{3,2},{4,5},{5,4},{6,7},{7,6},{8,9},{9,8},{10,11... | collective-permute-start | bytes 24584 | tf_op jit(solution)/shard_map/ppermute | solution.py:23

commit v10 on v9

--- a/solution.py
+++ b/solution.py
@@ -43,20 +43,15 @@
 
 
 def rank_kernel(acts, cots, down, up, sketch, _, right):
-    rows, lanes = acts.shape
     k2 = sketch.shape[1]
     folded = [dot(sketch[0], down[...]), dot(sketch[1], up[...], NT)]
-    coarse = [one.astype(BF16).astype(F32) for one in folded]
-    fine = [one - near for one, near in zip(folded, coarse)]
-    gap = jnp.zeros((k2, lanes), F32)
-    pad = jnp.zeros((LANES - 4 * k2, lanes), F32)
-    first = jnp.concatenate([coarse[0], gap, fine[0], gap, pad], axis=0).T.astype(BF16)
-    second = jnp.concatenate([gap, coarse[1], gap, fine[1], pad], axis=0).T.astype(BF16)
-    got = dot(acts[...], first) + dot(cots[...], second)
-    for at in range(0, rows, LANES):
-        size = min(LANES, rows - at)
-        turned = got[at : at + size].T
-        right[:, at : at + size] = (turned[: 2 * k2] + turned[2 * k2 : 4 * k2]).astype(right.dtype)
+    sums = []
+    for p, keep in enumerate((acts, cots)):
+        coarse = folded[p].astype(BF16).astype(F32)
+        weights = jnp.concatenate([coarse, folded[p] - coarse], axis=0).astype(BF16)
+        got = dot(weights, keep[...], NT)
+        sums.append(got[:k2] + got[k2:])
+    right[...] = jnp.concatenate(sums, axis=0).astype(right.dtype)
 
 
 def rank_side(acts, cots, down, up, sketch, gate):

time: 22.8 us -> 22.8 us (level)
  waiting for transfers between devices: 4.46 us -> 4.85 us
  Pallas kernels: 3.55 us -> 3.19 us
    ppermute x12, waiting for transfers between devices: 4.46 us -> 4.85 us  [swap(): return lax.ppermute(x, axis, [(i, i ^ mask) for i in range(size)])]
    pallas_call x1, Pallas kernels: 1.36 us -> 0.99 us  [rank_side(): pl.pallas_call(rank_kernel, out_shape=jax.ShapeDtypeStruct((2 * sketch.sh...]
  transfers between devices with their start and end apart: 12 -> 12, of which waited for: 6 -> 6; matrix products, arithmetic and copies ran while one was open for 3% -> 3% of each run, Pallas kernels for 10% -> 8%
where the time goes in v10:
time: 22.8 us; the launch traced here: 22.7 us
  starting transfers between devices  13.2 us (58%)
  waiting for transfers between devices  4.85 us (21%)
  Pallas kernels  3.19 us (14%)
  between operations  0.76 us (3%)
  local copies, waits for them, and re-layouts  0.64 us (3%)
    ppermute x12, starting transfers between devices, swap(): return lax.ppermute(x, axis, [(i, i ^ mask) for i in range(size)])  13.2 us
    ppermute x12, waiting for transfers between devices, swap(): return lax.ppermute(x, axis, [(i, i ^ mask) for i in range(size)])  4.85 us
    pallas_call x1, Pallas kernels, rank_side(): pl.pallas_call(rank_kernel, out_shape=jax.ShapeDtypeStruct((2 * sketch.sh...  0.99 us
    pallas_call x1, Pallas kernels, token_sums(): pl.pallas_call(functools.partial(sums_kernel, n_proj, seq_len, k2), out_s...  0.91 us
    pallas_call x1, Pallas kernels, final_scores(): pl.pallas_call(functools.partial(scores_kernel, len(notes), ex_dev, scale...  0.73 us
    unnamed x17, local copies, waits for them, and re-layouts  0.64 us
    pallas_call x1, Pallas kernels, partial_dots(): pl.pallas_call(functools.partial(dots_kernel, n_proj, r), out_shape=(pltp...  0.56 us
  transfers between devices with their start and end apart: 12, of which 6 were waited for; matrix products, arithmetic and copies ran while one was open for 3% of the time, Pallas kernels for 8%

profile of v10, /device:TPU:0, one launch (start us, length us, event | category | flops | bytes accessed | tf_op | source)
XLA Modules:
  0.0 22.7 jit_solution(10404669088358761689)
XLA Ops:
  0.7 5.1 %collective-permute-start.7 = (bf16[32,2048]{1,0:T(8,128)(2,1)}, bf16[32,2048]{1,0:T(8,128)(2,1)S(1)}, u32[]{:S(2)}, u32[]{:S(2)}) collective-permute-start(bf16[32,2048]{1,0:T(8,128)(2,1)} %refs_5_.1), channel_id=1, source_target_pairs={{0,12},{4,8},{8,4},{12,0},{1,13},{5,9},{9,5},{13,1},{2,14},{6,10},... | collective-permute-start | bytes 393224 | tf_op jit(solution)/shard_map/ppermute | solution.py:23
  5.8 0.0 copy-start.6
  5.9 0.0 copy-start.7
  5.9 1.0 %rank_side.1.refs_0_ = bf16[16,576]{1,0:T(8,128)(2,1)S(1)} custom-call(bf16[576,1280]{1,0:T(8,128)(2,1)S(1)} %bitcast.4, bf16[576,1280]{1,0:T(8,128)(2,1)S(1)} %bitcast.6, bf16[128,1280]{1,0:T(8,128)(2,1)S(1)} %copy-done.2, bf16[1280,128]{1,0:T(8,128)(2,1)S(1)} %copy-done.3, bf16[2,8,128]{2,1,0:T(8,128)(2,1)S(1)} %bitcast.8, f32[8,128]{1,0:T(8,128)S(1)} %opening.1._), custom_call_target="tpu_custom_call" | custom-call | tf_op jit(solution)/shard_map/rank_side/pallas_call | solution.py:59
  6.9 0.7 %collective-permute-start.2 = (bf16[16,576]{1,0:T(8,128)(2,1)S(1)}, bf16[16,576]{1,0:T(8,128)(2,1)S(1)}, u32[]{:S(2)}, u32[]{:S(2)}) collective-permute-start(bf16[16,576]{1,0:T(8,128)(2,1)S(1)} %rank_side.1.refs_0_), channel_id=1, source_target_pairs={{0,3},{1,2},{2,1},{3,0},{4,7},{5,6},{6,5},{7,4},{8,11},{9,10},{10,... | collective-permute-start | bytes 55304 | tf_op jit(solution)/shard_map/ppermute | solution.py:23
  7.5 0.9 %collective-permute-start.1 = (bf16[16,576]{1,0:T(8,128)(2,1)S(1)}, bf16[16,576]{1,0:T(8,128)(2,1)S(1)}, u32[]{:S(2)}, u32[]{:S(2)}) collective-permute-start(bf16[16,576]{1,0:T(8,128)(2,1)S(1)} %rank_side.1.refs_0_), channel_id=1, source_target_pairs={{0,2},{1,3},{2,0},{3,1},{4,6},{5,7},{6,4},{7,5},{8,10},{9,11},{10,... | collective-permute-start | bytes 55304 | tf_op jit(solution)/shard_map/ppermute | solution.py:23
  8.4 0.3 %collective-permute-start = (bf16[16,576]{1,0:T(8,128)(2,1)S(1)}, bf16[16,576]{1,0:T(8,128)(2,1)S(1)}, u32[]{:S(2)}, u32[]{:S(2)}) collective-permute-start(bf16[16,576]{1,0:T(8,128)(2,1)S(1)} %rank_side.1.refs_0_), channel_id=1, source_target_pairs={{0,1},{1,0},{2,3},{3,2},{4,5},{5,4},{6,7},{7,6},{8,9},{9,8},{10,11... | collective-permute-start | bytes 55304 | tf_op jit(solution)/shard_map/ppermute | solution.py:23
  8.8 0.9 %collective-permute-done.7.refs_8_ = bf16[32,2048]{1,0:T(8,128)(2,1)S(1)} collective-permute-done((bf16[32,2048]{1,0:T(8,128)(2,1)}, bf16[32,2048]{1,0:T(8,128)(2,1)S(1)}, u32[]{:S(2)}, u32[]{:S(2)}) %collective-permute-start.7) | collective-permute-done | bytes 131104 | tf_op jit(solution)/shard_map/ppermute | solution.py:23
  9.6 2.4 %collective-permute-start.8 = (bf16[32,2048]{1,0:T(8,128)(2,1)S(1)}, bf16[32,2048]{1,0:T(8,128)(2,1)S(1)}, u32[]{:S(2)}, u32[]{:S(2)}) collective-permute-start(bf16[32,2048]{1,0:T(8,128)(2,1)S(1)} %collective-permute-done.7.refs_8_), channel_id=1, source_target_pairs={{0,4},{4,0},{8,12},{12,8},{1,5},{5,1},{9,13},{13,9},{2,6},{6,2},{1... | collective-permute-start | bytes 393224 | tf_op jit(solution)/shard_map/ppermute | solution.py:23
  12.1 0.9 %token_sums.1 = (f32[64,128]{1,0:T(8,128)S(1)}, bf16[64,128]{1,0:T(8,128)(2,1)S(1)}, bf16[64,128]{1,0:T(8,128)(2,1)S(1)}, bf16[64,128]{1,0:T(8,128)(2,1)S(1)}) custom-call(bf16[16,576]{1,0:T(8,128)(2,1)S(1)} %rank_side.1.refs_0_, bf16[16,576]{1,0:T(8,128)(2,1)S(1)} %collective-permute-done.refs_1_, bf16[16,576]{1,0:T(8,128)(2,1)S(1)} %collective-permute-done.1.refs_2_, ...), custom_call_target="tpu_custom_call" | custom-call | flops 20000000000 | bytes 400000000 | tf_op jit(solution)/shard_map/token_sums/pallas_call | solution.py:96
  13.0 0.1 collective-permute-start.3
  13.1 1.6 %collective-permute-start.4 = (bf16[64,128]{1,0:T(8,128)(2,1)S(1)}, bf16[64,128]{1,0:T(8,128)(2,1)S(1)}, u32[]{:S(2)}, u32[]{:S(2)}) collective-permute-start(bf16[64,128]{1,0:T(8,128)(2,1)S(1)} %get-tuple-element.13), channel_id=1, source_target_pairs={{0,2},{1,3},{2,0},{3,1},{4,6},{5,7},{6,4},{7,5},{8,10},{9,11},{10,... | collective-permute-start | bytes 49160 | tf_op jit(solution)/shard_map/ppermute | solution.py:23
  14.6 0.3 %collective-permute-start.5 = (bf16[64,128]{1,0:T(8,128)(2,1)S(1)}, bf16[64,128]{1,0:T(8,128)(2,1)S(1)}, u32[]{:S(2)}, u32[]{:S(2)}) collective-permute-start(bf16[64,128]{1,0:T(8,128)(2,1)S(1)} %get-tuple-element.14), channel_id=1, source_target_pairs={{0,1},{1,0},{2,3},{3,2},{4,5},{5,4},{6,7},{7,6},{8,9},{9,8},{10,11... | collective-permute-start | bytes 49160 | tf_op jit(solution)/shard_map/ppermute | solution.py:23
  14.9 1.4 %collective-permute-done.3.refs_1_ = bf16[64,128]{1,0:T(8,128)(2,1)S(1)} collective-permute-done((bf16[64,128]{1,0:T(8,128)(2,1)S(1)}, bf16[64,128]{1,0:T(8,128)(2,1)S(1)}, u32[]{:S(2)}, u32[]{:S(2)}) %collective-permute-start.3) | collective-permute-done | bytes 16416 | tf_op jit(solution)/shard_map/ppermute | solution.py:23
  16.3 0.5 %collective-permute-done.4.refs_2_ = bf16[64,128]{1,0:T(8,128)(2,1)S(1)} collective-permute-done((bf16[64,128]{1,0:T(8,128)(2,1)S(1)}, bf16[64,128]{1,0:T(8,128)(2,1)S(1)}, u32[]{:S(2)}, u32[]{:S(2)}) %collective-permute-start.4) | collective-permute-done | bytes 16416 | tf_op jit(solution)/shard_map/ppermute | solution.py:23
  16.9 0.3 %collective-permute-done.8.refs_7_ = bf16[32,2048]{1,0:T(8,128)(2,1)S(1)} collective-permute-done((bf16[32,2048]{1,0:T(8,128)(2,1)S(1)}, bf16[32,2048]{1,0:T(8,128)(2,1)S(1)}, u32[]{:S(2)}, u32[]{:S(2)}) %collective-permute-start.8) | collective-permute-done | bytes 131104 | tf_op jit(solution)/shard_map/ppermute | solution.py:23
  17.2 0.6 %partial_dots.1 = (bf16[4,2048]{1,0:T(4,128)(2,1)S(1)}, f32[8,256]{1,0:T(8,128)S(1)}) custom-call(f32[64,128]{1,0:T(8,128)S(1)} %get-tuple-element.11.refs_0_, bf16[64,128]{1,0:T(8,128)(2,1)S(1)} %collective-permute-done.3.refs_1_, bf16[64,128]{1,0:T(8,128)(2,1)S(1)} %collective-permute-done.4.refs_2_, bf16[64,128]{1,0:T(8,128)(2,1)S(1)} %collective-permute-done.5.refs_3_, ...), custom_call_target="tpu_custom_call" | custom-call | tf_op jit(solution)/shard_map/partial_dots/pallas_call | solution.py:157
  17.7 0.5 %collective-permute-start.11 = (f32[8,256]{1,0:T(8,128)S(1)}, f32[8,256]{1,0:T(8,128)S(1)}, u32[]{:S(2)}, u32[]{:S(2)}) collective-permute-start(f32[8,256]{1,0:T(8,128)S(1)} %get-tuple-element.17.refs_0_), channel_id=1, source_target_pairs={{0,3},{1,2},{2,1},{3,0},{4,7},{5,6},{6,5},{7,4},{8,11},{9,10},{10,... | collective-permute-start | bytes 24584 | tf_op jit(solution)/shard_map/ppermute | solution.py:23
  18.3 1.3 %collective-permute-start.10 = (f32[8,256]{1,0:T(8,128)S(1)}, f32[8,256]{1,0:T(8,128)S(1)}, u32[]{:S(2)}, u32[]{:S(2)}) collective-permute-start(f32[8,256]{1,0:T(8,128)S(1)} %get-tuple-element.17.refs_0_), channel_id=1, source_target_pairs={{0,2},{1,3},{2,0},{3,1},{4,6},{5,7},{6,4},{7,5},{8,10},{9,11},{10,... | collective-permute-start | bytes 24584 | tf_op jit(solution)/shard_map/ppermute | solution.py:23
  19.5 0.1 collective-permute-start.9
  19.6 0.6 %copy.10 = bf16[4,2048]{1,0:T(4,128)(2,1)} copy(bf16[4,2048]{1,0:T(4,128)(2,1)S(1)} %get-tuple-element.18) | data formatting | bytes 32768
  20.2 0.6 %collective-permute-done.11.refs_3_ = f32[8,256]{1,0:T(8,128)S(1)} collective-permute-done((f32[8,256]{1,0:T(8,128)S(1)}, f32[8,256]{1,0:T(8,128)S(1)}, u32[]{:S(2)}, u32[]{:S(2)}) %collective-permute-start.11) | collective-permute-done | bytes 8224 | tf_op jit(solution)/shard_map/ppermute | solution.py:23
  20.8 1.1 %collective-permute-done.10.refs_2_ = f32[8,256]{1,0:T(8,128)S(1)} collective-permute-done((f32[8,256]{1,0:T(8,128)S(1)}, f32[8,256]{1,0:T(8,128)S(1)}, u32[]{:S(2)}, u32[]{:S(2)}) %collective-permute-start.10) | collective-permute-done | bytes 8224 | tf_op jit(solution)/shard_map/ppermute | solution.py:23
  21.9 0.7 %final_scores.1 = f32[4,32]{1,0:T(4,128)} custom-call(f32[8,256]{1,0:T(8,128)S(1)} %get-tuple-element.17.refs_0_, f32[8,256]{1,0:T(8,128)S(1)} %collective-permute-done.9.refs_1_, f32[8,256]{1,0:T(8,128)S(1)} %collective-permute-done.10.refs_2_, f32[8,256]{1,0:T(8,128)S(1)} %collective-permute-done.11.refs_3_), custom_call_target="tpu_custom_call" | custom-call | tf_op jit(solution)/shard_map/final_scores/pallas_call | solution.py:187
  (22 shorter events, 0.1 us)
Async XLA Ops:
  0.6 5.2 %copy-start.5 = (bf16[2,128,8]{1,2,0:T(8,128)(2,1)S(1)}, bf16[2,128,8]{1,2,0:T(8,128)(2,1)}, u32[]{:S(2)}) copy-start(bf16[2,128,8]{1,2,0:T(8,128)(2,1)} %param.14) | copy-start | bytes 12292
  0.6 5.2 %copy-start.3 = (bf16[1280,128]{1,0:T(8,128)(2,1)S(1)}, bf16[1280,128]{1,0:T(8,128)(2,1)}, u32[]{:S(2)}) copy-start(bf16[1280,128]{1,0:T(8,128)(2,1)} %up.1) | copy-start | bytes 983044
  0.7 5.2 %copy-start.2 = (bf16[128,1280]{1,0:T(8,128)(2,1)S(1)}, bf16[128,1280]{1,0:T(8,128)(2,1)}, u32[]{:S(2)}) copy-start(bf16[128,1280]{1,0:T(8,128)(2,1)} %down.1) | copy-start | bytes 983044
  0.7 5.2 %copy-start.1 = (bf16[4,144,1280]{2,1,0:T(8,128)(2,1)S(1)}, bf16[4,144,1280]{2,1,0:T(8,128)(2,1)}, u32[]{:S(2)}) copy-start(bf16[4,144,1280]{2,1,0:T(8,128)(2,1)} %param.9) | copy-start | bytes 4423684
  0.7 5.2 %copy-start = (bf16[4,144,1280]{2,1,0:T(8,128)(2,1)S(1)}, bf16[4,144,1280]{2,1,0:T(8,128)(2,1)}, u32[]{:S(2)}) copy-start(bf16[4,144,1280]{2,1,0:T(8,128)(2,1)} %param.8) | copy-start | bytes 4423684
  0.7 8.9 %collective-permute-start.7 = (bf16[32,2048]{1,0:T(8,128)(2,1)}, bf16[32,2048]{1,0:T(8,128)(2,1)S(1)}, u32[]{:S(2)}, u32[]{:S(2)}) collective-permute-start(bf16[32,2048]{1,0:T(8,128)(2,1)} %refs_5_.1), channel_id=1, source_target_pairs={{0,12},{4,8},{8,4},{12,0},{1,13},{5,9},{9,5},{13,1},{2,14},{6,10},... | collective-permute-start | bytes 393224 | tf_op jit(solution)/shard_map/ppermute | solution.py:23
  5.8 2.9 %copy-start.4 = (bf16[32,2048]{1,0:T(8,128)(2,1)S(1)}, bf16[32,2048]{1,0:T(8,128)(2,1)}, u32[]{:S(2)}) copy-start(bf16[32,2048]{1,0:T(8,128)(2,1)} %refs_5_.1) | copy-start | bytes 393220
  5.8 6.2 %copy-start.6 = (s32[4]{0:T(128)S(1)}, s32[4]{0:T(128)}, u32[]{:S(2)}) copy-start(s32[4]{0:T(128)} %param.10) | copy-start | bytes 52
  5.9 6.2 %copy-start.7 = (bf16[1280,512]{1,0:T(8,128)(2,1)S(1)}, bf16[1280,512]{1,0:T(8,128)(2,1)}, u32[]{:S(2)}) copy-start(bf16[1280,512]{1,0:T(8,128)(2,1)} %refs_7_.1) | copy-start | bytes 3932164
  6.9 5.2 %collective-permute-start.2 = (bf16[16,576]{1,0:T(8,128)(2,1)S(1)}, bf16[16,576]{1,0:T(8,128)(2,1)S(1)}, u32[]{:S(2)}, u32[]{:S(2)}) collective-permute-start(bf16[16,576]{1,0:T(8,128)(2,1)S(1)} %rank_side.1.refs_0_), channel_id=1, source_target_pairs={{0,3},{1,2},{2,1},{3,0},{4,7},{5,6},{6,5},{7,4},{8,11},{9,10},{10,... | collective-permute-start | bytes 55304 | tf_op jit(solution)/shard_map/ppermute | solution.py:23
  7.5 4.5 %collective-permute-start.1 = (bf16[16,576]{1,0:T(8,128)(2,1)S(1)}, bf16[16,576]{1,0:T(8,128)(2,1)S(1)}, u32[]{:S(2)}, u32[]{:S(2)}) collective-permute-start(bf16[16,576]{1,0:T(8,128)(2,1)S(1)} %rank_side.1.refs_0_), channel_id=1, source_target_pairs={{0,2},{1,3},{2,0},{3,1},{4,6},{5,7},{6,4},{7,5},{8,10},{9,11},{10,... | collective-permute-start | bytes 55304 | tf_op jit(solution)/shard_map/ppermute | solution.py:23
  8.4 3.6 %collective-permute-start = (bf16[16,576]{1,0:T(8,128)(2,1)S(1)}, bf16[16,576]{1,0:T(8,128)(2,1)S(1)}, u32[]{:S(2)}, u32[]{:S(2)}) collective-permute-start(bf16[16,576]{1,0:T(8,128)(2,1)S(1)} %rank_side.1.refs_0_), channel_id=1, source_target_pairs={{0,1},{1,0},{2,3},{3,2},{4,5},{5,4},{6,7},{7,6},{8,9},{9,8},{10,11... | collective-permute-start | bytes 55304 | tf_op jit(solution)/shard_map/ppermute | solution.py:23
  8.8 8.1 %collective-permute-start.6 = (bf16[32,2048]{1,0:T(8,128)(2,1)S(1)}, bf16[32,2048]{1,0:T(8,128)(2,1)S(1)}, u32[]{:S(2)}, u32[]{:S(2)}) collective-permute-start(bf16[32,2048]{1,0:T(8,128)(2,1)S(1)} %copy-done.4), channel_id=1, source_target_pairs={{0,4},{4,0},{8,12},{12,8},{1,5},{5,1},{9,13},{13,9},{2,6},{6,2},{1... | collective-permute-start | bytes 393224 | tf_op jit(solution)/shard_map/ppermute | solution.py:23
  9.6 7.5 %collective-permute-start.8 = (bf16[32,2048]{1,0:T(8,128)(2,1)S(1)}, bf16[32,2048]{1,0:T(8,128)(2,1)S(1)}, u32[]{:S(2)}, u32[]{:S(2)}) collective-permute-start(bf16[32,2048]{1,0:T(8,128)(2,1)S(1)} %collective-permute-done.7.refs_8_), channel_id=1, source_target_pairs={{0,4},{4,0},{8,12},{12,8},{1,5},{5,1},{9,13},{13,9},{2,6},{6,2},{1... | collective-permute-start | bytes 393224 | tf_op jit(solution)/shard_map/ppermute | solution.py:23
  13.0 3.4 %collective-permute-start.3 = (bf16[64,128]{1,0:T(8,128)(2,1)S(1)}, bf16[64,128]{1,0:T(8,128)(2,1)S(1)}, u32[]{:S(2)}, u32[]{:S(2)}) collective-permute-start(bf16[64,128]{1,0:T(8,128)(2,1)S(1)} %get-tuple-element.12), channel_id=1, source_target_pairs={{0,3},{1,2},{2,1},{3,0},{4,7},{5,6},{6,5},{7,4},{8,11},{9,10},{10,... | collective-permute-start | bytes 49160 | tf_op jit(solution)/shard_map/ppermute | solution.py:23
  13.1 3.8 %collective-permute-start.4 = (bf16[64,128]{1,0:T(8,128)(2,1)S(1)}, bf16[64,128]{1,0:T(8,128)(2,1)S(1)}, u32[]{:S(2)}, u32[]{:S(2)}) collective-permute-start(bf16[64,128]{1,0:T(8,128)(2,1)S(1)} %get-tuple-element.13), channel_id=1, source_target_pairs={{0,2},{1,3},{2,0},{3,1},{4,6},{5,7},{6,4},{7,5},{8,10},{9,11},{10,... | collective-permute-start | bytes 49160 | tf_op jit(solution)/shard_map/ppermute | solution.py:23
  14.6 2.2 %collective-permute-start.5 = (bf16[64,128]{1,0:T(8,128)(2,1)S(1)}, bf16[64,128]{1,0:T(8,128)(2,1)S(1)}, u32[]{:S(2)}, u32[]{:S(2)}) collective-permute-start(bf16[64,128]{1,0:T(8,128)(2,1)S(1)} %get-tuple-element.14), channel_id=1, source_target_pairs={{0,1},{1,0},{2,3},{3,2},{4,5},{5,4},{6,7},{7,6},{8,9},{9,8},{10,11... | collective-permute-start | bytes 49160 | tf_op jit(solution)/shard_map/ppermute | solution.py:23
  17.7 3.1 %collective-permute-start.11 = (f32[8,256]{1,0:T(8,128)S(1)}, f32[8,256]{1,0:T(8,128)S(1)}, u32[]{:S(2)}, u32[]{:S(2)}) collective-permute-start(f32[8,256]{1,0:T(8,128)S(1)} %get-tuple-element.17.refs_0_), channel_id=1, source_target_pairs={{0,3},{1,2},{2,1},{3,0},{4,7},{5,6},{6,5},{7,4},{8,11},{9,10},{10,... | collective-permute-start | bytes 24584 | tf_op jit(solution)/shard_map/ppermute | solution.py:23
  18.3 3.7 %collective-permute-start.10 = (f32[8,256]{1,0:T(8,128)S(1)}, f32[8,256]{1,0:T(8,128)S(1)}, u32[]{:S(2)}, u32[]{:S(2)}) collective-permute-start(f32[8,256]{1,0:T(8,128)S(1)} %get-tuple-element.17.refs_0_), channel_id=1, source_target_pairs={{0,2},{1,3},{2,0},{3,1},{4,6},{5,7},{6,4},{7,5},{8,10},{9,11},{10,... | collective-permute-start | bytes 24584 | tf_op jit(solution)/shard_map/ppermute | solution.py:23
  19.5 2.4 %collective-permute-start.9 = (f32[8,256]{1,0:T(8,128)S(1)}, f32[8,256]{1,0:T(8,128)S(1)}, u32[]{:S(2)}, u32[]{:S(2)}) collective-permute-start(f32[8,256]{1,0:T(8,128)S(1)} %get-tuple-element.17.refs_0_), channel_id=1, source_target_pairs={{0,1},{1,0},{2,3},{3,2},{4,5},{5,4},{6,7},{7,6},{8,9},{9,8},{10,11... | collective-permute-start | bytes 24584 | tf_op jit(solution)/shard_map/ppermute | solution.py:23

commit v11 on v10

--- a/solution.py
+++ b/solution.py
@@ -124,12 +124,13 @@
             lines[e] = jnp.where((lane >= lo * r) & (lane < (lo + 1) * r), moved, lines[e])
     for e in range(ex_dev):
         lined[pl.ds(e, high, stride=ex_dev), :] = lines[e]
-    squares = jnp.zeros((ex_dev, LANES), F32)
+    squares, own = jnp.zeros((ex_dev, LANES), F32), []
     for hi in range(high):
         line = lined[hi * ex_dev : (hi + 1) * ex_dev, :].astype(BF16)
         train[:, hi * LANES : (hi + 1) * LANES] = line
+        own.append(line)
         squares += line.astype(F32) * line.astype(F32)
-    own = train[...]
+    own = jnp.concatenate(own, axis=1)
     note[...] = jnp.zeros_like(note)
     at, rows, group = 0, 0, []
     for block in blocks:
@@ -146,7 +147,9 @@
                     square += piece * piece
                 note[ex_dev : ex_dev + 1, at : at + LANES] = jnp.sum(square.T, axis=0, keepdims=True)
                 at, rows, group = at + LANES, 0, []
-    note[:ex_dev, at : at + LANES] = jnp.broadcast_to(jnp.sum(squares, axis=1, keepdims=True), (ex_dev, LANES))
+    total_sq = jnp.sum(squares, axis=1, keepdims=True)
+    spot = lax.broadcasted_iota(jnp.int32, (ex_dev, LANES), 1) == lax.broadcasted_iota(jnp.int32, (ex_dev, LANES), 0)
+    note[ex_dev + 1 : ex_dev + 2, :LANES] = jnp.sum(jnp.where(spot, total_sq, 0.0), axis=0, keepdims=True)
 
 
 def partial_dots(pieces, lengths, blocks, r):
@@ -158,7 +161,7 @@
         functools.partial(dots_kernel, n_proj, r),
         out_shape=(
             pltpu.VMEM((ex_dev, k_own * r), BF16),
-            jax.ShapeDtypeStruct((2 * ex_dev, n_val + LANES), F32),
+            jax.ShapeDtypeStruct((2 * ex_dev, n_val), F32),
         ),
         in_specs=[VMEM] * n_proj + [VMEM] + [VMEM] * len(blocks),
         out_specs=(VMEM, VMEM),
@@ -171,9 +174,11 @@
 def scores_kernel(n_proj, ex_dev, scale, by_mask, *refs):
     notes, out = refs[:n_proj], refs[n_proj]
     total = sum([note[...] for note in notes[1:]], notes[0][...])
-    n_val = total.shape[1] - LANES
+    n_val = total.shape[1]
     share = out.shape[1]
-    train_sq = total[:ex_dev, n_val : n_val + 1]
+    spot = lax.broadcasted_iota(jnp.int32, (ex_dev, LANES), 1) == lax.broadcasted_iota(jnp.int32, (ex_dev, LANES), 0)
+    squares = jnp.broadcast_to(total[ex_dev + 1 : ex_dev + 2, :LANES], (ex_dev, LANES))
+    train_sq = jnp.sum(jnp.where(spot, squares, 0.0), axis=1, keepdims=True)
     val_sq = total[ex_dev : ex_dev + 1, :n_val]
     every = scale * total[:ex_dev, :n_val] * lax.rsqrt(train_sq + epsilon) * lax.rsqrt(val_sq + epsilon)
     at = lax.axis_index("proj")
@@ -232,7 +237,7 @@
     pieces = [pieces[0]] + [swap(pieces[m], "proj", m) for m in range(n_proj - 1, 0, -1)]
     train_proj, note = partial_dots(pieces, lengths, blocks, 2 * k2)
     notes = [note] + [swap(note, "proj", m) for m in range(1, n_proj)]
-    share = (note.shape[1] - LANES) // n_proj
+    share = note.shape[1] // n_proj
     scores = final_scores(notes, ex_dev, share, math.sqrt(k1 * 2 * k2), by_mask)
     return (train_proj, scores)
 

time: 22.8 us -> 22.8 us (level)
  no operation moved by 1% of the time
where the time goes in v11:
time: 22.8 us; the launch traced here: 22.6 us
  starting transfers between devices  13.2 us (58%)
  waiting for transfers between devices  4.8 us (21%)
  Pallas kernels  3.19 us (14%)
  between operations  0.76 us (3%)
  local copies, waits for them, and re-layouts  0.64 us (3%)
    ppermute x12, starting transfers between devices, swap(): return lax.ppermute(x, axis, [(i, i ^ mask) for i in range(size)])  13.2 us
    ppermute x12, waiting for transfers between devices, swap(): return lax.ppermute(x, axis, [(i, i ^ mask) for i in range(size)])  4.8 us
    pallas_call x1, Pallas kernels, rank_side(): pl.pallas_call(rank_kernel, out_shape=jax.ShapeDtypeStruct((2 * sketch.sh...  0.99 us
    pallas_call x1, Pallas kernels, token_sums(): pl.pallas_call(functools.partial(sums_kernel, n_proj, seq_len, k2), out_s...  0.91 us
    pallas_call x1, Pallas kernels, final_scores(): pl.pallas_call(functools.partial(scores_kernel, len(notes), ex_dev, scale...  0.74 us
    unnamed x17, local copies, waits for them, and re-layouts  0.64 us
    pallas_call x1, Pallas kernels, partial_dots(): pl.pallas_call(functools.partial(dots_kernel, n_proj, r), out_shape=(pltp...  0.55 us
  transfers between devices with their start and end apart: 12, of which 6 were waited for; matrix products, arithmetic and copies ran while one was open for 3% of the time, Pallas kernels for 8%

profile of v11, /device:TPU:0, one launch (start us, length us, event | category | flops | bytes accessed | tf_op | source)
XLA Modules:
  0.0 22.6 jit_solution(11472527362181499883)
XLA Ops:
  0.7 5.1 %collective-permute-start.7 = (bf16[32,2048]{1,0:T(8,128)(2,1)}, bf16[32,2048]{1,0:T(8,128)(2,1)S(1)}, u32[]{:S(2)}, u32[]{:S(2)}) collective-permute-start(bf16[32,2048]{1,0:T(8,128)(2,1)} %refs_5_.1), channel_id=1, source_target_pairs={{0,12},{4,8},{8,4},{12,0},{1,13},{5,9},{9,5},{13,1},{2,14},{6,10},... | collective-permute-start | bytes 393224 | tf_op jit(solution)/shard_map/ppermute | solution.py:23
  5.8 0.0 copy-start.6
  5.9 0.0 copy-start.7
  5.9 1.0 %rank_side.1.refs_0_ = bf16[16,576]{1,0:T(8,128)(2,1)S(1)} custom-call(bf16[576,1280]{1,0:T(8,128)(2,1)S(1)} %bitcast.4, bf16[576,1280]{1,0:T(8,128)(2,1)S(1)} %bitcast.6, bf16[128,1280]{1,0:T(8,128)(2,1)S(1)} %copy-done.2, bf16[1280,128]{1,0:T(8,128)(2,1)S(1)} %copy-done.3, bf16[2,8,128]{2,1,0:T(8,128)(2,1)S(1)} %bitcast.8, f32[8,128]{1,0:T(8,128)S(1)} %opening.1._), custom_call_target="tpu_custom_call" | custom-call | tf_op jit(solution)/shard_map/rank_side/pallas_call | solution.py:59
  6.9 0.7 %collective-permute-start.2 = (bf16[16,576]{1,0:T(8,128)(2,1)S(1)}, bf16[16,576]{1,0:T(8,128)(2,1)S(1)}, u32[]{:S(2)}, u32[]{:S(2)}) collective-permute-start(bf16[16,576]{1,0:T(8,128)(2,1)S(1)} %rank_side.1.refs_0_), channel_id=1, source_target_pairs={{0,3},{1,2},{2,1},{3,0},{4,7},{5,6},{6,5},{7,4},{8,11},{9,10},{10,... | collective-permute-start | bytes 55304 | tf_op jit(solution)/shard_map/ppermute | solution.py:23
  7.5 0.9 %collective-permute-start.1 = (bf16[16,576]{1,0:T(8,128)(2,1)S(1)}, bf16[16,576]{1,0:T(8,128)(2,1)S(1)}, u32[]{:S(2)}, u32[]{:S(2)}) collective-permute-start(bf16[16,576]{1,0:T(8,128)(2,1)S(1)} %rank_side.1.refs_0_), channel_id=1, source_target_pairs={{0,2},{1,3},{2,0},{3,1},{4,6},{5,7},{6,4},{7,5},{8,10},{9,11},{10,... | collective-permute-start | bytes 55304 | tf_op jit(solution)/shard_map/ppermute | solution.py:23
  8.4 0.3 %collective-permute-start = (bf16[16,576]{1,0:T(8,128)(2,1)S(1)}, bf16[16,576]{1,0:T(8,128)(2,1)S(1)}, u32[]{:S(2)}, u32[]{:S(2)}) collective-permute-start(bf16[16,576]{1,0:T(8,128)(2,1)S(1)} %rank_side.1.refs_0_), channel_id=1, source_target_pairs={{0,1},{1,0},{2,3},{3,2},{4,5},{5,4},{6,7},{7,6},{8,9},{9,8},{10,11... | collective-permute-start | bytes 55304 | tf_op jit(solution)/shard_map/ppermute | solution.py:23
  8.8 0.9 %collective-permute-done.7.refs_8_ = bf16[32,2048]{1,0:T(8,128)(2,1)S(1)} collective-permute-done((bf16[32,2048]{1,0:T(8,128)(2,1)}, bf16[32,2048]{1,0:T(8,128)(2,1)S(1)}, u32[]{:S(2)}, u32[]{:S(2)}) %collective-permute-start.7) | collective-permute-done | bytes 131104 | tf_op jit(solution)/shard_map/ppermute | solution.py:23
  9.6 2.4 %collective-permute-start.8 = (bf16[32,2048]{1,0:T(8,128)(2,1)S(1)}, bf16[32,2048]{1,0:T(8,128)(2,1)S(1)}, u32[]{:S(2)}, u32[]{:S(2)}) collective-permute-start(bf16[32,2048]{1,0:T(8,128)(2,1)S(1)} %collective-permute-done.7.refs_8_), channel_id=1, source_target_pairs={{0,4},{4,0},{8,12},{12,8},{1,5},{5,1},{9,13},{13,9},{2,6},{6,2},{1... | collective-permute-start | bytes 393224 | tf_op jit(solution)/shard_map/ppermute | solution.py:23
  12.1 0.9 %token_sums.1 = (f32[64,128]{1,0:T(8,128)S(1)}, bf16[64,128]{1,0:T(8,128)(2,1)S(1)}, bf16[64,128]{1,0:T(8,128)(2,1)S(1)}, bf16[64,128]{1,0:T(8,128)(2,1)S(1)}) custom-call(bf16[16,576]{1,0:T(8,128)(2,1)S(1)} %rank_side.1.refs_0_, bf16[16,576]{1,0:T(8,128)(2,1)S(1)} %collective-permute-done.refs_1_, bf16[16,576]{1,0:T(8,128)(2,1)S(1)} %collective-permute-done.1.refs_2_, ...), custom_call_target="tpu_custom_call" | custom-call | flops 20000000000 | bytes 400000000 | tf_op jit(solution)/shard_map/token_sums/pallas_call | solution.py:96
  13.0 0.1 collective-permute-start.3
  13.1 1.6 %collective-permute-start.4 = (bf16[64,128]{1,0:T(8,128)(2,1)S(1)}, bf16[64,128]{1,0:T(8,128)(2,1)S(1)}, u32[]{:S(2)}, u32[]{:S(2)}) collective-permute-start(bf16[64,128]{1,0:T(8,128)(2,1)S(1)} %get-tuple-element.13), channel_id=1, source_target_pairs={{0,2},{1,3},{2,0},{3,1},{4,6},{5,7},{6,4},{7,5},{8,10},{9,11},{10,... | collective-permute-start | bytes 49160 | tf_op jit(solution)/shard_map/ppermute | solution.py:23
  14.6 0.3 %collective-permute-start.5 = (bf16[64,128]{1,0:T(8,128)(2,1)S(1)}, bf16[64,128]{1,0:T(8,128)(2,1)S(1)}, u32[]{:S(2)}, u32[]{:S(2)}) collective-permute-start(bf16[64,128]{1,0:T(8,128)(2,1)S(1)} %get-tuple-element.14), channel_id=1, source_target_pairs={{0,1},{1,0},{2,3},{3,2},{4,5},{5,4},{6,7},{7,6},{8,9},{9,8},{10,11... | collective-permute-start | bytes 49160 | tf_op jit(solution)/shard_map/ppermute | solution.py:23
  14.9 1.4 %collective-permute-done.3.refs_1_ = bf16[64,128]{1,0:T(8,128)(2,1)S(1)} collective-permute-done((bf16[64,128]{1,0:T(8,128)(2,1)S(1)}, bf16[64,128]{1,0:T(8,128)(2,1)S(1)}, u32[]{:S(2)}, u32[]{:S(2)}) %collective-permute-start.3) | collective-permute-done | bytes 16416 | tf_op jit(solution)/shard_map/ppermute | solution.py:23
  16.3 0.5 %collective-permute-done.4.refs_2_ = bf16[64,128]{1,0:T(8,128)(2,1)S(1)} collective-permute-done((bf16[64,128]{1,0:T(8,128)(2,1)S(1)}, bf16[64,128]{1,0:T(8,128)(2,1)S(1)}, u32[]{:S(2)}, u32[]{:S(2)}) %collective-permute-start.4) | collective-permute-done | bytes 16416 | tf_op jit(solution)/shard_map/ppermute | solution.py:23
  16.9 0.3 %collective-permute-done.8.refs_7_ = bf16[32,2048]{1,0:T(8,128)(2,1)S(1)} collective-permute-done((bf16[32,2048]{1,0:T(8,128)(2,1)S(1)}, bf16[32,2048]{1,0:T(8,128)(2,1)S(1)}, u32[]{:S(2)}, u32[]{:S(2)}) %collective-permute-start.8) | collective-permute-done | bytes 131104 | tf_op jit(solution)/shard_map/ppermute | solution.py:23
  17.2 0.6 %partial_dots.1 = (bf16[4,2048]{1,0:T(4,128)(2,1)S(1)}, f32[8,128]{1,0:T(8,128)S(1)}) custom-call(f32[64,128]{1,0:T(8,128)S(1)} %get-tuple-element.11.refs_0_, bf16[64,128]{1,0:T(8,128)(2,1)S(1)} %collective-permute-done.3.refs_1_, bf16[64,128]{1,0:T(8,128)(2,1)S(1)} %collective-permute-done.4.refs_2_, bf16[64,128]{1,0:T(8,128)(2,1)S(1)} %collective-permute-done.5.refs_3_, ...), custom_call_target="tpu_custom_call" | custom-call | tf_op jit(solution)/shard_map/partial_dots/pallas_call | solution.py:160
  17.7 0.5 %collective-permute-start.11 = (f32[8,128]{1,0:T(8,128)S(1)}, f32[8,128]{1,0:T(8,128)S(1)}, u32[]{:S(2)}, u32[]{:S(2)}) collective-permute-start(f32[8,128]{1,0:T(8,128)S(1)} %get-tuple-element.17.refs_0_), channel_id=1, source_target_pairs={{0,3},{1,2},{2,1},{3,0},{4,7},{5,6},{6,5},{7,4},{8,11},{9,10},{10,... | collective-permute-start | bytes 12296 | tf_op jit(solution)/shard_map/ppermute | solution.py:23
  18.3 1.3 %collective-permute-start.10 = (f32[8,128]{1,0:T(8,128)S(1)}, f32[8,128]{1,0:T(8,128)S(1)}, u32[]{:S(2)}, u32[]{:S(2)}) collective-permute-start(f32[8,128]{1,0:T(8,128)S(1)} %get-tuple-element.17.refs_0_), channel_id=1, source_target_pairs={{0,2},{1,3},{2,0},{3,1},{4,6},{5,7},{6,4},{7,5},{8,10},{9,11},{10,... | collective-permute-start | bytes 12296 | tf_op jit(solution)/shard_map/ppermute | solution.py:23
  19.5 0.1 collective-permute-start.9
  19.6 0.6 %copy.10 = bf16[4,2048]{1,0:T(4,128)(2,1)} copy(bf16[4,2048]{1,0:T(4,128)(2,1)S(1)} %get-tuple-element.18) | data formatting | bytes 32768
  20.2 0.6 %collective-permute-done.11.refs_3_ = f32[8,128]{1,0:T(8,128)S(1)} collective-permute-done((f32[8,128]{1,0:T(8,128)S(1)}, f32[8,128]{1,0:T(8,128)S(1)}, u32[]{:S(2)}, u32[]{:S(2)}) %collective-permute-start.11) | collective-permute-done | bytes 4128 | tf_op jit(solution)/shard_map/ppermute | solution.py:23
  20.8 1.1 %collective-permute-done.10.refs_2_ = f32[8,128]{1,0:T(8,128)S(1)} collective-permute-done((f32[8,128]{1,0:T(8,128)S(1)}, f32[8,128]{1,0:T(8,128)S(1)}, u32[]{:S(2)}, u32[]{:S(2)}) %collective-permute-start.10) | collective-permute-done | bytes 4128 | tf_op jit(solution)/shard_map/ppermute | solution.py:23
  21.9 0.7 %final_scores.1 = f32[4,32]{1,0:T(4,128)} custom-call(f32[8,128]{1,0:T(8,128)S(1)} %get-tuple-element.17.refs_0_, f32[8,128]{1,0:T(8,128)S(1)} %collective-permute-done.9.refs_1_, f32[8,128]{1,0:T(8,128)S(1)} %collective-permute-done.10.refs_2_, f32[8,128]{1,0:T(8,128)S(1)} %collective-permute-done.11.refs_3_), custom_call_target="tpu_custom_call" | custom-call | tf_op jit(solution)/shard_map/final_scores/pallas_call | solution.py:192
  (22 shorter events, 0.1 us)
Async XLA Ops:
  0.6 5.2 %copy-start.5 = (bf16[2,128,8]{1,2,0:T(8,128)(2,1)S(1)}, bf16[2,128,8]{1,2,0:T(8,128)(2,1)}, u32[]{:S(2)}) copy-start(bf16[2,128,8]{1,2,0:T(8,128)(2,1)} %param.14) | copy-start | bytes 12292
  0.6 5.2 %copy-start.3 = (bf16[1280,128]{1,0:T(8,128)(2,1)S(1)}, bf16[1280,128]{1,0:T(8,128)(2,1)}, u32[]{:S(2)}) copy-start(bf16[1280,128]{1,0:T(8,128)(2,1)} %up.1) | copy-start | bytes 983044
  0.7 5.2 %copy-start.2 = (bf16[128,1280]{1,0:T(8,128)(2,1)S(1)}, bf16[128,1280]{1,0:T(8,128)(2,1)}, u32[]{:S(2)}) copy-start(bf16[128,1280]{1,0:T(8,128)(2,1)} %down.1) | copy-start | bytes 983044
  0.7 5.2 %copy-start.1 = (bf16[4,144,1280]{2,1,0:T(8,128)(2,1)S(1)}, bf16[4,144,1280]{2,1,0:T(8,128)(2,1)}, u32[]{:S(2)}) copy-start(bf16[4,144,1280]{2,1,0:T(8,128)(2,1)} %param.9) | copy-start | bytes 4423684
  0.7 5.2 %copy-start = (bf16[4,144,1280]{2,1,0:T(8,128)(2,1)S(1)}, bf16[4,144,1280]{2,1,0:T(8,128)(2,1)}, u32[]{:S(2)}) copy-start(bf16[4,144,1280]{2,1,0:T(8,128)(2,1)} %param.8) | copy-start | bytes 4423684
  0.7 8.9 %collective-permute-start.7 = (bf16[32,2048]{1,0:T(8,128)(2,1)}, bf16[32,2048]{1,0:T(8,128)(2,1)S(1)}, u32[]{:S(2)}, u32[]{:S(2)}) collective-permute-start(bf16[32,2048]{1,0:T(8,128)(2,1)} %refs_5_.1), channel_id=1, source_target_pairs={{0,12},{4,8},{8,4},{12,0},{1,13},{5,9},{9,5},{13,1},{2,14},{6,10},... | collective-permute-start | bytes 393224 | tf_op jit(solution)/shard_map/ppermute | solution.py:23
  5.8 2.9 %copy-start.4 = (bf16[32,2048]{1,0:T(8,128)(2,1)S(1)}, bf16[32,2048]{1,0:T(8,128)(2,1)}, u32[]{:S(2)}) copy-start(bf16[32,2048]{1,0:T(8,128)(2,1)} %refs_5_.1) | copy-start | bytes 393220
  5.8 6.2 %copy-start.6 = (s32[4]{0:T(128)S(1)}, s32[4]{0:T(128)}, u32[]{:S(2)}) copy-start(s32[4]{0:T(128)} %param.10) | copy-start | bytes 52
  5.9 6.2 %copy-start.7 = (bf16[1280,512]{1,0:T(8,128)(2,1)S(1)}, bf16[1280,512]{1,0:T(8,128)(2,1)}, u32[]{:S(2)}) copy-start(bf16[1280,512]{1,0:T(8,128)(2,1)} %refs_7_.1) | copy-start | bytes 3932164
  6.9 5.2 %collective-permute-start.2 = (bf16[16,576]{1,0:T(8,128)(2,1)S(1)}, bf16[16,576]{1,0:T(8,128)(2,1)S(1)}, u32[]{:S(2)}, u32[]{:S(2)}) collective-permute-start(bf16[16,576]{1,0:T(8,128)(2,1)S(1)} %rank_side.1.refs_0_), channel_id=1, source_target_pairs={{0,3},{1,2},{2,1},{3,0},{4,7},{5,6},{6,5},{7,4},{8,11},{9,10},{10,... | collective-permute-start | bytes 55304 | tf_op jit(solution)/shard_map/ppermute | solution.py:23
  7.5 4.5 %collective-permute-start.1 = (bf16[16,576]{1,0:T(8,128)(2,1)S(1)}, bf16[16,576]{1,0:T(8,128)(2,1)S(1)}, u32[]{:S(2)}, u32[]{:S(2)}) collective-permute-start(bf16[16,576]{1,0:T(8,128)(2,1)S(1)} %rank_side.1.refs_0_), channel_id=1, source_target_pairs={{0,2},{1,3},{2,0},{3,1},{4,6},{5,7},{6,4},{7,5},{8,10},{9,11},{10,... | collective-permute-start | bytes 55304 | tf_op jit(solution)/shard_map/ppermute | solution.py:23
  8.4 3.6 %collective-permute-start = (bf16[16,576]{1,0:T(8,128)(2,1)S(1)}, bf16[16,576]{1,0:T(8,128)(2,1)S(1)}, u32[]{:S(2)}, u32[]{:S(2)}) collective-permute-start(bf16[16,576]{1,0:T(8,128)(2,1)S(1)} %rank_side.1.refs_0_), channel_id=1, source_target_pairs={{0,1},{1,0},{2,3},{3,2},{4,5},{5,4},{6,7},{7,6},{8,9},{9,8},{10,11... | collective-permute-start | bytes 55304 | tf_op jit(solution)/shard_map/ppermute | solution.py:23
  8.8 8.1 %collective-permute-start.6 = (bf16[32,2048]{1,0:T(8,128)(2,1)S(1)}, bf16[32,2048]{1,0:T(8,128)(2,1)S(1)}, u32[]{:S(2)}, u32[]{:S(2)}) collective-permute-start(bf16[32,2048]{1,0:T(8,128)(2,1)S(1)} %copy-done.4), channel_id=1, source_target_pairs={{0,4},{4,0},{8,12},{12,8},{1,5},{5,1},{9,13},{13,9},{2,6},{6,2},{1... | collective-permute-start | bytes 393224 | tf_op jit(solution)/shard_map/ppermute | solution.py:23
  9.6 7.5 %collective-permute-start.8 = (bf16[32,2048]{1,0:T(8,128)(2,1)S(1)}, bf16[32,2048]{1,0:T(8,128)(2,1)S(1)}, u32[]{:S(2)}, u32[]{:S(2)}) collective-permute-start(bf16[32,2048]{1,0:T(8,128)(2,1)S(1)} %collective-permute-done.7.refs_8_), channel_id=1, source_target_pairs={{0,4},{4,0},{8,12},{12,8},{1,5},{5,1},{9,13},{13,9},{2,6},{6,2},{1... | collective-permute-start | bytes 393224 | tf_op jit(solution)/shard_map/ppermute | solution.py:23
  13.0 3.4 %collective-permute-start.3 = (bf16[64,128]{1,0:T(8,128)(2,1)S(1)}, bf16[64,128]{1,0:T(8,128)(2,1)S(1)}, u32[]{:S(2)}, u32[]{:S(2)}) collective-permute-start(bf16[64,128]{1,0:T(8,128)(2,1)S(1)} %get-tuple-element.12), channel_id=1, source_target_pairs={{0,3},{1,2},{2,1},{3,0},{4,7},{5,6},{6,5},{7,4},{8,11},{9,10},{10,... | collective-permute-start | bytes 49160 | tf_op jit(solution)/shard_map/ppermute | solution.py:23
  13.1 3.8 %collective-permute-start.4 = (bf16[64,128]{1,0:T(8,128)(2,1)S(1)}, bf16[64,128]{1,0:T(8,128)(2,1)S(1)}, u32[]{:S(2)}, u32[]{:S(2)}) collective-permute-start(bf16[64,128]{1,0:T(8,128)(2,1)S(1)} %get-tuple-element.13), channel_id=1, source_target_pairs={{0,2},{1,3},{2,0},{3,1},{4,6},{5,7},{6,4},{7,5},{8,10},{9,11},{10,... | collective-permute-start | bytes 49160 | tf_op jit(solution)/shard_map/ppermute | solution.py:23
  14.6 2.2 %collective-permute-start.5 = (bf16[64,128]{1,0:T(8,128)(2,1)S(1)}, bf16[64,128]{1,0:T(8,128)(2,1)S(1)}, u32[]{:S(2)}, u32[]{:S(2)}) collective-permute-start(bf16[64,128]{1,0:T(8,128)(2,1)S(1)} %get-tuple-element.14), channel_id=1, source_target_pairs={{0,1},{1,0},{2,3},{3,2},{4,5},{5,4},{6,7},{7,6},{8,9},{9,8},{10,11... | collective-permute-start | bytes 49160 | tf_op jit(solution)/shard_map/ppermute | solution.py:23
  17.7 3.0 %collective-permute-start.11 = (f32[8,128]{1,0:T(8,128)S(1)}, f32[8,128]{1,0:T(8,128)S(1)}, u32[]{:S(2)}, u32[]{:S(2)}) collective-permute-start(f32[8,128]{1,0:T(8,128)S(1)} %get-tuple-element.17.refs_0_), channel_id=1, source_target_pairs={{0,3},{1,2},{2,1},{3,0},{4,7},{5,6},{6,5},{7,4},{8,11},{9,10},{10,... | collective-permute-start | bytes 12296 | tf_op jit(solution)/shard_map/ppermute | solution.py:23
  18.3 3.6 %collective-permute-start.10 = (f32[8,128]{1,0:T(8,128)S(1)}, f32[8,128]{1,0:T(8,128)S(1)}, u32[]{:S(2)}, u32[]{:S(2)}) collective-permute-start(f32[8,128]{1,0:T(8,128)S(1)} %get-tuple-element.17.refs_0_), channel_id=1, source_target_pairs={{0,2},{1,3},{2,0},{3,1},{4,6},{5,7},{6,4},{7,5},{8,10},{9,11},{10,... | collective-permute-start | bytes 12296 | tf_op jit(solution)/shard_map/ppermute | solution.py:23
  19.5 2.4 %collective-permute-start.9 = (f32[8,128]{1,0:T(8,128)S(1)}, f32[8,128]{1,0:T(8,128)S(1)}, u32[]{:S(2)}, u32[]{:S(2)}) collective-permute-start(f32[8,128]{1,0:T(8,128)S(1)} %get-tuple-element.17.refs_0_), channel_id=1, source_target_pairs={{0,1},{1,0},{2,3},{3,2},{4,5},{5,4},{6,7},{7,6},{8,9},{9,8},{10,11... | collective-permute-start | bytes 12296 | tf_op jit(solution)/shard_map/ppermute | solution.py:23
